TPU v7x, 256 devices: a whole 4x4x8 slice. The times are simulated.
256 devices in a mesh: expert: 32 (over y_hi, z, core), dp: 8 (over x, y_lo).
Axes of the slice: x: 4, y: 4 (y_hi: 2, y_lo: 2; y = y_hi * 2 + y_lo), z: 8, core: 2. Of those that a mesh axis runs over, the one named last changes fastest.
Arguments:
- tokens: bfloat16 [2, 512, 3584], P(None, 'expert', 'dp'), may hold values from -6 to 6
- routes: int32 [2, 512, 8], P(None, 'expert'), may hold values from 0 to 63, all different within a row; in each aligned block of 16 rows (0 to 15, 16 to 31, ..., all dimensions but the last counted through in order) at most 4 rows name the same one
- gate_fix: int32 [2, 512, 8], P(None, 'expert'), may hold values from 1 to 65535
- position: int32 [64], replicated, may hold values from 0 to 63, each once
- swap_slot: int32 [32], replicated, may hold values from 0 to 1
- w_gate: bfloat16 [64, 3584, 1024], P('expert', None, 'dp'), may hold values from -0.09375 to 0.09375
- w_up: bfloat16 [64, 3584, 1024], P('expert', None, 'dp'), may hold values from -0.09375 to 0.09375
- w_down: bfloat16 [64, 1024, 3584], P('expert', 'dp'), may hold values from -0.1875 to 0.1875
Outputs:
- combined: bfloat16 [2, 512, 3584], P(None, 'expert', 'dp')
- device_load: float32 [32], P('expert')
- swapped_gate: bfloat16 [64, 3584, 1024], P('expert', None, 'dp')
- swapped_up: bfloat16 [64, 3584, 1024], P('expert', None, 'dp')
- swapped_down: bfloat16 [64, 1024, 3584], P('expert', 'dp')
Inputs may be any that keep to these rules, and one draw needn't show every extreme that they name: `routes`: in each step the 16 tokens of one index of expert name any one expert in at most 4 rows, and in some such block one expert is named by exactly 4. `position`: each expert once.
All inputs are finite; a program needn't handle non-finite values.
Results may differ from a plain program's by a relative error of at most 0.02.
Values may be sent and summed in bfloat16 or wider, within the bound.
No kernel may reach another device: no remote copies, remote signals or barrier semaphores. Data moves between devices by JAX's collectives and lax.ppermute only.
A program may use at most 128 MiB of HBM per device.

v0:
```python
import functools

import jax
import jax.numpy as jnp
import numpy as np
from jax import lax
from jax.experimental import pallas as pl
from jax.experimental.pallas import tpu as pltpu
from jax.sharding import Mesh, PartitionSpec as P

SIZES = {"yh": 2, "z": 8, "core": 2, "x": 4, "yl": 2}
EXPERT_AXES = ("yh", "z", "core")
DP_AXES = ("x", "yl")
Y = ("yh", "yl")
GROUP = 16
WIDTH = 448
PAIR = 2 * WIDTH
LANES = 512
SMALL = pltpu.CompilerParams(vmem_limit_bytes=4 * 2**20)


def ring_size(axes):
    return int(np.prod([SIZES[a] for a in axes]))


def send(value, axes, amount):
    count = ring_size(axes)
    return lax.ppermute(value, axes, [(i, (i + amount) % count) for i in range(count)])


def total(values):
    return functools.reduce(jnp.add, [v.astype(jnp.float32) for v in values]).astype(jnp.bfloat16)


def gather_ring(value, axes):
    return [value] + [send(value, axes, k) for k in range(1, ring_size(axes))]


def reduce_ring(pieces, axes):
    return total([pieces[0]] + [send(piece, axes, -k) for k, piece in enumerate(pieces) if k])


def gather_z(value):
    back, ahead, far = send(value, "z", 1), send(value, "z", -1), send(value, "z", 4)
    back2 = send(jnp.stack([value, back]), "z", 2)
    ahead2 = send(jnp.stack([value, ahead]), "z", -2)
    return run_join([value[None], back[None], back2, far[None], ahead2, ahead[None]])


def run_join(parts):
    vmem = pl.BlockSpec(memory_space=pltpu.VMEM)

    def join_kernel(*refs):
        at = 0
        for ref in refs[:-1]:
            refs[-1][at : at + ref.shape[0]] = ref[...]
            at += ref.shape[0]

    count = sum(p.shape[0] for p in parts)
    return pl.pallas_call(
        join_kernel,
        out_shape=jax.ShapeDtypeStruct((count,) + parts[0].shape[1:], parts[0].dtype),
        in_specs=[vmem] * len(parts),
        out_specs=vmem,
        compiler_params=SMALL,
        name="join",
    )(*parts)


def reduce_z(pieces):
    back2 = send(pieces[2:4], "z", -2)
    ahead2 = send(pieces[5:7], "z", 2)
    far = send(pieces[4], "z", -4)
    back = send(total([pieces[1], back2[1]]), "z", -1)
    ahead = send(total([pieces[7], ahead2[1]]), "z", 1)
    return total([pieces[0], back2[0], ahead2[0], far, back, ahead])


def ride_kernel(place, tokens_ref, routes_ref, gate_ref, out_ref):
    labels = lax.broadcasted_iota(jnp.int32, (2, GROUP, LANES - WIDTH), 2)
    gate = gate_ref[...]
    part = jnp.where(lax.rem(place[3], 2) == 0, gate >> 8, gate & 255)
    routes = routes_ref[...]
    ride = jnp.zeros(labels.shape, jnp.int32)
    for k in range(routes.shape[2]):
        ride = ride + jnp.where(routes[:, :, k : k + 1] == labels, part[:, :, k : k + 1], 0)
    ride = ride.astype(jnp.float32).astype(jnp.bfloat16)
    out_ref[...] = jnp.concatenate([tokens_ref[...], ride], axis=2)


def run_ride(place, tokens, routes, gate_fix):
    vmem = pl.BlockSpec(memory_space=pltpu.VMEM)
    return pl.pallas_call(
        ride_kernel,
        out_shape=jax.ShapeDtypeStruct((2, GROUP, LANES), jnp.bfloat16),
        in_specs=[pl.BlockSpec(memory_space=pltpu.SMEM)] + [vmem] * 3,
        out_specs=vmem,
        compiler_params=SMALL,
        name="ride",
    )(place, tokens, routes, gate_fix)


def merge_kernel(place, *refs):
    for k in range(4):
        y_at = lax.rem(place[3] - k + 4, 4)
        row = pl.multiple_of(lax.div(y_at, 2) * GROUP, GROUP)
        lane = pl.multiple_of(lax.rem(y_at, 2) * LANES, LANES)
        for step in range(2):
            refs[4 + step][pl.ds(row, GROUP), pl.ds(lane, LANES)] = refs[k][step]


def run_merge(place, from_y):
    vmem = pl.BlockSpec(memory_space=pltpu.VMEM)
    return pl.pallas_call(
        merge_kernel,
        out_shape=[jax.ShapeDtypeStruct((2 * GROUP, 2 * LANES), jnp.bfloat16)] * 2,
        in_specs=[pl.BlockSpec(memory_space=pltpu.SMEM)] + [vmem] * 4,
        out_specs=[vmem] * 2,
        compiler_params=SMALL,
        name="merge",
    )(place, *from_y)


def handed_kernel(place, lower_ref, *refs):
    copies = [pltpu.make_async_copy(refs[k].at[place[4]], refs[3 + k], refs[6].at[k]) for k in range(3)]
    for copy in copies:
        copy.start()
    for copy in copies:
        copy.wait()


def run_handed(place, lower, panels):
    hbm = pl.BlockSpec(memory_space=pltpu.HBM)
    return pl.pallas_call(
        handed_kernel,
        out_shape=[jax.ShapeDtypeStruct(p.shape[1:], p.dtype) for p in panels],
        in_specs=[pl.BlockSpec(memory_space=pltpu.SMEM), pl.BlockSpec(memory_space=pltpu.VMEM)] + [hbm] * 3,
        out_specs=[hbm] * 3,
        scratch_shapes=[pltpu.SemaphoreType.DMA((3,))],
        compiler_params=SMALL,
        cost_estimate=pl.CostEstimate(flops=0, bytes_accessed=6 * 2**20, transcendentals=0),
        name="handed",
    )(place, lower, *panels)


def swapped_kernel(place, *refs):
    slot = place[4]
    copies = []
    for k in range(3):
        panel, taken, out = refs[k], refs[3 + k], refs[6 + k]
        copies.append(pltpu.make_async_copy(panel.at[1 - slot], out.at[1 - slot], refs[9].at[2 * k]))
        copies.append(pltpu.make_async_copy(taken, out.at[slot], refs[9].at[2 * k + 1]))
    for copy in copies:
        copy.start()
    for copy in copies:
        copy.wait()


def run_swapped(place, panels, taken):
    hbm = pl.BlockSpec(memory_space=pltpu.HBM)
    return pl.pallas_call(
        swapped_kernel,
        out_shape=[jax.ShapeDtypeStruct(p.shape, p.dtype) for p in panels],
        in_specs=[pl.BlockSpec(memory_space=pltpu.SMEM)] + [hbm] * 6,
        out_specs=[hbm] * 3,
        scratch_shapes=[pltpu.SemaphoreType.DMA((6,))],
        compiler_params=SMALL,
        cost_estimate=pl.CostEstimate(flops=0, bytes_accessed=11 * 2**20, transcendentals=0),
        name="swapped",
    )(place, *panels, *taken)


def layer_kernel(z_last, *refs):
    n_pieces = 1 if z_last else 4
    place, position_ref = refs[:2]
    pieces = refs[2 : 2 + n_pieces]
    gate_own, up_own, down_own, gate_other, up_other, down_other = refs[2 + n_pieces : 8 + n_pieces]
    outs = refs[8 + n_pieces : 8 + 2 * n_pieces]
    count_ref = refs[8 + 2 * n_pieces]
    rows_ref, panel_ref, down_ref, result_ref, sems = refs[9 + 2 * n_pieces :]
    my_x, my_core, chip = place[0], place[1], place[2]

    copies = []
    for q, (gate_w, up_w, slot) in enumerate(
        ((gate_own, up_own, 0), (gate_own, up_own, 1), (gate_other, up_other, 0), (gate_other, up_other, 1))
    ):
        copies.append(
            [
                pltpu.make_async_copy(gate_w.at[slot], panel_ref.at[q, :, :WIDTH, :128], sems.at[2 * q]),
                pltpu.make_async_copy(up_w.at[slot], panel_ref.at[q, :, :WIDTH, 128:], sems.at[2 * q + 1]),
            ]
        )
    copies.append([pltpu.make_async_copy(down_own, down_ref.at[:2], sems.at[8])])
    copies.append([pltpu.make_async_copy(down_other, down_ref.at[2:], sems.at[9])])
    for group in copies:
        for copy in group:
            copy.start()

    for q in range(4):
        panel_ref[q, :, WIDTH:, :] = jnp.zeros((8, LANES - WIDTH, 256), jnp.bfloat16)
    for zr in range(8):
        for xr in range(4):
            x_at = lax.rem(my_x - xr + 4, 4)
            lane = pl.multiple_of(x_at * 2 * LANES, 2 * LANES)
            piece = pieces[0].at[zr, xr] if z_last else pieces[xr].at[zr]
            rows_ref[zr * 2 * GROUP : (zr + 1) * 2 * GROUP, pl.ds(lane, 2 * LANES)] = piece[...]

    gates = rows_ref[:, WIDTH:LANES].astype(jnp.float32) * 256.0
    gates = gates + rows_ref[:, LANES + WIDTH : 2 * LANES].astype(jnp.float32)
    count_ref[...] = jnp.broadcast_to(
        jnp.sum((gates > 0.0).astype(jnp.float32), axis=0, keepdims=True), count_ref.shape
    )
    positions = position_ref[...]
    hidden = []
    for q in range(4):
        stored = chip * 4 + (my_core if q < 2 else 1 - my_core) * 2 + q % 2
        share = jnp.sum(jnp.where(positions == stored, gates, 0.0), axis=1, keepdims=True) * (1.0 / 65536.0)
        for copy in copies[q]:
            copy.wait()
        act = jnp.dot(
            rows_ref[...], panel_ref[q].reshape(8 * LANES, 256), preferred_element_type=jnp.float32
        )
        hidden.append((jax.nn.silu(act[:, :128]) * act[:, 128:] * share).astype(jnp.bfloat16))
    hidden = jnp.concatenate(hidden, axis=1)
    for group in copies[4:]:
        for copy in group:
            copy.wait()
    for x_at in range(4):
        panel = down_ref[:, :, x_at * PAIR : (x_at + 1) * PAIR].reshape(4 * 128, PAIR)
        result_ref[x_at] = jnp.dot(hidden, panel, preferred_element_type=jnp.float32).astype(jnp.bfloat16)

    for zr in range(8):
        for xr in range(4):
            x_at = lax.rem(my_x - xr + 4, 4)
            out = outs[0].at[zr, xr] if z_last else outs[xr].at[zr]
            out[...] = result_ref[x_at, zr * 2 * GROUP : (zr + 1) * 2 * GROUP, :]


def run_layer(z_last, place, position, pieces, weights):
    vmem = pl.BlockSpec(memory_space=pltpu.VMEM)
    shape = pieces[0].shape[:-1] + (PAIR,)
    out = pl.pallas_call(
        functools.partial(layer_kernel, z_last),
        out_shape=[jax.ShapeDtypeStruct(shape, jnp.bfloat16)] * len(pieces)
        + [jax.ShapeDtypeStruct((8, 64), jnp.float32)],
        in_specs=[pl.BlockSpec(memory_space=pltpu.SMEM)]
        + [vmem] * (1 + len(pieces))
        + [pl.BlockSpec(memory_space=pltpu.HBM)] * 6,
        out_specs=[vmem] * (len(pieces) + 1),
        scratch_shapes=[
            pltpu.VMEM((256, 8 * LANES), jnp.bfloat16),
            pltpu.VMEM((4, 8, LANES, 256), jnp.bfloat16),
            pltpu.VMEM((4, 128, 3584), jnp.bfloat16),
            pltpu.VMEM((4, 256, PAIR), jnp.bfloat16),
            pltpu.SemaphoreType.DMA((10,)),
        ],
        compiler_params=pltpu.CompilerParams(vmem_limit_bytes=52 * 2**20),
        cost_estimate=pl.CostEstimate(flops=2 * 256 * 3584 * 1536, bytes_accessed=16 * 2**20, transcendentals=0),
        name="layer_z_last" if z_last else "layer_x_last",
    )(place, position, *pieces, *weights)
    return out[:-1], out[-1]


def after(value, *earlier):
    return lax.optimization_barrier((value, earlier))[0]


def on_device(tokens, routes, gate_fix, position, swap_slot, w_gate, w_up, w_down):
    yh, z, core = (lax.axis_index(a) for a in EXPERT_AXES)
    x, yl = (lax.axis_index(a) for a in DP_AXES)
    own_index = (yh * 8 + z) * 2 + core
    my_y = yh * 2 + yl
    given_slot = lax.dynamic_index_in_dim(swap_slot, own_index, 0, keepdims=False)
    place = jnp.stack([x, core, yh * 8 + z, my_y, given_slot]).astype(jnp.int32)

    lower = run_ride(place, tokens, routes, gate_fix)
    step_rows = run_merge(place, gather_ring(lower, Y))

    swap_core, swap_y = [(0, 1), (1, 0)], [(0, 1), (1, 0)]
    panels = (w_gate.reshape(2, 8, WIDTH, 128), w_up.reshape(2, 8, WIDTH, 128), w_down)
    other = tuple(lax.ppermute(w, "core", swap_core) for w in panels)
    weights = panels + other
    gate_given, up_given, down_given = run_handed(place, lower, panels)
    gate_taken = lax.ppermute(after(gate_given, *step_rows), "yh", swap_y)
    up_taken = lax.ppermute(after(up_given, gate_taken), "yh", swap_y)
    down_taken = lax.ppermute(after(down_given, up_taken), "yh", swap_y)

    piece0 = lax.all_gather(jnp.stack(gather_ring(step_rows[0], "x")), "z")
    pieces1 = gather_ring(gather_z(after(step_rows[1], *other)), "x")
    positions = position.reshape(1, 64)
    out1, counts = run_layer(False, after(place, gate_taken), positions, pieces1, weights)
    out0, _ = run_layer(True, after(place, up_taken, counts), positions, [piece0], weights)

    back0 = lax.psum_scatter(out0[0], "z", scatter_dimension=0)
    back0 = after(back0, down_taken)
    back1 = reduce_ring(out1, "x")
    back1 = reduce_z(back1)
    back0 = reduce_ring([back0[k] for k in range(4)], "x")
    back = jnp.stack([back0, back1]).reshape(2, 2, GROUP, PAIR)
    halves = [back[:, 0, :, :WIDTH], back[:, 0, :, WIDTH:], back[:, 1, :, :WIDTH], back[:, 1, :, WIDTH:]]
    combined = reduce_ring([lax.select_n(lax.rem(my_y - k + 4, 4), *halves) for k in range(4)], Y)

    counts = counts[0] + lax.ppermute(counts[0], "core", swap_core)
    holder, held_slot = position // 2, position % 2
    partner = jnp.bitwise_xor(holder, 16)
    owners = jnp.arange(32, dtype=jnp.int32)
    slot_of = lambda h: jnp.sum(jnp.where(h[:, None] == owners, swap_slot, 0), axis=1)
    new_holder = jnp.where(held_slot == slot_of(holder), partner, holder)
    device_load = (jnp.sum(jnp.where(new_holder == own_index, counts, 0.0)) / 128.0).reshape(1)

    new = run_swapped(place, panels, (gate_taken, up_taken, down_taken))
    return (combined, device_load, *[n.reshape(w.shape) for n, w in zip(new, (w_gate, w_up, w_down))])


def solution(mesh):
    fine = Mesh(mesh.devices.reshape(tuple(SIZES.values())), tuple(SIZES))
    in_specs = (
        P(None, EXPERT_AXES, DP_AXES),
        P(None, EXPERT_AXES, None),
        P(None, EXPERT_AXES, None),
        P(),
        P(),
        P(EXPERT_AXES, None, DP_AXES),
        P(EXPERT_AXES, None, DP_AXES),
        P(EXPERT_AXES, DP_AXES, None),
    )
    out_specs = (
        P(None, EXPERT_AXES, DP_AXES),
        P(EXPERT_AXES),
        P(EXPERT_AXES, None, DP_AXES),
        P(EXPERT_AXES, None, DP_AXES),
        P(EXPERT_AXES, DP_AXES, None),
    )
    return jax.shard_map(on_device, mesh=fine, in_specs=in_specs, out_specs=out_specs, check_vma=False)
```

profile of v0, /device:TPU:24, one launch (start us, length us, event | category | flops | bytes accessed | tf_op | source)
XLA Modules:
  0.0 204.2 jit_solution(9352222315992129379)
XLA Ops:
  8.8 1.2 dynamic_slice.4
  12.2 2.0 collective-permute-start
  15.2 1.0 collective-permute-done.refs_1_
  16.2 3.5 %collective-permute-done.1.refs_2_ = bf16[2,16,512]{2,1,0:T(8,128)(2,1)S(1)} collective-permute-done((bf16[2,16,512]{2,1,0:T(8,128)(2,1)S(1)}, bf16[2,16,512]{2,1,0:T(8,128)(2,1)S(1)}, u32[]{:S(2)}, u32[]{:S(2)}) %collective-permute-start.1) | collective-permute-done | bytes 32800 | tf_op jit(solution)/shard_map/ppermute | solution.py:28
  20.8 2.8 %collective-permute-start.18 = (bf16[32,1024]{1,0:T(8,128)(2,1)S(1)}, bf16[32,1024]{1,0:T(8,128)(2,1)S(1)}, u32[]{:S(2)}, u32[]{:S(2)}) collective-permute-start(bf16[32,1024]{1,0:T(8,128)(2,1)S(1)} %get-tuple-element.28), channel_id=1, source_target_pairs={{0,6},{2,0},{4,2},{6,4},{1,7},{3,1},{5,3},{7,5},{8,14},{10,8},{12,... | collective-permute-start | bytes 196616 | tf_op jit(solution)/shard_map/ppermute | solution.py:28
  25.5 3.9 %collective-permute-done.17 = bf16[32,1024]{1,0:T(8,128)(2,1)S(1)} collective-permute-done((bf16[32,1024]{1,0:T(8,128)(2,1)S(1)}, bf16[32,1024]{1,0:T(8,128)(2,1)S(1)}, u32[]{:S(2)}, u32[]{:S(2)}) %collective-permute-start.17) | collective-permute-done | bytes 65568 | tf_op jit(solution)/shard_map/ppermute | solution.py:28
  31.6 1.5 copy-done
  33.1 1.5 copy-done.2
  34.6 1.5 copy-done.4
  36.1 2.0 handed.1
  38.5 1.7 collective-permute-done.7.refs_11_.refs_8_
  40.3 1.9 collective-permute-start.8
  42.2 3.9 %collective-permute-start.11 = (bf16[32,1024]{1,0:T(8,128)(2,1)S(1)}, bf16[32,1024]{1,0:T(8,128)(2,1)S(1)}, u32[]{:S(2)}, u32[]{:S(2)}) collective-permute-start(bf16[32,1024]{1,0:T(8,128)(2,1)S(1)} %get-tuple-element.33), channel_id=1, source_target_pairs={{0,112},{16,0},{32,16},{48,32},{64,48},{80,64},{96,80},{112,96},{1... | collective-permute-start | bytes 196616 | tf_op jit(solution)/shard_map/ppermute | solution.py:28
  46.1 3.8 %collective-permute-done.8 = bf16[32,1024]{1,0:T(8,128)(2,1)S(1)} collective-permute-done((bf16[32,1024]{1,0:T(8,128)(2,1)S(1)}, bf16[32,1024]{1,0:T(8,128)(2,1)S(1)}, u32[]{:S(2)}, u32[]{:S(2)}) %collective-permute-start.8) | collective-permute-done | bytes 65568 | tf_op jit(solution)/shard_map/ppermute | solution.py:28
  49.9 1.9 collective-permute-start.9
  51.8 2.3 %collective-permute-start.12 = (bf16[2,32,1024]{2,1,0:T(8,128)(2,1)S(1)}, bf16[2,32,1024]{2,1,0:T(8,128)(2,1)S(1)}, u32[]{:S(2)}, u32[]{:S(2)}) collective-permute-start(bf16[2,32,1024]{2,1,0:T(8,128)(2,1)S(1)} %get-tuple-element.61), channel_id=1, source_target_pairs={{0,96},{16,112},{32,0},{48,16},{64,32},{80,48},{96,64},{112,80},{1... | collective-permute-start | bytes 393224 | tf_op jit(solution)/shard_map/ppermute | solution.py:28
  54.1 8.3 %collective-permute-done.3.refs_3_ = bf16[8,448,128]{2,1,0:T(8,128)(2,1)S(1)} collective-permute-done((bf16[8,448,128]{2,1,0:T(8,128)(2,1)S(1)}, bf16[8,448,128]{2,1,0:T(8,128)(2,1)S(1)}, u32[]{:S(2)}, u32[]{:S(2)}) %collective-permute-start.3) | collective-permute-done | bytes 917536 | tf_op jit(solution)/shard_map/ppermute | solution.py:284
  62.7 7.2 %collective-permute-start.10 = (bf16[32,1024]{1,0:T(8,128)(2,1)S(1)}, bf16[32,1024]{1,0:T(8,128)(2,1)S(1)}, u32[]{:S(2)}, u32[]{:S(2)}) collective-permute-start(bf16[32,1024]{1,0:T(8,128)(2,1)S(1)} %get-tuple-element.33), channel_id=1, source_target_pairs={{0,64},{16,80},{32,96},{48,112},{64,0},{80,16},{96,32},{112,48},{1... | collective-permute-start | bytes 196616 | tf_op jit(solution)/shard_map/ppermute | solution.py:28
  69.9 3.8 %collective-permute-done.10 = bf16[32,1024]{1,0:T(8,128)(2,1)S(1)} collective-permute-done((bf16[32,1024]{1,0:T(8,128)(2,1)S(1)}, bf16[32,1024]{1,0:T(8,128)(2,1)S(1)}, u32[]{:S(2)}, u32[]{:S(2)}) %collective-permute-start.10) | collective-permute-done | bytes 65568 | tf_op jit(solution)/shard_map/ppermute | solution.py:28
  73.8 1.9 collective-permute-start.14
  75.8 2.0 collective-permute-start.15
  77.8 21.2 %collective-permute-done.13.refs_3_ = bf16[8,32,1024]{2,1,0:T(8,128)(2,1)S(1)} collective-permute-done((bf16[8,32,1024]{2,1,0:T(8,128)(2,1)S(1)}, bf16[8,32,1024]{2,1,0:T(8,128)(2,1)S(1)}, u32[]{:S(2)}, u32[]{:S(2)}) %collective-permute-start.13) | collective-permute-done | bytes 524320 | tf_op jit(solution)/shard_map/ppermute | solution.py:28
  100.4 9.5 %layer_x_last.1 = (bf16[8,32,896]{2,1,0:T(8,128)(2,1)S(1)}, bf16[8,32,896]{2,1,0:T(8,128)(2,1)S(1)}, bf16[8,32,896]{2,1,0:T(8,128)(2,1)S(1)}, bf16[8,32,896]{2,1,0:T(8,128)(2,1)S(1)}, f32[8,64]{1,0:T(8,128)S(1)}) custom-call(s32[5]{0:T(128)S(1)} %stack.56.place.refs_0_, s32[1,64]{1,0:T(1,128)S(1)} %bitcast.80, bf16[8,32,1024]{2,1,0:T(8,128)(2,1)} %copy-done.6, ...), custom_call_target="tpu_custom_call" | custom-call | flops 2818572288 | bytes 16777216 | tf_op jit(solution)/shard_map/layer_x_last/pallas_call | solution.py:242
  111.4 1.0 copy-done.7
  112.4 10.8 %layer_z_last.1 = (bf16[8,4,32,896]{3,2,1,0:T(8,128)(2,1)}, f32[8,64]{1,0:T(8,128)}) custom-call(s32[5]{0:T(128)S(1)} %stack.56.place.refs_0_, s32[1,64]{1,0:T(1,128)S(1)} %bitcast.81, bf16[8,4,32,1024]{3,2,1,0:T(8,128)(2,1)} %bitcast.82, bf16[2,8,448,128]{3,2,1,0:T(8,128)(2,1)} %bitcast.64, bf16[2,8,448,128]{3,2,1,0:T(8,128)(2,1)} %bitcast.69, ...), custom_call_target="tpu_custom_call" | custom-call | flops 2818572288 | bytes 16777216 | tf_op jit(solution)/shard_map/layer_z_last/pallas_call | solution.py:242
  123.2 0.9 copy-done.16
  124.6 3.6 %collective-permute-start.24 = (bf16[8,32,896]{2,1,0:T(8,128)(2,1)S(1)}, bf16[8,32,896]{2,1,0:T(8,128)(2,1)S(1)}, u32[]{:S(2)}, u32[]{:S(2)}) collective-permute-start(bf16[8,32,896]{2,1,0:T(8,128)(2,1)S(1)} %copy-done.14), channel_id=1, source_target_pairs={{0,4},{2,6},{4,0},{6,2},{1,5},{3,7},{5,1},{7,3},{8,12},{10,14},{12... | collective-permute-start | bytes 1376264 | tf_op jit(solution)/shard_map/ppermute | solution.py:28
  128.3 3.1 %collective-permute-start.19 = (bf16[128,3584]{1,0:T(8,128)(2,1)}, bf16[128,3584]{1,0:T(8,128)(2,1)S(1)}, u32[]{:S(2)}, u32[]{:S(2)}) collective-permute-start(bf16[128,3584]{1,0:T(8,128)(2,1)} %get-tuple-element.38), channel_id=1, source_target_pairs={{0,128},{128,0},{1,129},{129,1},{2,130},{130,2},{3,131},{131,3},{4... | collective-permute-start | bytes 2752520 | tf_op jit(solution)/shard_map/ppermute | solution.py:286
  131.3 5.9 %collective-permute-done.25 = bf16[8,32,896]{2,1,0:T(8,128)(2,1)S(1)} collective-permute-done((bf16[8,32,896]{2,1,0:T(8,128)(2,1)S(1)}, bf16[8,32,896]{2,1,0:T(8,128)(2,1)S(1)}, u32[]{:S(2)}, u32[]{:S(2)}) %collective-permute-start.25) | collective-permute-done | bytes 458784 | tf_op jit(solution)/shard_map/ppermute | solution.py:28
  137.3 11.0 %collective-permute-done.24 = bf16[8,32,896]{2,1,0:T(8,128)(2,1)S(1)} collective-permute-done((bf16[8,32,896]{2,1,0:T(8,128)(2,1)S(1)}, bf16[8,32,896]{2,1,0:T(8,128)(2,1)S(1)}, u32[]{:S(2)}, u32[]{:S(2)}) %collective-permute-start.24) | collective-permute-done | bytes 458784 | tf_op jit(solution)/shard_map/ppermute | solution.py:28
  148.5 5.4 %collective-permute-start.26 = (bf16[2,32,896]{2,1,0:T(8,128)(2,1)S(1)}, bf16[2,32,896]{2,1,0:T(8,128)(2,1)S(1)}, u32[]{:S(2)}, u32[]{:S(2)}) collective-permute-start(bf16[2,32,896]{2,1,0:T(8,128)(2,1)S(1)} %get-tuple-element.54), channel_id=1, source_target_pairs={{0,96},{16,112},{32,0},{48,16},{64,32},{80,48},{96,64},{112,80},{1... | collective-permute-start | bytes 344072 | tf_op jit(solution)/shard_map/ppermute | solution.py:28
  153.9 4.4 %collective-permute-start.28 = (bf16[32,896]{1,0:T(8,128)(2,1)S(1)}, bf16[32,896]{1,0:T(8,128)(2,1)S(1)}, u32[]{:S(2)}, u32[]{:S(2)}) collective-permute-start(bf16[32,896]{1,0:T(8,128)(2,1)S(1)} %slice_bitcast_fusion), channel_id=1, source_target_pairs={{0,64},{16,80},{32,96},{48,112},{64,0},{80,16},{96,32},{112,48},{1... | collective-permute-start | bytes 172040 | tf_op jit(solution)/shard_map/ppermute | solution.py:28
  158.3 4.2 %collective-permute-done.26 = bf16[2,32,896]{2,1,0:T(8,128)(2,1)S(1)} collective-permute-done((bf16[2,32,896]{2,1,0:T(8,128)(2,1)S(1)}, bf16[2,32,896]{2,1,0:T(8,128)(2,1)S(1)}, u32[]{:S(2)}, u32[]{:S(2)}) %collective-permute-start.26) | collective-permute-done | bytes 114720 | tf_op jit(solution)/shard_map/ppermute | solution.py:28
  162.5 3.9 %collective-permute-done.27 = bf16[2,32,896]{2,1,0:T(8,128)(2,1)S(1)} collective-permute-done((bf16[2,32,896]{2,1,0:T(8,128)(2,1)S(1)}, bf16[2,32,896]{2,1,0:T(8,128)(2,1)S(1)}, u32[]{:S(2)}, u32[]{:S(2)}) %collective-permute-start.27) | collective-permute-done | bytes 114720 | tf_op jit(solution)/shard_map/ppermute | solution.py:28
  166.5 3.2 %collective-permute-start.29 = (bf16[32,896]{1,0:T(8,128)(2,1)S(1)}, bf16[32,896]{1,0:T(8,128)(2,1)S(1)}, u32[]{:S(2)}, u32[]{:S(2)}) collective-permute-start(bf16[32,896]{1,0:T(8,128)(2,1)S(1)} %get-tuple-element.52), channel_id=1, source_target_pairs={{0,112},{16,0},{32,16},{48,32},{64,48},{80,64},{96,80},{112,96},{1... | collective-permute-start | bytes 172040 | tf_op jit(solution)/shard_map/ppermute | solution.py:28
  169.8 0.9 copy-done.9
  170.7 1.5 reduce-scatter.2.cloned.1.call-done
  173.1 1.7 collective-permute-start.22
  174.8 2.7 %collective-permute-start.21 = (bf16[32,896]{1,0:T(8,128)(2,1)S(1)}, bf16[32,896]{1,0:T(8,128)(2,1)S(1)}, u32[]{:S(2)}, u32[]{:S(2)}) collective-permute-start(bf16[32,896]{1,0:T(8,128)(2,1)S(1)} %get-tuple-element.58), channel_id=1, source_target_pairs={{0,4},{2,6},{4,0},{6,2},{1,5},{3,7},{5,1},{7,3},{8,12},{10,14},{12... | collective-permute-start | bytes 172040 | tf_op jit(solution)/shard_map/ppermute | solution.py:28
  177.6 1.1 collective-permute-start.20
  179.6 0.9 collective-permute-done.21
  180.5 1.2 collective-permute-done.20
  183.5 2.4 %collective-permute-start.32 = (bf16[2,16,448]{2,1,0:T(8,128)(2,1)S(1)}, bf16[2,16,448]{2,1,0:T(8,128)(2,1)S(1)}, u32[]{:S(2)}, u32[]{:S(2)}) collective-permute-start(bf16[2,16,448]{2,1,0:T(8,128)(2,1)S(1)} %get-tuple-element.59), channel_id=1, source_target_pairs={{0,128},{1,129},{128,0},{129,1},{2,130},{3,131},{130,2},{131,3},{4... | collective-permute-start | bytes 86024 | tf_op jit(solution)/shard_map/ppermute | solution.py:28
  187.1 1.5 copy-done.3
  188.6 1.5 copy-done.5
  190.1 1.2 copy-done.8
  191.3 1.2 copy-done.10
  192.5 3.0 %swapped.1 = (bf16[2,8,448,128]{3,2,1,0:T(8,128)(2,1)}, bf16[2,8,448,128]{3,2,1,0:T(8,128)(2,1)}, bf16[2,128,3584]{2,1,0:T(8,128)(2,1)}) custom-call(s32[5]{0:T(128)S(1)} %stack.56.place.refs_0_, bf16[2,8,448,128]{3,2,1,0:T(8,128)(2,1)S(1)} %bitcast.66, bf16[2,8,448,128]{3,2,1,0:T(8,128)(2,1)S(1)} %bitcast.71, bf16[2,128,3584]{2,1,0:T(8,128)(2,1)S(1)} %copy-done.5, ...), custom_call_target="tpu_custom_call" | custom-call | bytes 11534336 | tf_op jit(solution)/shard_map/swapped/pallas_call | solution.py:161
  (105 shorter events, 19.5 us)
Async XLA Ops:
  7.2 105.2 %all-gather.3.cloned.1.call-start = ((), (), s32[]{:S(2)}) async-start(), calls=%async_computation.2 | async-start | bytes 2359296 | tf_op jit(solution)/shard_map/all_gather | solution.py:288
  12.2 3.9 %collective-permute-start = (bf16[2,16,512]{2,1,0:T(8,128)(2,1)S(1)}, bf16[2,16,512]{2,1,0:T(8,128)(2,1)S(1)}, u32[]{:S(2)}, u32[]{:S(2)}) collective-permute-start(bf16[2,16,512]{2,1,0:T(8,128)(2,1)S(1)} %ride.1.lower_ref.refs_0_), channel_id=1, source_target_pairs={{0,1},{1,128},{128,129},{129,0},{2,3},{3,130},{130,131},{131,2},{4... | collective-permute-start | bytes 98312 | tf_op jit(solution)/shard_map/ppermute | solution.py:28
  14.2 5.4 %collective-permute-start.1 = (bf16[2,16,512]{2,1,0:T(8,128)(2,1)S(1)}, bf16[2,16,512]{2,1,0:T(8,128)(2,1)S(1)}, u32[]{:S(2)}, u32[]{:S(2)}) collective-permute-start(bf16[2,16,512]{2,1,0:T(8,128)(2,1)S(1)} %ride.1.lower_ref.refs_0_), channel_id=1, source_target_pairs={{0,128},{1,129},{128,0},{129,1},{2,130},{3,131},{130,2},{131,3},{4... | collective-permute-start | bytes 98312 | tf_op jit(solution)/shard_map/ppermute | solution.py:28
  15.1 5.1 %collective-permute-start.2 = (bf16[2,16,512]{2,1,0:T(8,128)(2,1)S(1)}, bf16[2,16,512]{2,1,0:T(8,128)(2,1)S(1)}, u32[]{:S(2)}, u32[]{:S(2)}) collective-permute-start(bf16[2,16,512]{2,1,0:T(8,128)(2,1)S(1)} %ride.1.lower_ref.refs_0_), channel_id=1, source_target_pairs={{0,129},{1,0},{128,1},{129,128},{2,131},{3,2},{130,3},{131,130},{4... | collective-permute-start | bytes 98312 | tf_op jit(solution)/shard_map/ppermute | solution.py:28
  20.8 4.7 %collective-permute-start.18 = (bf16[32,1024]{1,0:T(8,128)(2,1)S(1)}, bf16[32,1024]{1,0:T(8,128)(2,1)S(1)}, u32[]{:S(2)}, u32[]{:S(2)}) collective-permute-start(bf16[32,1024]{1,0:T(8,128)(2,1)S(1)} %get-tuple-element.28), channel_id=1, source_target_pairs={{0,6},{2,0},{4,2},{6,4},{1,7},{3,1},{5,3},{7,5},{8,14},{10,8},{12,... | collective-permute-start | bytes 196616 | tf_op jit(solution)/shard_map/ppermute | solution.py:28
  23.6 5.8 %collective-permute-start.17 = (bf16[32,1024]{1,0:T(8,128)(2,1)S(1)}, bf16[32,1024]{1,0:T(8,128)(2,1)S(1)}, u32[]{:S(2)}, u32[]{:S(2)}) collective-permute-start(bf16[32,1024]{1,0:T(8,128)(2,1)S(1)} %get-tuple-element.28), channel_id=1, source_target_pairs={{0,4},{2,6},{4,0},{6,2},{1,5},{3,7},{5,1},{7,3},{8,12},{10,14},{12... | collective-permute-start | bytes 196616 | tf_op jit(solution)/shard_map/ppermute | solution.py:28
  24.4 5.7 %collective-permute-start.16 = (bf16[32,1024]{1,0:T(8,128)(2,1)S(1)}, bf16[32,1024]{1,0:T(8,128)(2,1)S(1)}, u32[]{:S(2)}, u32[]{:S(2)}) collective-permute-start(bf16[32,1024]{1,0:T(8,128)(2,1)S(1)} %get-tuple-element.28), channel_id=1, source_target_pairs={{0,2},{2,4},{4,6},{6,0},{1,3},{3,5},{5,7},{7,1},{8,10},{10,12},{12... | collective-permute-start | bytes 196616 | tf_op jit(solution)/shard_map/ppermute | solution.py:28
  30.9 141.3 %reduce-scatter.2.cloned.1.call-start = ((), (), s32[]{:S(2)}) async-start(), calls=%async_computation.1 | async-start | bytes 2064384 | tf_op jit(solution)/shard_map/reduce_scatter | solution.py:294
  30.9 7.6 %collective-permute-start.5 = (bf16[2,8,448,128]{3,2,1,0:T(8,128)(2,1)}, bf16[2,8,448,128]{3,2,1,0:T(8,128)(2,1)S(1)}, u32[]{:S(2)}, u32[]{:S(2)}) collective-permute-start(bf16[2,8,448,128]{3,2,1,0:T(8,128)(2,1)} %bitcast.62), channel_id=1, source_target_pairs={{0,8},{8,0},{1,9},{9,1},{2,10},{10,2},{3,11},{11,3},{4,12},{12,4},... | collective-permute-start | bytes 5505032 | tf_op jit(solution)/shard_map/ppermute | solution.py:281
  31.0 69.4 %copy-start.12 = (s32[64]{0:T(128)S(1)}, s32[64]{0:T(128)}, u32[]{:S(2)}) copy-start(s32[64]{0:T(128)} %param.11) | copy-start | bytes 772
  31.0 7.5 %collective-permute-start.6 = (bf16[2,8,448,128]{3,2,1,0:T(8,128)(2,1)}, bf16[2,8,448,128]{3,2,1,0:T(8,128)(2,1)S(1)}, u32[]{:S(2)}, u32[]{:S(2)}) collective-permute-start(bf16[2,8,448,128]{3,2,1,0:T(8,128)(2,1)} %bitcast.67), channel_id=1, source_target_pairs={{0,8},{8,0},{1,9},{9,1},{2,10},{10,2},{3,11},{11,3},{4,12},{12,4},... | collective-permute-start | bytes 5505032 | tf_op jit(solution)/shard_map/ppermute | solution.py:281
  31.5 8.7 %collective-permute-start.7 = (bf16[2,128,3584]{2,1,0:T(8,128)(2,1)}, bf16[2,128,3584]{2,1,0:T(8,128)(2,1)S(1)}, u32[]{:S(2)}, u32[]{:S(2)}) collective-permute-start(bf16[2,128,3584]{2,1,0:T(8,128)(2,1)} %refs_2_.3), channel_id=1, source_target_pairs={{0,8},{8,0},{1,9},{9,1},{2,10},{10,2},{3,11},{11,3},{4,12},{12,4},... | collective-permute-start | bytes 5505032 | tf_op jit(solution)/shard_map/ppermute | solution.py:281
  31.6 1.5 copy-start
  33.1 1.5 copy-start.2
  38.1 24.3 %collective-permute-start.3 = (bf16[8,448,128]{2,1,0:T(8,128)(2,1)S(1)}, bf16[8,448,128]{2,1,0:T(8,128)(2,1)S(1)}, u32[]{:S(2)}, u32[]{:S(2)}) collective-permute-start(bf16[8,448,128]{2,1,0:T(8,128)(2,1)S(1)} %get-tuple-element.30), channel_id=1, source_target_pairs={{0,128},{128,0},{1,129},{129,1},{2,130},{130,2},{3,131},{131,3},{4... | collective-permute-start | bytes 2752520 | tf_op jit(solution)/shard_map/ppermute | solution.py:284
  38.5 61.8 %copy-start.17 = (bf16[2,8,448,128]{3,2,1,0:T(8,128)(2,1)}, bf16[2,8,448,128]{3,2,1,0:T(8,128)(2,1)S(1)}, u32[]{:S(2)}) copy-start(bf16[2,8,448,128]{3,2,1,0:T(8,128)(2,1)S(1)} %collective-permute-done.5.refs_9_.refs_6_) | copy-start | bytes 5505028
  38.5 61.8 %copy-start.18 = (bf16[2,8,448,128]{3,2,1,0:T(8,128)(2,1)}, bf16[2,8,448,128]{3,2,1,0:T(8,128)(2,1)S(1)}, u32[]{:S(2)}) copy-start(bf16[2,8,448,128]{3,2,1,0:T(8,128)(2,1)S(1)} %collective-permute-done.6.refs_10_.refs_7_) | copy-start | bytes 5505028
  40.3 60.1 %copy-start.19 = (bf16[2,128,3584]{2,1,0:T(8,128)(2,1)}, bf16[2,128,3584]{2,1,0:T(8,128)(2,1)S(1)}, u32[]{:S(2)}) copy-start(bf16[2,128,3584]{2,1,0:T(8,128)(2,1)S(1)} %collective-permute-done.7.refs_11_.refs_8_) | copy-start | bytes 5505028
  40.3 9.6 %collective-permute-start.8 = (bf16[32,1024]{1,0:T(8,128)(2,1)S(1)}, bf16[32,1024]{1,0:T(8,128)(2,1)S(1)}, u32[]{:S(2)}, u32[]{:S(2)}) collective-permute-start(bf16[32,1024]{1,0:T(8,128)(2,1)S(1)} %get-tuple-element.33), channel_id=1, source_target_pairs={{0,16},{16,32},{32,48},{48,64},{64,80},{80,96},{96,112},{112,0},{1... | collective-permute-start | bytes 196616 | tf_op jit(solution)/shard_map/ppermute | solution.py:28
  42.2 7.7 %collective-permute-start.11 = (bf16[32,1024]{1,0:T(8,128)(2,1)S(1)}, bf16[32,1024]{1,0:T(8,128)(2,1)S(1)}, u32[]{:S(2)}, u32[]{:S(2)}) collective-permute-start(bf16[32,1024]{1,0:T(8,128)(2,1)S(1)} %get-tuple-element.33), channel_id=1, source_target_pairs={{0,112},{16,0},{32,16},{48,32},{64,48},{80,64},{96,80},{112,96},{1... | collective-permute-start | bytes 196616 | tf_op jit(solution)/shard_map/ppermute | solution.py:28
  49.9 23.8 %collective-permute-start.9 = (bf16[2,32,1024]{2,1,0:T(8,128)(2,1)S(1)}, bf16[2,32,1024]{2,1,0:T(8,128)(2,1)S(1)}, u32[]{:S(2)}, u32[]{:S(2)}) collective-permute-start(bf16[2,32,1024]{2,1,0:T(8,128)(2,1)S(1)} %get-tuple-element.62), channel_id=1, source_target_pairs={{0,32},{16,48},{32,64},{48,80},{64,96},{80,112},{96,0},{112,16},{1... | collective-permute-start | bytes 393224 | tf_op jit(solution)/shard_map/ppermute | solution.py:28
  51.8 21.9 %collective-permute-start.12 = (bf16[2,32,1024]{2,1,0:T(8,128)(2,1)S(1)}, bf16[2,32,1024]{2,1,0:T(8,128)(2,1)S(1)}, u32[]{:S(2)}, u32[]{:S(2)}) collective-permute-start(bf16[2,32,1024]{2,1,0:T(8,128)(2,1)S(1)} %get-tuple-element.61), channel_id=1, source_target_pairs={{0,96},{16,112},{32,0},{48,16},{64,32},{80,48},{96,64},{112,80},{1... | collective-permute-start | bytes 393224 | tf_op jit(solution)/shard_map/ppermute | solution.py:28
  62.4 49.0 %collective-permute-start.4 = (bf16[8,448,128]{2,1,0:T(8,128)(2,1)S(1)}, bf16[8,448,128]{2,1,0:T(8,128)(2,1)S(1)}, u32[]{:S(2)}, u32[]{:S(2)}) collective-permute-start(bf16[8,448,128]{2,1,0:T(8,128)(2,1)S(1)} %get-tuple-element.31), channel_id=1, source_target_pairs={{0,128},{128,0},{1,129},{129,1},{2,130},{130,2},{3,131},{131,3},{4... | collective-permute-start | bytes 2752520 | tf_op jit(solution)/shard_map/ppermute | solution.py:285
  62.7 11.0 %collective-permute-start.10 = (bf16[32,1024]{1,0:T(8,128)(2,1)S(1)}, bf16[32,1024]{1,0:T(8,128)(2,1)S(1)}, u32[]{:S(2)}, u32[]{:S(2)}) collective-permute-start(bf16[32,1024]{1,0:T(8,128)(2,1)S(1)} %get-tuple-element.33), channel_id=1, source_target_pairs={{0,64},{16,80},{32,96},{48,112},{64,0},{80,16},{96,32},{112,48},{1... | collective-permute-start | bytes 196616 | tf_op jit(solution)/shard_map/ppermute | solution.py:28
  73.7 26.6 %copy-start.6 = (bf16[8,32,1024]{2,1,0:T(8,128)(2,1)}, bf16[8,32,1024]{2,1,0:T(8,128)(2,1)S(1)}, u32[]{:S(2)}) copy-start(bf16[8,32,1024]{2,1,0:T(8,128)(2,1)S(1)} %join.1.refs_2_) | copy-start | bytes 1572868
  73.8 25.2 %collective-permute-start.13 = (bf16[8,32,1024]{2,1,0:T(8,128)(2,1)S(1)}, bf16[8,32,1024]{2,1,0:T(8,128)(2,1)S(1)}, u32[]{:S(2)}, u32[]{:S(2)}) collective-permute-start(bf16[8,32,1024]{2,1,0:T(8,128)(2,1)S(1)} %join.1.refs_2_), channel_id=1, source_target_pairs={{0,2},{2,4},{4,6},{6,0},{1,3},{3,5},{5,7},{7,1},{8,10},{10,12},{12... | collective-permute-start | bytes 1572872 | tf_op jit(solution)/shard_map/ppermute | solution.py:28
  73.8 25.1 %collective-permute-start.14 = (bf16[8,32,1024]{2,1,0:T(8,128)(2,1)S(1)}, bf16[8,32,1024]{2,1,0:T(8,128)(2,1)S(1)}, u32[]{:S(2)}, u32[]{:S(2)}) collective-permute-start(bf16[8,32,1024]{2,1,0:T(8,128)(2,1)S(1)} %join.1.refs_2_), channel_id=1, source_target_pairs={{0,4},{2,6},{4,0},{6,2},{1,5},{3,7},{5,1},{7,3},{8,12},{10,14},{12... | collective-permute-start | bytes 1572872 | tf_op jit(solution)/shard_map/ppermute | solution.py:28
  75.8 23.8 %collective-permute-start.15 = (bf16[8,32,1024]{2,1,0:T(8,128)(2,1)S(1)}, bf16[8,32,1024]{2,1,0:T(8,128)(2,1)S(1)}, u32[]{:S(2)}, u32[]{:S(2)}) collective-permute-start(bf16[8,32,1024]{2,1,0:T(8,128)(2,1)S(1)} %join.1.refs_2_), channel_id=1, source_target_pairs={{0,6},{2,0},{4,2},{6,4},{1,7},{3,1},{5,3},{7,5},{8,14},{10,8},{12,... | collective-permute-start | bytes 1572872 | tf_op jit(solution)/shard_map/ppermute | solution.py:28
  123.2 5.0 %copy-start.24 = (s32[32]{0:T(128)S(1)}, s32[32]{0:T(128)}, u32[]{:S(2)}) copy-start(s32[32]{0:T(128)} %param.12) | copy-start | bytes 388
  124.2 13.1 %collective-permute-start.25 = (bf16[8,32,896]{2,1,0:T(8,128)(2,1)S(1)}, bf16[8,32,896]{2,1,0:T(8,128)(2,1)S(1)}, u32[]{:S(2)}, u32[]{:S(2)}) collective-permute-start(bf16[8,32,896]{2,1,0:T(8,128)(2,1)S(1)} %copy-done.16), channel_id=1, source_target_pairs={{0,2},{2,4},{4,6},{6,0},{1,3},{3,5},{5,7},{7,1},{8,10},{10,12},{12... | collective-permute-start | bytes 1376264 | tf_op jit(solution)/shard_map/ppermute | solution.py:28
  124.6 23.7 %collective-permute-start.24 = (bf16[8,32,896]{2,1,0:T(8,128)(2,1)S(1)}, bf16[8,32,896]{2,1,0:T(8,128)(2,1)S(1)}, u32[]{:S(2)}, u32[]{:S(2)}) collective-permute-start(bf16[8,32,896]{2,1,0:T(8,128)(2,1)S(1)} %copy-done.14), channel_id=1, source_target_pairs={{0,4},{2,6},{4,0},{6,2},{1,5},{3,7},{5,1},{7,3},{8,12},{10,14},{12... | collective-permute-start | bytes 1376264 | tf_op jit(solution)/shard_map/ppermute | solution.py:28
  128.2 20.1 %collective-permute-start.23 = (bf16[8,32,896]{2,1,0:T(8,128)(2,1)S(1)}, bf16[8,32,896]{2,1,0:T(8,128)(2,1)S(1)}, u32[]{:S(2)}, u32[]{:S(2)}) collective-permute-start(bf16[8,32,896]{2,1,0:T(8,128)(2,1)S(1)} %get-tuple-element.41), channel_id=1, source_target_pairs={{0,6},{2,0},{4,2},{6,4},{1,7},{3,1},{5,3},{7,5},{8,14},{10,8},{12,... | collective-permute-start | bytes 1376264 | tf_op jit(solution)/shard_map/ppermute | solution.py:28
  128.3 41.5 %collective-permute-start.19 = (bf16[128,3584]{1,0:T(8,128)(2,1)}, bf16[128,3584]{1,0:T(8,128)(2,1)S(1)}, u32[]{:S(2)}, u32[]{:S(2)}) collective-permute-start(bf16[128,3584]{1,0:T(8,128)(2,1)} %get-tuple-element.38), channel_id=1, source_target_pairs={{0,128},{128,0},{1,129},{129,1},{2,130},{130,2},{3,131},{131,3},{4... | collective-permute-start | bytes 2752520 | tf_op jit(solution)/shard_map/ppermute | solution.py:286
  131.3 54.5 %collective-permute-start.34 = (f32[64]{0:T(128)S(1)}, f32[64]{0:T(128)S(1)}, u32[]{:S(2)}, u32[]{:S(2)}) collective-permute-start(f32[64]{0:T(128)S(1)} %slice_bitcast_fusion.4), channel_id=1, source_target_pairs={{0,8},{8,0},{1,9},{9,1},{2,10},{10,2},{3,11},{11,3},{4,12},{12,4},... | collective-permute-start | bytes 776 | tf_op jit(solution)/shard_map/ppermute | solution.py:303
  148.3 38.8 %copy-start.1 = (bf16[2,3584,128]{2,1,0:T(8,128)(2,1)S(1)}, bf16[2,3584,128]{2,1,0:T(8,128)(2,1)}, u32[]{:S(2)}) copy-start(bf16[2,3584,128]{2,1,0:T(8,128)(2,1)} %param.13) | copy-start | bytes 5505028
  148.5 18.0 %copy-start.20 = (bf16[8,32,896]{2,1,0:T(8,128)(2,1)}, bf16[8,32,896]{2,1,0:T(8,128)(2,1)S(1)}, u32[]{:S(2)}) copy-start(bf16[8,32,896]{2,1,0:T(8,128)(2,1)S(1)} %add_convert_fusion) | copy-start | bytes 1376260
  148.5 14.0 %collective-permute-start.26 = (bf16[2,32,896]{2,1,0:T(8,128)(2,1)S(1)}, bf16[2,32,896]{2,1,0:T(8,128)(2,1)S(1)}, u32[]{:S(2)}, u32[]{:S(2)}) collective-permute-start(bf16[2,32,896]{2,1,0:T(8,128)(2,1)S(1)} %get-tuple-element.54), channel_id=1, source_target_pairs={{0,96},{16,112},{32,0},{48,16},{64,32},{80,48},{96,64},{112,80},{1... | collective-permute-start | bytes 344072 | tf_op jit(solution)/shard_map/ppermute | solution.py:28
  153.9 12.5 %collective-permute-start.27 = (bf16[2,32,896]{2,1,0:T(8,128)(2,1)S(1)}, bf16[2,32,896]{2,1,0:T(8,128)(2,1)S(1)}, u32[]{:S(2)}, u32[]{:S(2)}) collective-permute-start(bf16[2,32,896]{2,1,0:T(8,128)(2,1)S(1)} %get-tuple-element.55), channel_id=1, source_target_pairs={{0,32},{16,48},{32,64},{48,80},{64,96},{80,112},{96,0},{112,16},{1... | collective-permute-start | bytes 344072 | tf_op jit(solution)/shard_map/ppermute | solution.py:28
  153.9 20.9 %collective-permute-start.28 = (bf16[32,896]{1,0:T(8,128)(2,1)S(1)}, bf16[32,896]{1,0:T(8,128)(2,1)S(1)}, u32[]{:S(2)}, u32[]{:S(2)}) collective-permute-start(bf16[32,896]{1,0:T(8,128)(2,1)S(1)} %slice_bitcast_fusion), channel_id=1, source_target_pairs={{0,64},{16,80},{32,96},{48,112},{64,0},{80,16},{96,32},{112,48},{1... | collective-permute-start | bytes 172040 | tf_op jit(solution)/shard_map/ppermute | solution.py:28
  166.4 11.1 %collective-permute-start.30 = (bf16[32,896]{1,0:T(8,128)(2,1)S(1)}, bf16[32,896]{1,0:T(8,128)(2,1)S(1)}, u32[]{:S(2)}, u32[]{:S(2)}) collective-permute-start(bf16[32,896]{1,0:T(8,128)(2,1)S(1)} %get-tuple-element.53), channel_id=1, source_target_pairs={{0,16},{16,32},{32,48},{48,64},{64,80},{80,96},{96,112},{112,0},{1... | collective-permute-start | bytes 172040 | tf_op jit(solution)/shard_map/ppermute | solution.py:28
  166.5 12.1 %collective-permute-start.29 = (bf16[32,896]{1,0:T(8,128)(2,1)S(1)}, bf16[32,896]{1,0:T(8,128)(2,1)S(1)}, u32[]{:S(2)}, u32[]{:S(2)}) collective-permute-start(bf16[32,896]{1,0:T(8,128)(2,1)S(1)} %get-tuple-element.52), channel_id=1, source_target_pairs={{0,112},{16,0},{32,16},{48,32},{64,48},{80,64},{96,80},{112,96},{1... | collective-permute-start | bytes 172040 | tf_op jit(solution)/shard_map/ppermute | solution.py:28
  173.1 6.5 %collective-permute-start.22 = (bf16[32,896]{1,0:T(8,128)(2,1)S(1)}, bf16[32,896]{1,0:T(8,128)(2,1)S(1)}, u32[]{:S(2)}, u32[]{:S(2)}) collective-permute-start(bf16[32,896]{1,0:T(8,128)(2,1)S(1)} %get-tuple-element.57), channel_id=1, source_target_pairs={{0,2},{2,4},{4,6},{6,0},{1,3},{3,5},{5,7},{7,1},{8,10},{10,12},{12... | collective-permute-start | bytes 172040 | tf_op jit(solution)/shard_map/ppermute | solution.py:28
  174.8 5.7 %collective-permute-start.21 = (bf16[32,896]{1,0:T(8,128)(2,1)S(1)}, bf16[32,896]{1,0:T(8,128)(2,1)S(1)}, u32[]{:S(2)}, u32[]{:S(2)}) collective-permute-start(bf16[32,896]{1,0:T(8,128)(2,1)S(1)} %get-tuple-element.58), channel_id=1, source_target_pairs={{0,4},{2,6},{4,0},{6,2},{1,5},{3,7},{5,1},{7,3},{8,12},{10,14},{12... | collective-permute-start | bytes 172040 | tf_op jit(solution)/shard_map/ppermute | solution.py:28
  177.6 4.2 %collective-permute-start.20 = (bf16[32,896]{1,0:T(8,128)(2,1)S(1)}, bf16[32,896]{1,0:T(8,128)(2,1)S(1)}, u32[]{:S(2)}, u32[]{:S(2)}) collective-permute-start(bf16[32,896]{1,0:T(8,128)(2,1)S(1)} %get-tuple-element.56), channel_id=1, source_target_pairs={{0,6},{2,0},{4,2},{6,4},{1,7},{3,1},{5,3},{7,5},{8,14},{10,8},{12,... | collective-permute-start | bytes 172040 | tf_op jit(solution)/shard_map/ppermute | solution.py:28
  182.7 12.8 %collective-permute-start.33 = (bf16[2,16,448]{2,1,0:T(8,128)(2,1)S(1)}, bf16[2,16,448]{2,1,0:T(8,128)(2,1)S(1)}, u32[]{:S(2)}, u32[]{:S(2)}) collective-permute-start(bf16[2,16,448]{2,1,0:T(8,128)(2,1)S(1)} %get-tuple-element.60), channel_id=1, source_target_pairs={{0,1},{1,128},{128,129},{129,0},{2,3},{3,130},{130,131},{131,2},{4... | collective-permute-start | bytes 86024 | tf_op jit(solution)/shard_map/ppermute | solution.py:28
  183.5 12.1 %collective-permute-start.32 = (bf16[2,16,448]{2,1,0:T(8,128)(2,1)S(1)}, bf16[2,16,448]{2,1,0:T(8,128)(2,1)S(1)}, u32[]{:S(2)}, u32[]{:S(2)}) collective-permute-start(bf16[2,16,448]{2,1,0:T(8,128)(2,1)S(1)} %get-tuple-element.59), channel_id=1, source_target_pairs={{0,128},{1,129},{128,0},{129,1},{2,130},{3,131},{130,2},{131,3},{4... | collective-permute-start | bytes 86024 | tf_op jit(solution)/shard_map/ppermute | solution.py:28
  185.8 9.7 %collective-permute-start.31 = (bf16[2,16,448]{2,1,0:T(8,128)(2,1)S(1)}, bf16[2,16,448]{2,1,0:T(8,128)(2,1)S(1)}, u32[]{:S(2)}, u32[]{:S(2)}) collective-permute-start(bf16[2,16,448]{2,1,0:T(8,128)(2,1)S(1)} %get-tuple-element.47), channel_id=1, source_target_pairs={{0,129},{1,0},{128,1},{129,128},{2,131},{3,2},{130,3},{131,130},{4... | collective-permute-start | bytes 86024 | tf_op jit(solution)/shard_map/ppermute | solution.py:28
  187.1 1.5 copy-start.3
  (14 other events, 15.7 us)
Sparse Core Ops, SparseCore 0:
  31.0 49.2 all-gather.2
  123.3 48.8 reduce-scatter.1
where the time goes:
time: 207 us; the launch traced here: 204 us
  waiting for transfers between devices  77.9 us (38%)
  starting transfers between devices  59 us (29%)
  Pallas kernels  26.6 us (13%)
  local copies, waits for them, and re-layouts  20.2 us (10%)
  between operations  16.2 us (8%)
  other arithmetic  4.23 us (2%)
    ppermute x28, waiting for transfers between devices, send(): lax.ppermute(value, axes, [(i, (i + amount) % count) for i in range(count)])  66.4 us
    ppermute x28, starting transfers between devices, send(): lax.ppermute(value, axes, [(i, (i + amount) % count) for i in range(count)])  54.5 us
    pallas_call x2, Pallas kernels, run_layer(): pl.pallas_call(functools.partial(layer_kernel, z_last), out_shape=[jax.Sh...  20.2 us
    unnamed x52, local copies, waits for them, and re-layouts  17.3 us
    ppermute x1, waiting for transfers between devices, on_device(): gate_taken = lax.ppermute(after(gate_given, *step_rows), 'yh', swap_y)  8.27 us
  transfers between devices with their start and end apart: 37, of which 19 were waited for; matrix products, arithmetic and copies ran while one was open for 2% of the time, Pallas kernels for 7%

commit v1 on v0

--- a/solution.py
+++ b/solution.py
@@ -16,6 +16,7 @@
 WIDTH = 448
 PAIR = 2 * WIDTH
 LANES = 512
+LARGE = pltpu.CompilerParams(vmem_limit_bytes=60 * 2**20)
 SMALL = pltpu.CompilerParams(vmem_limit_bytes=4 * 2**20)
 
 
@@ -137,7 +138,7 @@
         in_specs=[pl.BlockSpec(memory_space=pltpu.SMEM), pl.BlockSpec(memory_space=pltpu.VMEM)] + [hbm] * 3,
         out_specs=[hbm] * 3,
         scratch_shapes=[pltpu.SemaphoreType.DMA((3,))],
-        compiler_params=SMALL,
+        compiler_params=LARGE,
         cost_estimate=pl.CostEstimate(flops=0, bytes_accessed=6 * 2**20, transcendentals=0),
         name="handed",
     )(place, lower, *panels)
@@ -164,21 +165,19 @@
         in_specs=[pl.BlockSpec(memory_space=pltpu.SMEM)] + [hbm] * 6,
         out_specs=[hbm] * 3,
         scratch_shapes=[pltpu.SemaphoreType.DMA((6,))],
-        compiler_params=SMALL,
+        compiler_params=LARGE,
         cost_estimate=pl.CostEstimate(flops=0, bytes_accessed=11 * 2**20, transcendentals=0),
         name="swapped",
     )(place, *panels, *taken)
 
 
-def layer_kernel(z_last, *refs):
-    n_pieces = 1 if z_last else 4
-    place, position_ref = refs[:2]
-    pieces = refs[2 : 2 + n_pieces]
-    gate_own, up_own, down_own, gate_other, up_other, down_other = refs[2 + n_pieces : 8 + n_pieces]
-    outs = refs[8 + n_pieces : 8 + 2 * n_pieces]
-    count_ref = refs[8 + 2 * n_pieces]
-    rows_ref, panel_ref, down_ref, result_ref, sems = refs[9 + 2 * n_pieces :]
+def layer_kernel(place, position_ref, *refs):
+    piece0, pieces1 = refs[0], refs[1:5]
+    gate_own, up_own, down_own, gate_other, up_other, down_other = refs[5:11]
+    out0, outs1, count_ref = refs[11], refs[12:16], refs[16]
+    rows_ref, panel_ref, down_ref, result_ref, sems = refs[17:]
     my_x, my_core, chip = place[0], place[1], place[2]
+    span = 2 * GROUP
 
     copies = []
     for q, (gate_w, up_w, slot) in enumerate(
@@ -198,17 +197,17 @@
 
     for q in range(4):
         panel_ref[q, :, WIDTH:, :] = jnp.zeros((8, LANES - WIDTH, 256), jnp.bfloat16)
-    for zr in range(8):
-        for xr in range(4):
-            x_at = lax.rem(my_x - xr + 4, 4)
-            lane = pl.multiple_of(x_at * 2 * LANES, 2 * LANES)
-            piece = pieces[0].at[zr, xr] if z_last else pieces[xr].at[zr]
-            rows_ref[zr * 2 * GROUP : (zr + 1) * 2 * GROUP, pl.ds(lane, 2 * LANES)] = piece[...]
+    for xr in range(4):
+        x_at = lax.rem(my_x - xr + 4, 4)
+        lanes = pl.ds(pl.multiple_of(x_at * 2 * LANES, 2 * LANES), 2 * LANES)
+        for zr in range(8):
+            rows_ref[zr * span : (zr + 1) * span, lanes] = piece0[zr, xr]
+            rows_ref[(8 + zr) * span : (9 + zr) * span, lanes] = pieces1[xr][zr]
 
     gates = rows_ref[:, WIDTH:LANES].astype(jnp.float32) * 256.0
     gates = gates + rows_ref[:, LANES + WIDTH : 2 * LANES].astype(jnp.float32)
     count_ref[...] = jnp.broadcast_to(
-        jnp.sum((gates > 0.0).astype(jnp.float32), axis=0, keepdims=True), count_ref.shape
+        jnp.sum((gates[8 * span :] > 0.0).astype(jnp.float32), axis=0, keepdims=True), count_ref.shape
     )
     positions = position_ref[...]
     hidden = []
@@ -229,36 +228,36 @@
         panel = down_ref[:, :, x_at * PAIR : (x_at + 1) * PAIR].reshape(4 * 128, PAIR)
         result_ref[x_at] = jnp.dot(hidden, panel, preferred_element_type=jnp.float32).astype(jnp.bfloat16)
 
-    for zr in range(8):
-        for xr in range(4):
-            x_at = lax.rem(my_x - xr + 4, 4)
-            out = outs[0].at[zr, xr] if z_last else outs[xr].at[zr]
-            out[...] = result_ref[x_at, zr * 2 * GROUP : (zr + 1) * 2 * GROUP, :]
-
-
-def run_layer(z_last, place, position, pieces, weights):
+    for xr in range(4):
+        x_at = lax.rem(my_x - xr + 4, 4)
+        for zr in range(8):
+            out0[zr, xr] = result_ref[x_at, zr * span : (zr + 1) * span, :]
+            outs1[xr][zr] = result_ref[x_at, (8 + zr) * span : (9 + zr) * span, :]
+
+
+def run_layer(place, position, piece0, pieces1, weights):
     vmem = pl.BlockSpec(memory_space=pltpu.VMEM)
-    shape = pieces[0].shape[:-1] + (PAIR,)
     out = pl.pallas_call(
-        functools.partial(layer_kernel, z_last),
-        out_shape=[jax.ShapeDtypeStruct(shape, jnp.bfloat16)] * len(pieces)
+        layer_kernel,
+        out_shape=[jax.ShapeDtypeStruct((8, 4, 2 * GROUP, PAIR), jnp.bfloat16)]
+        + [jax.ShapeDtypeStruct((8, 2 * GROUP, PAIR), jnp.bfloat16)] * 4
         + [jax.ShapeDtypeStruct((8, 64), jnp.float32)],
         in_specs=[pl.BlockSpec(memory_space=pltpu.SMEM)]
-        + [vmem] * (1 + len(pieces))
+        + [vmem] * 6
         + [pl.BlockSpec(memory_space=pltpu.HBM)] * 6,
-        out_specs=[vmem] * (len(pieces) + 1),
+        out_specs=[vmem] * 6,
         scratch_shapes=[
-            pltpu.VMEM((256, 8 * LANES), jnp.bfloat16),
+            pltpu.VMEM((512, 8 * LANES), jnp.bfloat16),
             pltpu.VMEM((4, 8, LANES, 256), jnp.bfloat16),
             pltpu.VMEM((4, 128, 3584), jnp.bfloat16),
-            pltpu.VMEM((4, 256, PAIR), jnp.bfloat16),
+            pltpu.VMEM((4, 512, PAIR), jnp.bfloat16),
             pltpu.SemaphoreType.DMA((10,)),
         ],
         compiler_params=pltpu.CompilerParams(vmem_limit_bytes=52 * 2**20),
-        cost_estimate=pl.CostEstimate(flops=2 * 256 * 3584 * 1536, bytes_accessed=16 * 2**20, transcendentals=0),
-        name="layer_z_last" if z_last else "layer_x_last",
-    )(place, position, *pieces, *weights)
-    return out[:-1], out[-1]
+        cost_estimate=pl.CostEstimate(flops=2 * 512 * 3584 * 1536, bytes_accessed=20 * 2**20, transcendentals=0),
+        name="layer",
+    )(place, position, piece0, *pieces1, *weights)
+    return out[0], out[1:5], out[5]
 
 
 def after(value, *earlier):
@@ -282,17 +281,16 @@
     weights = panels + other
     gate_given, up_given, down_given = run_handed(place, lower, panels)
     gate_taken = lax.ppermute(after(gate_given, *step_rows), "yh", swap_y)
-    up_taken = lax.ppermute(after(up_given, gate_taken), "yh", swap_y)
+    piece0 = lax.all_gather(jnp.stack(gather_ring(step_rows[0], "x")), "z")
+    over_z = gather_z(after(step_rows[1], *other))
+    up_taken = lax.ppermute(after(up_given, gate_taken, over_z), "yh", swap_y)
     down_taken = lax.ppermute(after(down_given, up_taken), "yh", swap_y)
-
-    piece0 = lax.all_gather(jnp.stack(gather_ring(step_rows[0], "x")), "z")
-    pieces1 = gather_ring(gather_z(after(step_rows[1], *other)), "x")
-    positions = position.reshape(1, 64)
-    out1, counts = run_layer(False, after(place, gate_taken), positions, pieces1, weights)
-    out0, _ = run_layer(True, after(place, up_taken, counts), positions, [piece0], weights)
-
-    back0 = lax.psum_scatter(out0[0], "z", scatter_dimension=0)
-    back0 = after(back0, down_taken)
+    pieces1 = gather_ring(over_z, "x")
+    out0, out1, counts = run_layer(after(place, up_taken), position.reshape(1, 64), piece0, pieces1, weights)
+    new = run_swapped(place, panels, (gate_taken, up_taken, down_taken))
+
+    back0 = lax.psum_scatter(out0, "z", scatter_dimension=0)
+    back0 = after(back0, *new)
     back1 = reduce_ring(out1, "x")
     back1 = reduce_z(back1)
     back0 = reduce_ring([back0[k] for k in range(4)], "x")
@@ -308,7 +306,6 @@
     new_holder = jnp.where(held_slot == slot_of(holder), partner, holder)
     device_load = (jnp.sum(jnp.where(new_holder == own_index, counts, 0.0)) / 128.0).reshape(1)
 
-    new = run_swapped(place, panels, (gate_taken, up_taken, down_taken))
     return (combined, device_load, *[n.reshape(w.shape) for n, w in zip(new, (w_gate, w_up, w_down))])
 
 

time: 207 us -> 428 us (2.07)
  Pallas kernels: 26.6 us -> 272 us
  local copies, waits for them, and re-layouts: 20.2 us -> 7.65 us
  waiting for transfers between devices: 77.9 us -> 67.8 us
    pallas_call x1, Pallas kernels: 3.03 us -> 169 us  [run_swapped(): pl.pallas_call(swapped_kernel, out_shape=[jax.ShapeDtypeStruct(p.shape, p...]
    pallas_call x1, Pallas kernels: 1.98 us -> 85.3 us  [run_handed(): pl.pallas_call(handed_kernel, out_shape=[jax.ShapeDtypeStruct(p.shape[1:]...]
    ppermute x28, waiting for transfers between devices: 66.4 us -> 33.1 us  [send(): lax.ppermute(value, axes, [(i, (i + amount) % count) for i in range(count)])]
    ppermute x1, waiting for transfers between devices: 0.01 us -> 17.1 us  [on_device(): up_taken = lax.ppermute(after(up_given, gate_taken, over_z), 'yh', swap_y)]
    ppermute x1, waiting for transfers between devices: 0.01 us -> 16.4 us  [on_device(): down_taken = lax.ppermute(after(down_given, up_taken), 'yh', swap_y)]
    unnamed x52 -> x26, local copies, waits for them, and re-layouts: 17.3 us -> 4.77 us
    ppermute x1, waiting for transfers between devices: 8.27 us -> 1.12 us  [on_device(): gate_taken = lax.ppermute(after(gate_given, *step_rows), 'yh', swap_y)]
    pallas_call x2 -> x1, Pallas kernels: 20.2 us -> 16.9 us  [run_layer(): pl.pallas_call(layer_kernel, out_shape=[jax.ShapeDtypeStruct((8, 4, 2 * G...]
  transfers between devices with their start and end apart: 37 -> 37, of which waited for: 19 -> 19; matrix products, arithmetic and copies ran while one was open for 2% -> 1% of each run, Pallas kernels for 7% -> 59%
where the time goes in v1:
time: 428 us
  Pallas kernels  272 us (64%)
  waiting for transfers between devices  67.8 us (16%)
  starting transfers between devices  59.6 us (14%)
  between operations  16.1 us (4%)
  local copies, waits for them, and re-layouts  7.65 us (2%)
  other arithmetic  4.44 us (1%)
    pallas_call x1, Pallas kernels, run_swapped(): pl.pallas_call(swapped_kernel, out_shape=[jax.ShapeDtypeStruct(p.shape, p...  169 us
    pallas_call x1, Pallas kernels, run_handed(): pl.pallas_call(handed_kernel, out_shape=[jax.ShapeDtypeStruct(p.shape[1:]...  85.3 us
    ppermute x28, starting transfers between devices, send(): lax.ppermute(value, axes, [(i, (i + amount) % count) for i in range(count)])  52.8 us
    ppermute x28, waiting for transfers between devices, send(): lax.ppermute(value, axes, [(i, (i + amount) % count) for i in range(count)])  33.1 us
    ppermute x1, waiting for transfers between devices, on_device(): up_taken = lax.ppermute(after(up_given, gate_taken, over_z), 'yh', swap_y)  17.1 us
    pallas_call x1, Pallas kernels, run_layer(): pl.pallas_call(layer_kernel, out_shape=[jax.ShapeDtypeStruct((8, 4, 2 * G...  16.9 us
    ppermute x1, waiting for transfers between devices, on_device(): down_taken = lax.ppermute(after(down_given, up_taken), 'yh', swap_y)  16.4 us
  transfers between devices with their start and end apart: 37, of which 19 were waited for; matrix products, arithmetic and copies ran while one was open for 1% of the time, Pallas kernels for 59%

profile of v1, /device:TPU:24, one launch (start us, length us, event | category | flops | bytes accessed | tf_op | source)
XLA Modules:
  0.0 427.7 jit_solution(16318020809164788747)
XLA Ops:
  7.2 0.8 copy.21.routes_ref
  8.0 0.8 copy.22.gate_ref
  8.8 1.2 dynamic_slice.4
  12.3 2.0 collective-permute-start
  14.2 0.9 collective-permute-start.1
  15.2 1.0 collective-permute-done.refs_1_
  16.2 3.5 collective-permute-done.1.refs_2_
  20.8 1.6 collective-permute-start.13
  22.4 2.7 collective-permute-start.14
  25.1 1.4 collective-permute-start.15
  26.5 1.6 collective-permute-done.14
  28.1 1.2 collective-permute-done.15
  29.4 0.8 pad_maximum_fusion
  30.9 85.3 %handed.1 = (bf16[8,448,128]{2,1,0:T(8,128)(2,1)}, bf16[8,448,128]{2,1,0:T(8,128)(2,1)}, bf16[128,3584]{1,0:T(8,128)(2,1)}) custom-call(s32[5]{0:T(128)} %copy-done.3, bf16[2,16,512]{2,1,0:T(8,128)(2,1)} %copy-done.1, bf16[2,8,448,128]{3,2,1,0:T(8,128)(2,1)} %bitcast.72, bf16[2,8,448,128]{3,2,1,0:T(8,128)(2,1)} %bitcast.76, bf16[2,128,3584]{2,1,0:T(8,128)(2,1)} %refs_2_.3), custom_call_target="tpu_custom_call" | custom-call | bytes 6291456 | tf_op jit(solution)/shard_map/handed/pallas_call | solution.py:135
  116.6 2.0 collective-permute-start.7
  118.6 4.0 collective-permute-start.10
  122.6 2.3 collective-permute-done.7
  125.0 3.4 collective-permute-start.11
  128.4 4.0 collective-permute-start.9
  132.4 4.3 %collective-permute-done.9 = bf16[32,1024]{1,0:T(8,128)(2,1)S(1)} collective-permute-done((bf16[32,1024]{1,0:T(8,128)(2,1)S(1)}, bf16[32,1024]{1,0:T(8,128)(2,1)S(1)}, u32[]{:S(2)}, u32[]{:S(2)}) %collective-permute-start.9) | collective-permute-done | bytes 65568 | tf_op jit(solution)/shard_map/ppermute | solution.py:29
  136.7 2.8 collective-permute-done.8.refs_2_
  139.6 1.1 collective-permute-done.3.refs_3_
  140.7 2.3 collective-permute-start.12
  143.5 3.5 collective-permute-start.17
  147.2 17.1 %collective-permute-done.12.refs_4_ = bf16[8,448,128]{2,1,0:T(8,128)(2,1)S(1)} collective-permute-done((bf16[8,448,128]{2,1,0:T(8,128)(2,1)}, bf16[8,448,128]{2,1,0:T(8,128)(2,1)S(1)}, u32[]{:S(2)}, u32[]{:S(2)}) %collective-permute-start.12) | collective-permute-done | bytes 917536 | tf_op jit(solution)/shard_map/ppermute | solution.py:286
  164.3 3.2 collective-permute-done.17.refs_3_
  167.5 0.8 copy-done.10
  169.0 16.9 %layer.1 = (bf16[8,4,32,896]{3,2,1,0:T(8,128)(2,1)}, bf16[8,32,896]{2,1,0:T(8,128)(2,1)S(1)}, bf16[8,32,896]{2,1,0:T(8,128)(2,1)S(1)}, bf16[8,32,896]{2,1,0:T(8,...) custom-call(s32[5]{0:T(128)S(1)} %copy-done.4, s32[1,64]{1,0:T(1,128)S(1)} %bitcast.70, ...), custom_call_target="tpu_custom_call" | custom-call | flops 5637144576 | bytes 20971520 | tf_op jit(solution)/shard_map/layer/pallas_call | solution.py:240
  185.9 3.3 collective-permute-start.19
  189.3 1.7 collective-permute-start.23
  192.0 16.4 %collective-permute-done.19.refs_5_ = bf16[128,3584]{1,0:T(8,128)(2,1)S(1)} collective-permute-done((bf16[128,3584]{1,0:T(8,128)(2,1)}, bf16[128,3584]{1,0:T(8,128)(2,1)S(1)}, u32[]{:S(2)}, u32[]{:S(2)}) %collective-permute-start.19) | collective-permute-done | bytes 917536 | tf_op jit(solution)/shard_map/ppermute | solution.py:287
  208.4 1.0 copy-done.8
  209.4 168.6 %swapped.1 = (bf16[2,8,448,128]{3,2,1,0:T(8,128)(2,1)}, bf16[2,8,448,128]{3,2,1,0:T(8,128)(2,1)}, bf16[2,128,3584]{2,1,0:T(8,128)(2,1)}) custom-call(s32[5]{0:T(128)} %copy-done.3, bf16[2,8,448,128]{3,2,1,0:T(8,128)(2,1)} %bitcast.74, bf16[2,8,448,128]{3,2,1,0:T(8,128)(2,1)} %bitcast.78, bf16[2,128,3584]{2,1,0:T(8,128)(2,1)} %refs_2_.3, ...), custom_call_target="tpu_custom_call" | custom-call | bytes 11534336 | tf_op jit(solution)/shard_map/swapped/pallas_call | solution.py:162
  378.0 1.3 add_convert_fusion
  379.3 6.6 %collective-permute-start.26 = (bf16[2,32,896]{2,1,0:T(8,128)(2,1)S(1)}, bf16[2,32,896]{2,1,0:T(8,128)(2,1)S(1)}, u32[]{:S(2)}, u32[]{:S(2)}) collective-permute-start(bf16[2,32,896]{2,1,0:T(8,128)(2,1)S(1)} %get-tuple-element.52), channel_id=1, source_target_pairs={{0,96},{16,112},{32,0},{48,16},{64,32},{80,48},{96,64},{112,80},{1... | collective-permute-start | bytes 344072 | tf_op jit(solution)/shard_map/ppermute | solution.py:29
  385.9 3.8 collective-permute-start.28
  389.8 1.2 collective-permute-done.26
  391.0 3.1 collective-permute-done.27
  394.2 2.0 collective-permute-start.30
  396.2 0.9 slice_bitcast_fusion.3
  397.1 5.4 %collective-permute-start.20 = (bf16[32,896]{1,0:T(8,128)(2,1)S(1)}, bf16[32,896]{1,0:T(8,128)(2,1)S(1)}, u32[]{:S(2)}, u32[]{:S(2)}) collective-permute-start(bf16[32,896]{1,0:T(8,128)(2,1)S(1)} %get-tuple-element.54), channel_id=1, source_target_pairs={{0,6},{2,0},{4,2},{6,4},{1,7},{3,1},{5,3},{7,5},{8,14},{10,8},{12,... | collective-permute-start | bytes 172040 | tf_op jit(solution)/shard_map/ppermute | solution.py:29
  403.5 0.8 collective-permute-done.20
  404.3 3.9 collective-permute-done.21
  408.8 0.9 fusion.2
  409.8 3.0 collective-permute-start.32
  412.7 1.2 collective-permute-start.33
  413.9 0.8 collective-permute-start.31
  416.7 2.4 collective-permute-done.31
  (78 shorter events, 10.9 us)
Async XLA Ops:
  7.2 161.1 %all-gather.3.cloned.1.call-start = ((), (), s32[]{:S(2)}) async-start(), calls=%async_computation.2 | async-start | bytes 2359296 | tf_op jit(solution)/shard_map/all_gather | solution.py:284
  10.7 0.8 copy-start.2
  11.5 19.4 %copy-start.3 = (s32[5]{0:T(128)}, s32[5]{0:T(128)S(1)}, u32[]{:S(2)}) copy-start(s32[5]{0:T(128)S(1)} %stack.56.place) | copy-start | bytes 64
  12.3 18.7 %copy-start.1 = (bf16[2,16,512]{2,1,0:T(8,128)(2,1)}, bf16[2,16,512]{2,1,0:T(8,128)(2,1)S(1)}, u32[]{:S(2)}) copy-start(bf16[2,16,512]{2,1,0:T(8,128)(2,1)S(1)} %ride.1.lower_ref.refs_0_) | copy-start | bytes 98308
  12.3 3.9 collective-permute-start
  14.2 5.4 %collective-permute-start.1 = (bf16[2,16,512]{2,1,0:T(8,128)(2,1)S(1)}, bf16[2,16,512]{2,1,0:T(8,128)(2,1)S(1)}, u32[]{:S(2)}, u32[]{:S(2)}) collective-permute-start(bf16[2,16,512]{2,1,0:T(8,128)(2,1)S(1)} %ride.1.lower_ref.refs_0_), channel_id=1, source_target_pairs={{0,128},{1,129},{128,0},{129,1},{2,130},{3,131},{130,2},{131,3},{4... | collective-permute-start | bytes 98312 | tf_op jit(solution)/shard_map/ppermute | solution.py:29
  15.1 5.1 %collective-permute-start.2 = (bf16[2,16,512]{2,1,0:T(8,128)(2,1)S(1)}, bf16[2,16,512]{2,1,0:T(8,128)(2,1)S(1)}, u32[]{:S(2)}, u32[]{:S(2)}) collective-permute-start(bf16[2,16,512]{2,1,0:T(8,128)(2,1)S(1)} %ride.1.lower_ref.refs_0_), channel_id=1, source_target_pairs={{0,129},{1,0},{128,1},{129,128},{2,131},{3,2},{130,3},{131,130},{4... | collective-permute-start | bytes 98312 | tf_op jit(solution)/shard_map/ppermute | solution.py:29
  20.8 5.7 %collective-permute-start.13 = (bf16[32,1024]{1,0:T(8,128)(2,1)S(1)}, bf16[32,1024]{1,0:T(8,128)(2,1)S(1)}, u32[]{:S(2)}, u32[]{:S(2)}) collective-permute-start(bf16[32,1024]{1,0:T(8,128)(2,1)S(1)} %get-tuple-element.27), channel_id=1, source_target_pairs={{0,2},{2,4},{4,6},{6,0},{1,3},{3,5},{5,7},{7,1},{8,10},{10,12},{12... | collective-permute-start | bytes 196616 | tf_op jit(solution)/shard_map/ppermute | solution.py:29
  22.4 5.8 %collective-permute-start.14 = (bf16[32,1024]{1,0:T(8,128)(2,1)S(1)}, bf16[32,1024]{1,0:T(8,128)(2,1)S(1)}, u32[]{:S(2)}, u32[]{:S(2)}) collective-permute-start(bf16[32,1024]{1,0:T(8,128)(2,1)S(1)} %get-tuple-element.27), channel_id=1, source_target_pairs={{0,4},{2,6},{4,0},{6,2},{1,5},{3,7},{5,1},{7,3},{8,12},{10,14},{12... | collective-permute-start | bytes 196616 | tf_op jit(solution)/shard_map/ppermute | solution.py:29
  25.1 4.3 collective-permute-start.15
  30.1 366.0 %reduce-scatter.2.cloned.1.call-start = ((), (), s32[]{:S(2)}) async-start(), calls=%async_computation.1 | async-start | bytes 2064384 | tf_op jit(solution)/shard_map/reduce_scatter | solution.py:292
  30.2 86.4 %collective-permute-start.4 = (bf16[2,8,448,128]{3,2,1,0:T(8,128)(2,1)}, bf16[2,8,448,128]{3,2,1,0:T(8,128)(2,1)}, u32[]{:S(2)}, u32[]{:S(2)}) collective-permute-start(bf16[2,8,448,128]{3,2,1,0:T(8,128)(2,1)} %bitcast.71), channel_id=1, source_target_pairs={{0,8},{8,0},{1,9},{9,1},{2,10},{10,2},{3,11},{11,3},{4,12},{12,4},... | collective-permute-start | bytes 5505032 | tf_op jit(solution)/shard_map/ppermute | solution.py:280
  30.3 138.0 %copy-start.5 = (s32[64]{0:T(128)S(1)}, s32[64]{0:T(128)}, u32[]{:S(2)}) copy-start(s32[64]{0:T(128)} %param.11) | copy-start | bytes 772
  30.3 86.3 %collective-permute-start.5 = (bf16[2,8,448,128]{3,2,1,0:T(8,128)(2,1)}, bf16[2,8,448,128]{3,2,1,0:T(8,128)(2,1)}, u32[]{:S(2)}, u32[]{:S(2)}) collective-permute-start(bf16[2,8,448,128]{3,2,1,0:T(8,128)(2,1)} %bitcast.75), channel_id=1, source_target_pairs={{0,8},{8,0},{1,9},{9,1},{2,10},{10,2},{3,11},{11,3},{4,12},{12,4},... | collective-permute-start | bytes 5505032 | tf_op jit(solution)/shard_map/ppermute | solution.py:280
  30.8 85.8 %collective-permute-start.6 = (bf16[2,128,3584]{2,1,0:T(8,128)(2,1)}, bf16[2,128,3584]{2,1,0:T(8,128)(2,1)}, u32[]{:S(2)}, u32[]{:S(2)}) collective-permute-start(bf16[2,128,3584]{2,1,0:T(8,128)(2,1)} %refs_2_.3), channel_id=1, source_target_pairs={{0,8},{8,0},{1,9},{9,1},{2,10},{10,2},{3,11},{11,3},{4,12},{12,4},... | collective-permute-start | bytes 5505032 | tf_op jit(solution)/shard_map/ppermute | solution.py:280
  116.2 24.5 %collective-permute-start.3 = (bf16[8,448,128]{2,1,0:T(8,128)(2,1)}, bf16[8,448,128]{2,1,0:T(8,128)(2,1)S(1)}, u32[]{:S(2)}, u32[]{:S(2)}) collective-permute-start(bf16[8,448,128]{2,1,0:T(8,128)(2,1)} %get-tuple-element.29), channel_id=1, source_target_pairs={{0,128},{128,0},{1,129},{129,1},{2,130},{130,2},{3,131},{131,3},{4... | collective-permute-start | bytes 2752520 | tf_op jit(solution)/shard_map/ppermute | solution.py:283
  116.6 8.3 %collective-permute-start.7 = (bf16[32,1024]{1,0:T(8,128)(2,1)S(1)}, bf16[32,1024]{1,0:T(8,128)(2,1)S(1)}, u32[]{:S(2)}, u32[]{:S(2)}) collective-permute-start(bf16[32,1024]{1,0:T(8,128)(2,1)S(1)} %get-tuple-element.30), channel_id=1, source_target_pairs={{0,16},{16,32},{32,48},{48,64},{64,80},{80,96},{96,112},{112,0},{1... | collective-permute-start | bytes 196616 | tf_op jit(solution)/shard_map/ppermute | solution.py:29
  118.6 6.3 %collective-permute-start.10 = (bf16[32,1024]{1,0:T(8,128)(2,1)S(1)}, bf16[32,1024]{1,0:T(8,128)(2,1)S(1)}, u32[]{:S(2)}, u32[]{:S(2)}) collective-permute-start(bf16[32,1024]{1,0:T(8,128)(2,1)S(1)} %get-tuple-element.30), channel_id=1, source_target_pairs={{0,112},{16,0},{32,16},{48,32},{64,48},{80,64},{96,80},{112,96},{1... | collective-permute-start | bytes 196616 | tf_op jit(solution)/shard_map/ppermute | solution.py:29
  125.0 11.8 %collective-permute-start.11 = (bf16[2,32,1024]{2,1,0:T(8,128)(2,1)S(1)}, bf16[2,32,1024]{2,1,0:T(8,128)(2,1)S(1)}, u32[]{:S(2)}, u32[]{:S(2)}) collective-permute-start(bf16[2,32,1024]{2,1,0:T(8,128)(2,1)S(1)} %get-tuple-element.59), channel_id=1, source_target_pairs={{0,96},{16,112},{32,0},{48,16},{64,32},{80,48},{96,64},{112,80},{1... | collective-permute-start | bytes 393224 | tf_op jit(solution)/shard_map/ppermute | solution.py:29
  128.4 11.2 %collective-permute-start.8 = (bf16[2,32,1024]{2,1,0:T(8,128)(2,1)S(1)}, bf16[2,32,1024]{2,1,0:T(8,128)(2,1)S(1)}, u32[]{:S(2)}, u32[]{:S(2)}) collective-permute-start(bf16[2,32,1024]{2,1,0:T(8,128)(2,1)S(1)} %get-tuple-element.60), channel_id=1, source_target_pairs={{0,32},{16,48},{32,64},{48,80},{64,96},{80,112},{96,0},{112,16},{1... | collective-permute-start | bytes 393224 | tf_op jit(solution)/shard_map/ppermute | solution.py:29
  128.4 8.4 %collective-permute-start.9 = (bf16[32,1024]{1,0:T(8,128)(2,1)S(1)}, bf16[32,1024]{1,0:T(8,128)(2,1)S(1)}, u32[]{:S(2)}, u32[]{:S(2)}) collective-permute-start(bf16[32,1024]{1,0:T(8,128)(2,1)S(1)} %get-tuple-element.30), channel_id=1, source_target_pairs={{0,64},{16,80},{32,96},{48,112},{64,0},{80,16},{96,32},{112,48},{1... | collective-permute-start | bytes 196616 | tf_op jit(solution)/shard_map/ppermute | solution.py:29
  139.6 28.7 %copy-start = (bf16[8,32,1024]{2,1,0:T(8,128)(2,1)}, bf16[8,32,1024]{2,1,0:T(8,128)(2,1)S(1)}, u32[]{:S(2)}) copy-start(bf16[8,32,1024]{2,1,0:T(8,128)(2,1)S(1)} %join.1.refs_1_) | copy-start | bytes 1572868
  140.7 45.2 %copy-start.6 = (bf16[8,448,128]{2,1,0:T(8,128)(2,1)}, bf16[8,448,128]{2,1,0:T(8,128)(2,1)S(1)}, u32[]{:S(2)}) copy-start(bf16[8,448,128]{2,1,0:T(8,128)(2,1)S(1)} %collective-permute-done.3.refs_3_) | copy-start | bytes 2752516
  140.7 23.6 %collective-permute-start.12 = (bf16[8,448,128]{2,1,0:T(8,128)(2,1)}, bf16[8,448,128]{2,1,0:T(8,128)(2,1)S(1)}, u32[]{:S(2)}, u32[]{:S(2)}) collective-permute-start(bf16[8,448,128]{2,1,0:T(8,128)(2,1)} %get-tuple-element.31), channel_id=1, source_target_pairs={{0,128},{128,0},{1,129},{129,1},{2,130},{130,2},{3,131},{131,3},{4... | collective-permute-start | bytes 2752520 | tf_op jit(solution)/shard_map/ppermute | solution.py:286
  143.0 21.3 %collective-permute-start.16 = (bf16[8,32,1024]{2,1,0:T(8,128)(2,1)S(1)}, bf16[8,32,1024]{2,1,0:T(8,128)(2,1)S(1)}, u32[]{:S(2)}, u32[]{:S(2)}) collective-permute-start(bf16[8,32,1024]{2,1,0:T(8,128)(2,1)S(1)} %join.1.refs_1_), channel_id=1, source_target_pairs={{0,2},{2,4},{4,6},{6,0},{1,3},{3,5},{5,7},{7,1},{8,10},{10,12},{12... | collective-permute-start | bytes 1572872 | tf_op jit(solution)/shard_map/ppermute | solution.py:29
  143.5 23.9 %collective-permute-start.17 = (bf16[8,32,1024]{2,1,0:T(8,128)(2,1)S(1)}, bf16[8,32,1024]{2,1,0:T(8,128)(2,1)S(1)}, u32[]{:S(2)}, u32[]{:S(2)}) collective-permute-start(bf16[8,32,1024]{2,1,0:T(8,128)(2,1)S(1)} %join.1.refs_1_), channel_id=1, source_target_pairs={{0,4},{2,6},{4,0},{6,2},{1,5},{3,7},{5,1},{7,3},{8,12},{10,14},{12... | collective-permute-start | bytes 1572872 | tf_op jit(solution)/shard_map/ppermute | solution.py:29
  147.1 21.2 %collective-permute-start.18 = (bf16[8,32,1024]{2,1,0:T(8,128)(2,1)S(1)}, bf16[8,32,1024]{2,1,0:T(8,128)(2,1)}, u32[]{:S(2)}, u32[]{:S(2)}) collective-permute-start(bf16[8,32,1024]{2,1,0:T(8,128)(2,1)S(1)} %join.1.refs_1_), channel_id=1, source_target_pairs={{0,6},{2,0},{4,2},{6,4},{1,7},{3,1},{5,3},{7,5},{8,14},{10,8},{12,... | collective-permute-start | bytes 1572872 | tf_op jit(solution)/shard_map/ppermute | solution.py:29
  164.3 4.0 copy-start.7
  164.3 4.0 copy-start.9
  167.5 0.8 copy-start.10
  185.9 5.9 %copy-start.11 = (s32[32]{0:T(128)S(1)}, s32[32]{0:T(128)}, u32[]{:S(2)}) copy-start(s32[32]{0:T(128)} %param.12) | copy-start | bytes 388
  185.9 22.5 %collective-permute-start.19 = (bf16[128,3584]{1,0:T(8,128)(2,1)}, bf16[128,3584]{1,0:T(8,128)(2,1)S(1)}, u32[]{:S(2)}, u32[]{:S(2)}) collective-permute-start(bf16[128,3584]{1,0:T(8,128)(2,1)} %get-tuple-element.35), channel_id=1, source_target_pairs={{0,128},{128,0},{1,129},{129,1},{2,130},{130,2},{3,131},{131,3},{4... | collective-permute-start | bytes 2752520 | tf_op jit(solution)/shard_map/ppermute | solution.py:287
  189.3 188.7 %collective-permute-start.23 = (bf16[8,32,896]{2,1,0:T(8,128)(2,1)S(1)}, bf16[8,32,896]{2,1,0:T(8,128)(2,1)S(1)}, u32[]{:S(2)}, u32[]{:S(2)}) collective-permute-start(bf16[8,32,896]{2,1,0:T(8,128)(2,1)S(1)} %get-tuple-element.41), channel_id=1, source_target_pairs={{0,6},{2,0},{4,2},{6,4},{1,7},{3,1},{5,3},{7,5},{8,14},{10,8},{12,... | collective-permute-start | bytes 1376264 | tf_op jit(solution)/shard_map/ppermute | solution.py:29
  191.0 187.0 %collective-permute-start.24 = (bf16[8,32,896]{2,1,0:T(8,128)(2,1)S(1)}, bf16[8,32,896]{2,1,0:T(8,128)(2,1)S(1)}, u32[]{:S(2)}, u32[]{:S(2)}) collective-permute-start(bf16[8,32,896]{2,1,0:T(8,128)(2,1)S(1)} %get-tuple-element.42), channel_id=1, source_target_pairs={{0,4},{2,6},{4,0},{6,2},{1,5},{3,7},{5,1},{7,3},{8,12},{10,14},{12... | collective-permute-start | bytes 1376264 | tf_op jit(solution)/shard_map/ppermute | solution.py:29
  191.3 186.7 %collective-permute-start.25 = (bf16[8,32,896]{2,1,0:T(8,128)(2,1)S(1)}, bf16[8,32,896]{2,1,0:T(8,128)(2,1)}, u32[]{:S(2)}, u32[]{:S(2)}) collective-permute-start(bf16[8,32,896]{2,1,0:T(8,128)(2,1)S(1)} %get-tuple-element.43), channel_id=1, source_target_pairs={{0,2},{2,4},{4,6},{6,0},{1,3},{3,5},{5,7},{7,1},{8,10},{10,12},{12... | collective-permute-start | bytes 1376264 | tf_op jit(solution)/shard_map/ppermute | solution.py:29
  191.9 222.8 %collective-permute-start.34 = (f32[64]{0:T(128)S(1)}, f32[64]{0:T(128)S(1)}, u32[]{:S(2)}, u32[]{:S(2)}) collective-permute-start(f32[64]{0:T(128)S(1)} %slice_bitcast_fusion.4), channel_id=1, source_target_pairs={{0,8},{8,0},{1,9},{9,1},{2,10},{10,2},{3,11},{11,3},{4,12},{12,4},... | collective-permute-start | bytes 776 | tf_op jit(solution)/shard_map/ppermute | solution.py:301
  208.4 1.0 copy-start.8
  379.3 11.6 %collective-permute-start.26 = (bf16[2,32,896]{2,1,0:T(8,128)(2,1)S(1)}, bf16[2,32,896]{2,1,0:T(8,128)(2,1)S(1)}, u32[]{:S(2)}, u32[]{:S(2)}) collective-permute-start(bf16[2,32,896]{2,1,0:T(8,128)(2,1)S(1)} %get-tuple-element.52), channel_id=1, source_target_pairs={{0,96},{16,112},{32,0},{48,16},{64,32},{80,48},{96,64},{112,80},{1... | collective-permute-start | bytes 344072 | tf_op jit(solution)/shard_map/ppermute | solution.py:29
  385.9 8.1 %collective-permute-start.27 = (bf16[2,32,896]{2,1,0:T(8,128)(2,1)S(1)}, bf16[2,32,896]{2,1,0:T(8,128)(2,1)S(1)}, u32[]{:S(2)}, u32[]{:S(2)}) collective-permute-start(bf16[2,32,896]{2,1,0:T(8,128)(2,1)S(1)} %get-tuple-element.53), channel_id=1, source_target_pairs={{0,32},{16,48},{32,64},{48,80},{64,96},{80,112},{96,0},{112,16},{1... | collective-permute-start | bytes 344072 | tf_op jit(solution)/shard_map/ppermute | solution.py:29
  385.9 16.5 %collective-permute-start.28 = (bf16[32,896]{1,0:T(8,128)(2,1)S(1)}, bf16[32,896]{1,0:T(8,128)(2,1)S(1)}, u32[]{:S(2)}, u32[]{:S(2)}) collective-permute-start(bf16[32,896]{1,0:T(8,128)(2,1)S(1)} %slice_bitcast_fusion), channel_id=1, source_target_pairs={{0,64},{16,80},{32,96},{48,112},{64,0},{80,16},{96,32},{112,48},{1... | collective-permute-start | bytes 172040 | tf_op jit(solution)/shard_map/ppermute | solution.py:29
  394.1 8.7 %collective-permute-start.29 = (bf16[32,896]{1,0:T(8,128)(2,1)S(1)}, bf16[32,896]{1,0:T(8,128)(2,1)S(1)}, u32[]{:S(2)}, u32[]{:S(2)}) collective-permute-start(bf16[32,896]{1,0:T(8,128)(2,1)S(1)} %get-tuple-element.50), channel_id=1, source_target_pairs={{0,112},{16,0},{32,16},{48,32},{64,48},{80,64},{96,80},{112,96},{1... | collective-permute-start | bytes 172040 | tf_op jit(solution)/shard_map/ppermute | solution.py:29
  394.2 9.3 %collective-permute-start.30 = (bf16[32,896]{1,0:T(8,128)(2,1)S(1)}, bf16[32,896]{1,0:T(8,128)(2,1)S(1)}, u32[]{:S(2)}, u32[]{:S(2)}) collective-permute-start(bf16[32,896]{1,0:T(8,128)(2,1)S(1)} %get-tuple-element.51), channel_id=1, source_target_pairs={{0,16},{16,32},{32,48},{48,64},{64,80},{80,96},{96,112},{112,0},{1... | collective-permute-start | bytes 172040 | tf_op jit(solution)/shard_map/ppermute | solution.py:29
  397.1 7.2 %collective-permute-start.20 = (bf16[32,896]{1,0:T(8,128)(2,1)S(1)}, bf16[32,896]{1,0:T(8,128)(2,1)S(1)}, u32[]{:S(2)}, u32[]{:S(2)}) collective-permute-start(bf16[32,896]{1,0:T(8,128)(2,1)S(1)} %get-tuple-element.54), channel_id=1, source_target_pairs={{0,6},{2,0},{4,2},{6,4},{1,7},{3,1},{5,3},{7,5},{8,14},{10,8},{12,... | collective-permute-start | bytes 172040 | tf_op jit(solution)/shard_map/ppermute | solution.py:29
  402.5 5.7 %collective-permute-start.21 = (bf16[32,896]{1,0:T(8,128)(2,1)S(1)}, bf16[32,896]{1,0:T(8,128)(2,1)S(1)}, u32[]{:S(2)}, u32[]{:S(2)}) collective-permute-start(bf16[32,896]{1,0:T(8,128)(2,1)S(1)} %get-tuple-element.56), channel_id=1, source_target_pairs={{0,4},{2,6},{4,0},{6,2},{1,5},{3,7},{5,1},{7,3},{8,12},{10,14},{12... | collective-permute-start | bytes 172040 | tf_op jit(solution)/shard_map/ppermute | solution.py:29
  402.8 6.0 %collective-permute-start.22 = (bf16[32,896]{1,0:T(8,128)(2,1)S(1)}, bf16[32,896]{1,0:T(8,128)(2,1)S(1)}, u32[]{:S(2)}, u32[]{:S(2)}) collective-permute-start(bf16[32,896]{1,0:T(8,128)(2,1)S(1)} %get-tuple-element.55), channel_id=1, source_target_pairs={{0,2},{2,4},{4,6},{6,0},{1,3},{3,5},{5,7},{7,1},{8,10},{10,12},{12... | collective-permute-start | bytes 172040 | tf_op jit(solution)/shard_map/ppermute | solution.py:29
  409.8 6.3 %collective-permute-start.32 = (bf16[2,16,448]{2,1,0:T(8,128)(2,1)S(1)}, bf16[2,16,448]{2,1,0:T(8,128)(2,1)S(1)}, u32[]{:S(2)}, u32[]{:S(2)}) collective-permute-start(bf16[2,16,448]{2,1,0:T(8,128)(2,1)S(1)} %get-tuple-element.57), channel_id=1, source_target_pairs={{0,128},{1,129},{128,0},{129,1},{2,130},{3,131},{130,2},{131,3},{4... | collective-permute-start | bytes 86024 | tf_op jit(solution)/shard_map/ppermute | solution.py:29
  412.7 3.9 collective-permute-start.33
  413.9 5.1 %collective-permute-start.31 = (bf16[2,16,448]{2,1,0:T(8,128)(2,1)S(1)}, bf16[2,16,448]{2,1,0:T(8,128)(2,1)S(1)}, u32[]{:S(2)}, u32[]{:S(2)}) collective-permute-start(bf16[2,16,448]{2,1,0:T(8,128)(2,1)S(1)} %get-tuple-element.45), channel_id=1, source_target_pairs={{0,129},{1,0},{128,1},{129,128},{2,131},{3,2},{130,3},{131,130},{4... | collective-permute-start | bytes 86024 | tf_op jit(solution)/shard_map/ppermute | solution.py:29
  (1 other events, 0.7 us)
Sparse Core Ops, SparseCore 0:
  30.3 94.0 all-gather.2
  186.1 43.1 reduce-scatter.1

commit v2 on v1

--- a/solution.py
+++ b/solution.py
@@ -123,10 +123,14 @@
 
 
 def handed_kernel(place, lower_ref, *refs):
-    copies = [pltpu.make_async_copy(refs[k].at[place[4]], refs[3 + k], refs[6].at[k]) for k in range(3)]
-    for copy in copies:
+    ins = [pltpu.make_async_copy(refs[k].at[place[4]], refs[6 + k], refs[9].at[k]) for k in range(3)]
+    outs = [pltpu.make_async_copy(refs[6 + k], refs[3 + k], refs[9].at[3 + k]) for k in range(3)]
+    for copy in ins:
         copy.start()
-    for copy in copies:
+    for copy_in, copy_out in zip(ins, outs):
+        copy_in.wait()
+        copy_out.start()
+    for copy in outs:
         copy.wait()
 
 
@@ -137,7 +141,7 @@
         out_shape=[jax.ShapeDtypeStruct(p.shape[1:], p.dtype) for p in panels],
         in_specs=[pl.BlockSpec(memory_space=pltpu.SMEM), pl.BlockSpec(memory_space=pltpu.VMEM)] + [hbm] * 3,
         out_specs=[hbm] * 3,
-        scratch_shapes=[pltpu.SemaphoreType.DMA((3,))],
+        scratch_shapes=[pltpu.VMEM(p.shape[1:], p.dtype) for p in panels] + [pltpu.SemaphoreType.DMA((6,))],
         compiler_params=LARGE,
         cost_estimate=pl.CostEstimate(flops=0, bytes_accessed=6 * 2**20, transcendentals=0),
         name="handed",
@@ -146,14 +150,18 @@
 
 def swapped_kernel(place, *refs):
     slot = place[4]
-    copies = []
+    ins, outs = [], []
     for k in range(3):
-        panel, taken, out = refs[k], refs[3 + k], refs[6 + k]
-        copies.append(pltpu.make_async_copy(panel.at[1 - slot], out.at[1 - slot], refs[9].at[2 * k]))
-        copies.append(pltpu.make_async_copy(taken, out.at[slot], refs[9].at[2 * k + 1]))
-    for copy in copies:
+        panel, taken, out, room = refs[k], refs[3 + k], refs[6 + k], refs[9 + k]
+        for j, source, at in ((0, panel.at[1 - slot], 1 - slot), (1, taken, slot)):
+            ins.append(pltpu.make_async_copy(source, room.at[j], refs[12].at[2 * k + j]))
+            outs.append(pltpu.make_async_copy(room.at[j], out.at[at], refs[12].at[6 + 2 * k + j]))
+    for copy in ins:
         copy.start()
-    for copy in copies:
+    for copy_in, copy_out in zip(ins, outs):
+        copy_in.wait()
+        copy_out.start()
+    for copy in outs:
         copy.wait()
 
 
@@ -164,7 +172,7 @@
         out_shape=[jax.ShapeDtypeStruct(p.shape, p.dtype) for p in panels],
         in_specs=[pl.BlockSpec(memory_space=pltpu.SMEM)] + [hbm] * 6,
         out_specs=[hbm] * 3,
-        scratch_shapes=[pltpu.SemaphoreType.DMA((6,))],
+        scratch_shapes=[pltpu.VMEM(p.shape, p.dtype) for p in panels] + [pltpu.SemaphoreType.DMA((12,))],
         compiler_params=LARGE,
         cost_estimate=pl.CostEstimate(flops=0, bytes_accessed=11 * 2**20, transcendentals=0),
         name="swapped",
@@ -175,7 +183,7 @@
     piece0, pieces1 = refs[0], refs[1:5]
     gate_own, up_own, down_own, gate_other, up_other, down_other = refs[5:11]
     out0, outs1, count_ref = refs[11], refs[12:16], refs[16]
-    rows_ref, panel_ref, down_ref, result_ref, sems = refs[17:]
+    rows_ref, panel_ref, down_ref, hidden_ref, result_ref, sems = refs[17:]
     my_x, my_core, chip = place[0], place[1], place[2]
     span = 2 * GROUP
 
@@ -210,23 +218,28 @@
         jnp.sum((gates[8 * span :] > 0.0).astype(jnp.float32), axis=0, keepdims=True), count_ref.shape
     )
     positions = position_ref[...]
-    hidden = []
     for q in range(4):
         stored = chip * 4 + (my_core if q < 2 else 1 - my_core) * 2 + q % 2
         share = jnp.sum(jnp.where(positions == stored, gates, 0.0), axis=1, keepdims=True) * (1.0 / 65536.0)
         for copy in copies[q]:
             copy.wait()
-        act = jnp.dot(
-            rows_ref[...], panel_ref[q].reshape(8 * LANES, 256), preferred_element_type=jnp.float32
-        )
-        hidden.append((jax.nn.silu(act[:, :128]) * act[:, 128:] * share).astype(jnp.bfloat16))
-    hidden = jnp.concatenate(hidden, axis=1)
+        for step in range(2):
+            at = slice(step * 256, (step + 1) * 256)
+            act = jnp.zeros((256, 256), jnp.float32)
+            for block in range(8):
+                act = act + jnp.dot(
+                    rows_ref[at, block * LANES : (block + 1) * LANES],
+                    panel_ref[q, block],
+                    preferred_element_type=jnp.float32,
+                )
+            value = jax.nn.silu(act[:, :128]) * act[:, 128:] * share[at]
+            hidden_ref[at, q * 128 : (q + 1) * 128] = value.astype(jnp.bfloat16)
     for group in copies[4:]:
         for copy in group:
             copy.wait()
     for x_at in range(4):
         panel = down_ref[:, :, x_at * PAIR : (x_at + 1) * PAIR].reshape(4 * 128, PAIR)
-        result_ref[x_at] = jnp.dot(hidden, panel, preferred_element_type=jnp.float32).astype(jnp.bfloat16)
+        result_ref[x_at] = jnp.dot(hidden_ref[...], panel, preferred_element_type=jnp.float32).astype(jnp.bfloat16)
 
     for xr in range(4):
         x_at = lax.rem(my_x - xr + 4, 4)
@@ -250,6 +263,7 @@
             pltpu.VMEM((512, 8 * LANES), jnp.bfloat16),
             pltpu.VMEM((4, 8, LANES, 256), jnp.bfloat16),
             pltpu.VMEM((4, 128, 3584), jnp.bfloat16),
+            pltpu.VMEM((512, 512), jnp.bfloat16),
             pltpu.VMEM((4, 512, PAIR), jnp.bfloat16),
             pltpu.SemaphoreType.DMA((10,)),
         ],

time: 428 us -> 184 us (0.43)
  Pallas kernels: 272 us -> 23.1 us
  waiting for transfers between devices: 67.8 us -> 77.8 us
  starting transfers between devices: 59.6 us -> 53.9 us
    pallas_call x1, Pallas kernels: 169 us -> 5.55 us  [run_swapped(): pl.pallas_call(swapped_kernel, out_shape=[jax.ShapeDtypeStruct(p.shape, p...]
    pallas_call x1, Pallas kernels: 85.3 us -> 3.53 us  [run_handed(): pl.pallas_call(handed_kernel, out_shape=[jax.ShapeDtypeStruct(p.shape[1:]...]
    ppermute x28, waiting for transfers between devices: 33.1 us -> 40.8 us  [send(): lax.ppermute(value, axes, [(i, (i + amount) % count) for i in range(count)])]
    ppermute x3, waiting for transfers between devices: 0.01 us -> 4.82 us  [on_device(): other = tuple((lax.ppermute(w, 'core', swap_core) for w in panels))]
  transfers between devices with their start and end apart: 37 -> 37, of which waited for: 19 -> 20; matrix products, arithmetic and copies ran while one was open for 1% -> 2% of each run, Pallas kernels for 59% -> 5%
where the time goes in v2:
time: 184 us; the launch traced here: 183 us
  waiting for transfers between devices  77.8 us (42%)
  starting transfers between devices  53.9 us (29%)
  Pallas kernels  23.1 us (13%)
  between operations  16.1 us (9%)
  local copies, waits for them, and re-layouts  7.65 us (4%)
  other arithmetic  4.45 us (2%)
    ppermute x28, starting transfers between devices, send(): lax.ppermute(value, axes, [(i, (i + amount) % count) for i in range(count)])  49.1 us
    ppermute x28, waiting for transfers between devices, send(): lax.ppermute(value, axes, [(i, (i + amount) % count) for i in range(count)])  40.8 us
    ppermute x1, waiting for transfers between devices, on_device(): down_taken = lax.ppermute(after(down_given, up_taken), 'yh', swap_y)  16.2 us
    ppermute x1, waiting for transfers between devices, on_device(): up_taken = lax.ppermute(after(up_given, gate_taken, over_z), 'yh', swap_y)  15.9 us
    pallas_call x1, Pallas kernels, run_layer(): pl.pallas_call(layer_kernel, out_shape=[jax.ShapeDtypeStruct((8, 4, 2 * G...  12.7 us
    pallas_call x1, Pallas kernels, run_swapped(): pl.pallas_call(swapped_kernel, out_shape=[jax.ShapeDtypeStruct(p.shape, p...  5.55 us
    ppermute x3, waiting for transfers between devices, on_device(): other = tuple((lax.ppermute(w, 'core', swap_core) for w in panels))  4.82 us
    unnamed x26, local copies, waits for them, and re-layouts  4.77 us
  transfers between devices with their start and end apart: 37, of which 20 were waited for; matrix products, arithmetic and copies ran while one was open for 2% of the time, Pallas kernels for 5%

profile of v2, /device:TPU:24, one launch (start us, length us, event | category | flops | bytes accessed | tf_op | source)
XLA Modules:
  0.0 183.0 jit_solution(17345343423234727806)
XLA Ops:
  8.0 0.8 copy.22.gate_ref
  8.8 1.2 dynamic_slice.4
  12.3 2.0 %collective-permute-start = (bf16[2,16,512]{2,1,0:T(8,128)(2,1)S(1)}, bf16[2,16,512]{2,1,0:T(8,128)(2,1)S(1)}, u32[]{:S(2)}, u32[]{:S(2)}) collective-permute-start(bf16[2,16,512]{2,1,0:T(8,128)(2,1)S(1)} %ride.1.lower_ref.refs_0_), channel_id=1, source_target_pairs={{0,1},{1,128},{128,129},{129,0},{2,3},{3,130},{130,131},{131,2},{4... | collective-permute-start | bytes 98312 | tf_op jit(solution)/shard_map/ppermute | solution.py:29
  14.2 0.9 collective-permute-start.1
  15.2 1.0 collective-permute-done.refs_1_
  16.2 3.5 %collective-permute-done.1.refs_2_ = bf16[2,16,512]{2,1,0:T(8,128)(2,1)S(1)} collective-permute-done((bf16[2,16,512]{2,1,0:T(8,128)(2,1)S(1)}, bf16[2,16,512]{2,1,0:T(8,128)(2,1)S(1)}, u32[]{:S(2)}, u32[]{:S(2)}) %collective-permute-start.1) | collective-permute-done | bytes 32800 | tf_op jit(solution)/shard_map/ppermute | solution.py:29
  20.8 1.6 collective-permute-start.13
  22.4 2.7 %collective-permute-start.14 = (bf16[32,1024]{1,0:T(8,128)(2,1)S(1)}, bf16[32,1024]{1,0:T(8,128)(2,1)S(1)}, u32[]{:S(2)}, u32[]{:S(2)}) collective-permute-start(bf16[32,1024]{1,0:T(8,128)(2,1)S(1)} %get-tuple-element.27), channel_id=1, source_target_pairs={{0,4},{2,6},{4,0},{6,2},{1,5},{3,7},{5,1},{7,3},{8,12},{10,14},{12... | collective-permute-start | bytes 196616 | tf_op jit(solution)/shard_map/ppermute | solution.py:29
  25.1 1.4 collective-permute-start.15
  26.5 1.6 collective-permute-done.14
  28.1 1.2 collective-permute-done.15
  30.9 3.5 %handed.1 = (bf16[8,448,128]{2,1,0:T(8,128)(2,1)}, bf16[8,448,128]{2,1,0:T(8,128)(2,1)}, bf16[128,3584]{1,0:T(8,128)(2,1)}) custom-call(s32[5]{0:T(128)} %copy-done.3, bf16[2,16,512]{2,1,0:T(8,128)(2,1)} %copy-done.1, bf16[2,8,448,128]{3,2,1,0:T(8,128)(2,1)} %bitcast.72, bf16[2,8,448,128]{3,2,1,0:T(8,128)(2,1)} %bitcast.76, bf16[2,128,3584]{2,1,0:T(8,128)(2,1)} %refs_2_.3), custom_call_target="tpu_custom_call" | custom-call | bytes 6291456 | tf_op jit(solution)/shard_map/handed/pallas_call | solution.py:139
  34.8 2.2 %collective-permute-done.5.refs_9_ = bf16[2,8,448,128]{3,2,1,0:T(8,128)(2,1)} collective-permute-done((bf16[2,8,448,128]{3,2,1,0:T(8,128)(2,1)}, bf16[2,8,448,128]{3,2,1,0:T(8,128)(2,1)}, u32[]{:S(2)}, u32[]{:S(2)}) %collective-permute-start.5) | collective-permute-done | bytes 1835040 | tf_op jit(solution)/shard_map/ppermute | solution.py:294
  37.0 2.6 %collective-permute-done.6.refs_10_ = bf16[2,128,3584]{2,1,0:T(8,128)(2,1)} collective-permute-done((bf16[2,128,3584]{2,1,0:T(8,128)(2,1)}, bf16[2,128,3584]{2,1,0:T(8,128)(2,1)}, u32[]{:S(2)}, u32[]{:S(2)}) %collective-permute-start.6) | collective-permute-done | bytes 1835040 | tf_op jit(solution)/shard_map/ppermute | solution.py:294
  39.7 1.9 %collective-permute-start.7 = (bf16[32,1024]{1,0:T(8,128)(2,1)S(1)}, bf16[32,1024]{1,0:T(8,128)(2,1)S(1)}, u32[]{:S(2)}, u32[]{:S(2)}) collective-permute-start(bf16[32,1024]{1,0:T(8,128)(2,1)S(1)} %get-tuple-element.30), channel_id=1, source_target_pairs={{0,16},{16,32},{32,48},{48,64},{64,80},{80,96},{96,112},{112,0},{1... | collective-permute-start | bytes 196616 | tf_op jit(solution)/shard_map/ppermute | solution.py:29
  41.6 3.9 %collective-permute-start.10 = (bf16[32,1024]{1,0:T(8,128)(2,1)S(1)}, bf16[32,1024]{1,0:T(8,128)(2,1)S(1)}, u32[]{:S(2)}, u32[]{:S(2)}) collective-permute-start(bf16[32,1024]{1,0:T(8,128)(2,1)S(1)} %get-tuple-element.30), channel_id=1, source_target_pairs={{0,112},{16,0},{32,16},{48,32},{64,48},{80,64},{96,80},{112,96},{1... | collective-permute-start | bytes 196616 | tf_op jit(solution)/shard_map/ppermute | solution.py:29
  45.5 3.5 %collective-permute-done.7 = bf16[32,1024]{1,0:T(8,128)(2,1)S(1)} collective-permute-done((bf16[32,1024]{1,0:T(8,128)(2,1)S(1)}, bf16[32,1024]{1,0:T(8,128)(2,1)S(1)}, u32[]{:S(2)}, u32[]{:S(2)}) %collective-permute-start.7) | collective-permute-done | bytes 65568 | tf_op jit(solution)/shard_map/ppermute | solution.py:29
  49.1 3.8 %collective-permute-start.11 = (bf16[2,32,1024]{2,1,0:T(8,128)(2,1)S(1)}, bf16[2,32,1024]{2,1,0:T(8,128)(2,1)S(1)}, u32[]{:S(2)}, u32[]{:S(2)}) collective-permute-start(bf16[2,32,1024]{2,1,0:T(8,128)(2,1)S(1)} %get-tuple-element.59), channel_id=1, source_target_pairs={{0,96},{16,112},{32,0},{48,16},{64,32},{80,48},{96,64},{112,80},{1... | collective-permute-start | bytes 393224 | tf_op jit(solution)/shard_map/ppermute | solution.py:29
  52.8 4.0 %collective-permute-start.9 = (bf16[32,1024]{1,0:T(8,128)(2,1)S(1)}, bf16[32,1024]{1,0:T(8,128)(2,1)S(1)}, u32[]{:S(2)}, u32[]{:S(2)}) collective-permute-start(bf16[32,1024]{1,0:T(8,128)(2,1)S(1)} %get-tuple-element.30), channel_id=1, source_target_pairs={{0,64},{16,80},{32,96},{48,112},{64,0},{80,16},{96,32},{112,48},{1... | collective-permute-start | bytes 196616 | tf_op jit(solution)/shard_map/ppermute | solution.py:29
  56.9 12.3 %collective-permute-done.9 = bf16[32,1024]{1,0:T(8,128)(2,1)S(1)} collective-permute-done((bf16[32,1024]{1,0:T(8,128)(2,1)S(1)}, bf16[32,1024]{1,0:T(8,128)(2,1)S(1)}, u32[]{:S(2)}, u32[]{:S(2)}) %collective-permute-start.9) | collective-permute-done | bytes 65568 | tf_op jit(solution)/shard_map/ppermute | solution.py:29
  70.0 3.8 %collective-permute-start.17 = (bf16[8,32,1024]{2,1,0:T(8,128)(2,1)S(1)}, bf16[8,32,1024]{2,1,0:T(8,128)(2,1)S(1)}, u32[]{:S(2)}, u32[]{:S(2)}) collective-permute-start(bf16[8,32,1024]{2,1,0:T(8,128)(2,1)S(1)} %join.1.refs_1_), channel_id=1, source_target_pairs={{0,4},{2,6},{4,0},{6,2},{1,5},{3,7},{5,1},{7,3},{8,12},{10,14},{12... | collective-permute-start | bytes 1572872 | tf_op jit(solution)/shard_map/ppermute | solution.py:29
  73.7 15.9 %collective-permute-done.12.refs_4_ = bf16[8,448,128]{2,1,0:T(8,128)(2,1)S(1)} collective-permute-done((bf16[8,448,128]{2,1,0:T(8,128)(2,1)}, bf16[8,448,128]{2,1,0:T(8,128)(2,1)S(1)}, u32[]{:S(2)}, u32[]{:S(2)}) %collective-permute-start.12) | collective-permute-done | bytes 917536 | tf_op jit(solution)/shard_map/ppermute | solution.py:300
  89.7 3.7 %collective-permute-done.17.refs_3_ = bf16[8,32,1024]{2,1,0:T(8,128)(2,1)S(1)} collective-permute-done((bf16[8,32,1024]{2,1,0:T(8,128)(2,1)S(1)}, bf16[8,32,1024]{2,1,0:T(8,128)(2,1)S(1)}, u32[]{:S(2)}, u32[]{:S(2)}) %collective-permute-start.17) | collective-permute-done | bytes 524320 | tf_op jit(solution)/shard_map/ppermute | solution.py:29
  93.4 0.8 copy-done.10
  94.9 12.7 %layer.1 = (bf16[8,4,32,896]{3,2,1,0:T(8,128)(2,1)}, bf16[8,32,896]{2,1,0:T(8,128)(2,1)S(1)}, bf16[8,32,896]{2,1,0:T(8,128)(2,1)S(1)}, bf16[8,32,896]{2,1,0:T(8,...) custom-call(s32[5]{0:T(128)S(1)} %copy-done.4, s32[1,64]{1,0:T(1,128)S(1)} %bitcast.70, ...), custom_call_target="tpu_custom_call" | custom-call | flops 5637144576 | bytes 20971520 | tf_op jit(solution)/shard_map/layer/pallas_call | solution.py:253
  107.6 3.2 %collective-permute-start.19 = (bf16[128,3584]{1,0:T(8,128)(2,1)}, bf16[128,3584]{1,0:T(8,128)(2,1)S(1)}, u32[]{:S(2)}, u32[]{:S(2)}) collective-permute-start(bf16[128,3584]{1,0:T(8,128)(2,1)} %get-tuple-element.35), channel_id=1, source_target_pairs={{0,128},{128,0},{1,129},{129,1},{2,130},{130,2},{3,131},{131,3},{4... | collective-permute-start | bytes 2752520 | tf_op jit(solution)/shard_map/ppermute | solution.py:301
  110.8 1.4 collective-permute-start.23
  112.2 0.9 collective-permute-start.25
  113.3 16.2 %collective-permute-done.19.refs_5_ = bf16[128,3584]{1,0:T(8,128)(2,1)S(1)} collective-permute-done((bf16[128,3584]{1,0:T(8,128)(2,1)}, bf16[128,3584]{1,0:T(8,128)(2,1)S(1)}, u32[]{:S(2)}, u32[]{:S(2)}) %collective-permute-start.19) | collective-permute-done | bytes 917536 | tf_op jit(solution)/shard_map/ppermute | solution.py:301
  129.5 1.0 copy-done.8
  130.5 5.5 %swapped.1 = (bf16[2,8,448,128]{3,2,1,0:T(8,128)(2,1)}, bf16[2,8,448,128]{3,2,1,0:T(8,128)(2,1)}, bf16[2,128,3584]{2,1,0:T(8,128)(2,1)}) custom-call(s32[5]{0:T(128)} %copy-done.3, bf16[2,8,448,128]{3,2,1,0:T(8,128)(2,1)} %bitcast.74, bf16[2,8,448,128]{3,2,1,0:T(8,128)(2,1)} %bitcast.78, bf16[2,128,3584]{2,1,0:T(8,128)(2,1)} %refs_2_.3, ...), custom_call_target="tpu_custom_call" | custom-call | bytes 11534336 | tf_op jit(solution)/shard_map/swapped/pallas_call | solution.py:170
  136.1 1.3 add_convert_fusion
  137.4 2.9 %collective-permute-start.26 = (bf16[2,32,896]{2,1,0:T(8,128)(2,1)S(1)}, bf16[2,32,896]{2,1,0:T(8,128)(2,1)S(1)}, u32[]{:S(2)}, u32[]{:S(2)}) collective-permute-start(bf16[2,32,896]{2,1,0:T(8,128)(2,1)S(1)} %get-tuple-element.52), channel_id=1, source_target_pairs={{0,96},{16,112},{32,0},{48,16},{64,32},{80,48},{96,64},{112,80},{1... | collective-permute-start | bytes 344072 | tf_op jit(solution)/shard_map/ppermute | solution.py:29
  140.3 1.0 collective-permute-start.27
  141.4 3.4 %collective-permute-start.28 = (bf16[32,896]{1,0:T(8,128)(2,1)S(1)}, bf16[32,896]{1,0:T(8,128)(2,1)S(1)}, u32[]{:S(2)}, u32[]{:S(2)}) collective-permute-start(bf16[32,896]{1,0:T(8,128)(2,1)S(1)} %slice_bitcast_fusion), channel_id=1, source_target_pairs={{0,64},{16,80},{32,96},{48,112},{64,0},{80,16},{96,32},{112,48},{1... | collective-permute-start | bytes 172040 | tf_op jit(solution)/shard_map/ppermute | solution.py:29
  144.7 3.3 %collective-permute-done.26 = bf16[2,32,896]{2,1,0:T(8,128)(2,1)S(1)} collective-permute-done((bf16[2,32,896]{2,1,0:T(8,128)(2,1)S(1)}, bf16[2,32,896]{2,1,0:T(8,128)(2,1)S(1)}, u32[]{:S(2)}, u32[]{:S(2)}) %collective-permute-start.26) | collective-permute-done | bytes 114720 | tf_op jit(solution)/shard_map/ppermute | solution.py:29
  148.0 1.8 %collective-permute-done.27 = bf16[2,32,896]{2,1,0:T(8,128)(2,1)S(1)} collective-permute-done((bf16[2,32,896]{2,1,0:T(8,128)(2,1)S(1)}, bf16[2,32,896]{2,1,0:T(8,128)(2,1)S(1)}, u32[]{:S(2)}, u32[]{:S(2)}) %collective-permute-start.27) | collective-permute-done | bytes 114720 | tf_op jit(solution)/shard_map/ppermute | solution.py:29
  149.9 2.4 %collective-permute-start.29 = (bf16[32,896]{1,0:T(8,128)(2,1)S(1)}, bf16[32,896]{1,0:T(8,128)(2,1)S(1)}, u32[]{:S(2)}, u32[]{:S(2)}) collective-permute-start(bf16[32,896]{1,0:T(8,128)(2,1)S(1)} %get-tuple-element.50), channel_id=1, source_target_pairs={{0,112},{16,0},{32,16},{48,32},{64,48},{80,64},{96,80},{112,96},{1... | collective-permute-start | bytes 172040 | tf_op jit(solution)/shard_map/ppermute | solution.py:29
  152.3 1.9 %collective-permute-start.30 = (bf16[32,896]{1,0:T(8,128)(2,1)S(1)}, bf16[32,896]{1,0:T(8,128)(2,1)S(1)}, u32[]{:S(2)}, u32[]{:S(2)}) collective-permute-start(bf16[32,896]{1,0:T(8,128)(2,1)S(1)} %get-tuple-element.51), channel_id=1, source_target_pairs={{0,16},{16,32},{32,48},{48,64},{64,80},{80,96},{96,112},{112,0},{1... | collective-permute-start | bytes 172040 | tf_op jit(solution)/shard_map/ppermute | solution.py:29
  154.1 0.9 slice_bitcast_fusion.3
  155.0 3.6 %collective-permute-start.20 = (bf16[32,896]{1,0:T(8,128)(2,1)S(1)}, bf16[32,896]{1,0:T(8,128)(2,1)S(1)}, u32[]{:S(2)}, u32[]{:S(2)}) collective-permute-start(bf16[32,896]{1,0:T(8,128)(2,1)S(1)} %get-tuple-element.54), channel_id=1, source_target_pairs={{0,6},{2,0},{4,2},{6,4},{1,7},{3,1},{5,3},{7,5},{8,14},{10,8},{12,... | collective-permute-start | bytes 172040 | tf_op jit(solution)/shard_map/ppermute | solution.py:29
  159.7 0.8 collective-permute-done.20
  160.5 3.9 %collective-permute-done.21 = bf16[32,896]{1,0:T(8,128)(2,1)S(1)} collective-permute-done((bf16[32,896]{1,0:T(8,128)(2,1)S(1)}, bf16[32,896]{1,0:T(8,128)(2,1)S(1)}, u32[]{:S(2)}, u32[]{:S(2)}) %collective-permute-start.21) | collective-permute-done | bytes 57376 | tf_op jit(solution)/shard_map/ppermute | solution.py:29
  165.0 0.9 fusion.2
  166.0 2.1 %collective-permute-start.32 = (bf16[2,16,448]{2,1,0:T(8,128)(2,1)S(1)}, bf16[2,16,448]{2,1,0:T(8,128)(2,1)S(1)}, u32[]{:S(2)}, u32[]{:S(2)}) collective-permute-start(bf16[2,16,448]{2,1,0:T(8,128)(2,1)S(1)} %get-tuple-element.57), channel_id=1, source_target_pairs={{0,128},{1,129},{128,0},{129,1},{2,130},{3,131},{130,2},{131,3},{4... | collective-permute-start | bytes 86024 | tf_op jit(solution)/shard_map/ppermute | solution.py:29
  168.0 1.2 collective-permute-start.33
  169.3 0.8 collective-permute-start.31
  171.9 2.5 %collective-permute-done.31 = bf16[2,16,448]{2,1,0:T(8,128)(2,1)S(1)} collective-permute-done((bf16[2,16,448]{2,1,0:T(8,128)(2,1)S(1)}, bf16[2,16,448]{2,1,0:T(8,128)(2,1)S(1)}, u32[]{:S(2)}, u32[]{:S(2)}) %collective-permute-start.31) | collective-permute-done | bytes 28704 | tf_op jit(solution)/shard_map/ppermute | solution.py:29
  (78 shorter events, 11.6 us)
Async XLA Ops:
  7.2 87.0 %all-gather.3.cloned.1.call-start = ((), (), s32[]{:S(2)}) async-start(), calls=%async_computation.2 | async-start | bytes 2359296 | tf_op jit(solution)/shard_map/all_gather | solution.py:298
  10.7 0.8 copy-start.2
  11.5 19.4 %copy-start.3 = (s32[5]{0:T(128)}, s32[5]{0:T(128)S(1)}, u32[]{:S(2)}) copy-start(s32[5]{0:T(128)S(1)} %stack.56.place) | copy-start | bytes 64
  12.3 18.7 %copy-start.1 = (bf16[2,16,512]{2,1,0:T(8,128)(2,1)}, bf16[2,16,512]{2,1,0:T(8,128)(2,1)S(1)}, u32[]{:S(2)}) copy-start(bf16[2,16,512]{2,1,0:T(8,128)(2,1)S(1)} %ride.1.lower_ref.refs_0_) | copy-start | bytes 98308
  12.3 3.9 %collective-permute-start = (bf16[2,16,512]{2,1,0:T(8,128)(2,1)S(1)}, bf16[2,16,512]{2,1,0:T(8,128)(2,1)S(1)}, u32[]{:S(2)}, u32[]{:S(2)}) collective-permute-start(bf16[2,16,512]{2,1,0:T(8,128)(2,1)S(1)} %ride.1.lower_ref.refs_0_), channel_id=1, source_target_pairs={{0,1},{1,128},{128,129},{129,0},{2,3},{3,130},{130,131},{131,2},{4... | collective-permute-start | bytes 98312 | tf_op jit(solution)/shard_map/ppermute | solution.py:29
  14.2 5.4 %collective-permute-start.1 = (bf16[2,16,512]{2,1,0:T(8,128)(2,1)S(1)}, bf16[2,16,512]{2,1,0:T(8,128)(2,1)S(1)}, u32[]{:S(2)}, u32[]{:S(2)}) collective-permute-start(bf16[2,16,512]{2,1,0:T(8,128)(2,1)S(1)} %ride.1.lower_ref.refs_0_), channel_id=1, source_target_pairs={{0,128},{1,129},{128,0},{129,1},{2,130},{3,131},{130,2},{131,3},{4... | collective-permute-start | bytes 98312 | tf_op jit(solution)/shard_map/ppermute | solution.py:29
  15.1 5.1 %collective-permute-start.2 = (bf16[2,16,512]{2,1,0:T(8,128)(2,1)S(1)}, bf16[2,16,512]{2,1,0:T(8,128)(2,1)S(1)}, u32[]{:S(2)}, u32[]{:S(2)}) collective-permute-start(bf16[2,16,512]{2,1,0:T(8,128)(2,1)S(1)} %ride.1.lower_ref.refs_0_), channel_id=1, source_target_pairs={{0,129},{1,0},{128,1},{129,128},{2,131},{3,2},{130,3},{131,130},{4... | collective-permute-start | bytes 98312 | tf_op jit(solution)/shard_map/ppermute | solution.py:29
  20.8 5.7 %collective-permute-start.13 = (bf16[32,1024]{1,0:T(8,128)(2,1)S(1)}, bf16[32,1024]{1,0:T(8,128)(2,1)S(1)}, u32[]{:S(2)}, u32[]{:S(2)}) collective-permute-start(bf16[32,1024]{1,0:T(8,128)(2,1)S(1)} %get-tuple-element.27), channel_id=1, source_target_pairs={{0,2},{2,4},{4,6},{6,0},{1,3},{3,5},{5,7},{7,1},{8,10},{10,12},{12... | collective-permute-start | bytes 196616 | tf_op jit(solution)/shard_map/ppermute | solution.py:29
  22.4 5.8 %collective-permute-start.14 = (bf16[32,1024]{1,0:T(8,128)(2,1)S(1)}, bf16[32,1024]{1,0:T(8,128)(2,1)S(1)}, u32[]{:S(2)}, u32[]{:S(2)}) collective-permute-start(bf16[32,1024]{1,0:T(8,128)(2,1)S(1)} %get-tuple-element.27), channel_id=1, source_target_pairs={{0,4},{2,6},{4,0},{6,2},{1,5},{3,7},{5,1},{7,3},{8,12},{10,14},{12... | collective-permute-start | bytes 196616 | tf_op jit(solution)/shard_map/ppermute | solution.py:29
  25.1 4.3 %collective-permute-start.15 = (bf16[32,1024]{1,0:T(8,128)(2,1)S(1)}, bf16[32,1024]{1,0:T(8,128)(2,1)S(1)}, u32[]{:S(2)}, u32[]{:S(2)}) collective-permute-start(bf16[32,1024]{1,0:T(8,128)(2,1)S(1)} %get-tuple-element.27), channel_id=1, source_target_pairs={{0,6},{2,0},{4,2},{6,4},{1,7},{3,1},{5,3},{7,5},{8,14},{10,8},{12,... | collective-permute-start | bytes 196616 | tf_op jit(solution)/shard_map/ppermute | solution.py:29
  30.1 124.0 %reduce-scatter.2.cloned.1.call-start = ((), (), s32[]{:S(2)}) async-start(), calls=%async_computation.1 | async-start | bytes 2064384 | tf_op jit(solution)/shard_map/reduce_scatter | solution.py:306
  30.2 4.6 %collective-permute-start.4 = (bf16[2,8,448,128]{3,2,1,0:T(8,128)(2,1)}, bf16[2,8,448,128]{3,2,1,0:T(8,128)(2,1)}, u32[]{:S(2)}, u32[]{:S(2)}) collective-permute-start(bf16[2,8,448,128]{3,2,1,0:T(8,128)(2,1)} %bitcast.71), channel_id=1, source_target_pairs={{0,8},{8,0},{1,9},{9,1},{2,10},{10,2},{3,11},{11,3},{4,12},{12,4},... | collective-permute-start | bytes 5505032 | tf_op jit(solution)/shard_map/ppermute | solution.py:294
  30.3 63.9 %copy-start.5 = (s32[64]{0:T(128)S(1)}, s32[64]{0:T(128)}, u32[]{:S(2)}) copy-start(s32[64]{0:T(128)} %param.11) | copy-start | bytes 772
  30.3 6.7 %collective-permute-start.5 = (bf16[2,8,448,128]{3,2,1,0:T(8,128)(2,1)}, bf16[2,8,448,128]{3,2,1,0:T(8,128)(2,1)}, u32[]{:S(2)}, u32[]{:S(2)}) collective-permute-start(bf16[2,8,448,128]{3,2,1,0:T(8,128)(2,1)} %bitcast.75), channel_id=1, source_target_pairs={{0,8},{8,0},{1,9},{9,1},{2,10},{10,2},{3,11},{11,3},{4,12},{12,4},... | collective-permute-start | bytes 5505032 | tf_op jit(solution)/shard_map/ppermute | solution.py:294
  30.8 8.9 %collective-permute-start.6 = (bf16[2,128,3584]{2,1,0:T(8,128)(2,1)}, bf16[2,128,3584]{2,1,0:T(8,128)(2,1)}, u32[]{:S(2)}, u32[]{:S(2)}) collective-permute-start(bf16[2,128,3584]{2,1,0:T(8,128)(2,1)} %refs_2_.3), channel_id=1, source_target_pairs={{0,8},{8,0},{1,9},{9,1},{2,10},{10,2},{3,11},{11,3},{4,12},{12,4},... | collective-permute-start | bytes 5505032 | tf_op jit(solution)/shard_map/ppermute | solution.py:294
  34.5 34.7 %collective-permute-start.3 = (bf16[8,448,128]{2,1,0:T(8,128)(2,1)}, bf16[8,448,128]{2,1,0:T(8,128)(2,1)S(1)}, u32[]{:S(2)}, u32[]{:S(2)}) collective-permute-start(bf16[8,448,128]{2,1,0:T(8,128)(2,1)} %get-tuple-element.29), channel_id=1, source_target_pairs={{0,128},{128,0},{1,129},{129,1},{2,130},{130,2},{3,131},{131,3},{4... | collective-permute-start | bytes 2752520 | tf_op jit(solution)/shard_map/ppermute | solution.py:297
  39.7 9.4 %collective-permute-start.7 = (bf16[32,1024]{1,0:T(8,128)(2,1)S(1)}, bf16[32,1024]{1,0:T(8,128)(2,1)S(1)}, u32[]{:S(2)}, u32[]{:S(2)}) collective-permute-start(bf16[32,1024]{1,0:T(8,128)(2,1)S(1)} %get-tuple-element.30), channel_id=1, source_target_pairs={{0,16},{16,32},{32,48},{48,64},{64,80},{80,96},{96,112},{112,0},{1... | collective-permute-start | bytes 196616 | tf_op jit(solution)/shard_map/ppermute | solution.py:29
  41.6 7.5 %collective-permute-start.10 = (bf16[32,1024]{1,0:T(8,128)(2,1)S(1)}, bf16[32,1024]{1,0:T(8,128)(2,1)S(1)}, u32[]{:S(2)}, u32[]{:S(2)}) collective-permute-start(bf16[32,1024]{1,0:T(8,128)(2,1)S(1)} %get-tuple-element.30), channel_id=1, source_target_pairs={{0,112},{16,0},{32,16},{48,32},{64,48},{80,64},{96,80},{112,96},{1... | collective-permute-start | bytes 196616 | tf_op jit(solution)/shard_map/ppermute | solution.py:29
  49.1 20.1 %collective-permute-start.11 = (bf16[2,32,1024]{2,1,0:T(8,128)(2,1)S(1)}, bf16[2,32,1024]{2,1,0:T(8,128)(2,1)S(1)}, u32[]{:S(2)}, u32[]{:S(2)}) collective-permute-start(bf16[2,32,1024]{2,1,0:T(8,128)(2,1)S(1)} %get-tuple-element.59), channel_id=1, source_target_pairs={{0,96},{16,112},{32,0},{48,16},{64,32},{80,48},{96,64},{112,80},{1... | collective-permute-start | bytes 393224 | tf_op jit(solution)/shard_map/ppermute | solution.py:29
  52.8 16.3 %collective-permute-start.8 = (bf16[2,32,1024]{2,1,0:T(8,128)(2,1)S(1)}, bf16[2,32,1024]{2,1,0:T(8,128)(2,1)S(1)}, u32[]{:S(2)}, u32[]{:S(2)}) collective-permute-start(bf16[2,32,1024]{2,1,0:T(8,128)(2,1)S(1)} %get-tuple-element.60), channel_id=1, source_target_pairs={{0,32},{16,48},{32,64},{48,80},{64,96},{80,112},{96,0},{112,16},{1... | collective-permute-start | bytes 393224 | tf_op jit(solution)/shard_map/ppermute | solution.py:29
  52.8 16.3 %collective-permute-start.9 = (bf16[32,1024]{1,0:T(8,128)(2,1)S(1)}, bf16[32,1024]{1,0:T(8,128)(2,1)S(1)}, u32[]{:S(2)}, u32[]{:S(2)}) collective-permute-start(bf16[32,1024]{1,0:T(8,128)(2,1)S(1)} %get-tuple-element.30), channel_id=1, source_target_pairs={{0,64},{16,80},{32,96},{48,112},{64,0},{80,16},{96,32},{112,48},{1... | collective-permute-start | bytes 196616 | tf_op jit(solution)/shard_map/ppermute | solution.py:29
  69.2 25.0 %copy-start = (bf16[8,32,1024]{2,1,0:T(8,128)(2,1)}, bf16[8,32,1024]{2,1,0:T(8,128)(2,1)S(1)}, u32[]{:S(2)}) copy-start(bf16[8,32,1024]{2,1,0:T(8,128)(2,1)S(1)} %join.1.refs_1_) | copy-start | bytes 1572868
  69.2 38.3 %copy-start.6 = (bf16[8,448,128]{2,1,0:T(8,128)(2,1)}, bf16[8,448,128]{2,1,0:T(8,128)(2,1)S(1)}, u32[]{:S(2)}) copy-start(bf16[8,448,128]{2,1,0:T(8,128)(2,1)S(1)} %collective-permute-done.3.refs_3_) | copy-start | bytes 2752516
  69.2 20.5 %collective-permute-start.12 = (bf16[8,448,128]{2,1,0:T(8,128)(2,1)}, bf16[8,448,128]{2,1,0:T(8,128)(2,1)S(1)}, u32[]{:S(2)}, u32[]{:S(2)}) collective-permute-start(bf16[8,448,128]{2,1,0:T(8,128)(2,1)} %get-tuple-element.31), channel_id=1, source_target_pairs={{0,128},{128,0},{1,129},{129,1},{2,130},{130,2},{3,131},{131,3},{4... | collective-permute-start | bytes 2752520 | tf_op jit(solution)/shard_map/ppermute | solution.py:300
  69.5 20.2 %collective-permute-start.16 = (bf16[8,32,1024]{2,1,0:T(8,128)(2,1)S(1)}, bf16[8,32,1024]{2,1,0:T(8,128)(2,1)S(1)}, u32[]{:S(2)}, u32[]{:S(2)}) collective-permute-start(bf16[8,32,1024]{2,1,0:T(8,128)(2,1)S(1)} %join.1.refs_1_), channel_id=1, source_target_pairs={{0,2},{2,4},{4,6},{6,0},{1,3},{3,5},{5,7},{7,1},{8,10},{10,12},{12... | collective-permute-start | bytes 1572872 | tf_op jit(solution)/shard_map/ppermute | solution.py:29
  70.0 23.4 %collective-permute-start.17 = (bf16[8,32,1024]{2,1,0:T(8,128)(2,1)S(1)}, bf16[8,32,1024]{2,1,0:T(8,128)(2,1)S(1)}, u32[]{:S(2)}, u32[]{:S(2)}) collective-permute-start(bf16[8,32,1024]{2,1,0:T(8,128)(2,1)S(1)} %join.1.refs_1_), channel_id=1, source_target_pairs={{0,4},{2,6},{4,0},{6,2},{1,5},{3,7},{5,1},{7,3},{8,12},{10,14},{12... | collective-permute-start | bytes 1572872 | tf_op jit(solution)/shard_map/ppermute | solution.py:29
  73.7 20.4 %collective-permute-start.18 = (bf16[8,32,1024]{2,1,0:T(8,128)(2,1)S(1)}, bf16[8,32,1024]{2,1,0:T(8,128)(2,1)}, u32[]{:S(2)}, u32[]{:S(2)}) collective-permute-start(bf16[8,32,1024]{2,1,0:T(8,128)(2,1)S(1)} %join.1.refs_1_), channel_id=1, source_target_pairs={{0,6},{2,0},{4,2},{6,4},{1,7},{3,1},{5,3},{7,5},{8,14},{10,8},{12,... | collective-permute-start | bytes 1572872 | tf_op jit(solution)/shard_map/ppermute | solution.py:29
  89.7 4.5 %copy-start.7 = (bf16[8,448,128]{2,1,0:T(8,128)(2,1)}, bf16[8,448,128]{2,1,0:T(8,128)(2,1)S(1)}, u32[]{:S(2)}) copy-start(bf16[8,448,128]{2,1,0:T(8,128)(2,1)S(1)} %collective-permute-done.12.refs_4_) | copy-start | bytes 2752516
  89.7 4.5 %copy-start.9 = (bf16[8,32,1024]{2,1,0:T(8,128)(2,1)}, bf16[8,32,1024]{2,1,0:T(8,128)(2,1)S(1)}, u32[]{:S(2)}) copy-start(bf16[8,32,1024]{2,1,0:T(8,128)(2,1)S(1)} %collective-permute-done.16.refs_2_) | copy-start | bytes 1572868
  93.4 0.8 copy-start.10
  107.5 5.5 %copy-start.11 = (s32[32]{0:T(128)S(1)}, s32[32]{0:T(128)}, u32[]{:S(2)}) copy-start(s32[32]{0:T(128)} %param.12) | copy-start | bytes 388
  107.6 21.9 %collective-permute-start.19 = (bf16[128,3584]{1,0:T(8,128)(2,1)}, bf16[128,3584]{1,0:T(8,128)(2,1)S(1)}, u32[]{:S(2)}, u32[]{:S(2)}) collective-permute-start(bf16[128,3584]{1,0:T(8,128)(2,1)} %get-tuple-element.35), channel_id=1, source_target_pairs={{0,128},{128,0},{1,129},{129,1},{2,130},{130,2},{3,131},{131,3},{4... | collective-permute-start | bytes 2752520 | tf_op jit(solution)/shard_map/ppermute | solution.py:301
  110.8 25.2 %collective-permute-start.23 = (bf16[8,32,896]{2,1,0:T(8,128)(2,1)S(1)}, bf16[8,32,896]{2,1,0:T(8,128)(2,1)S(1)}, u32[]{:S(2)}, u32[]{:S(2)}) collective-permute-start(bf16[8,32,896]{2,1,0:T(8,128)(2,1)S(1)} %get-tuple-element.41), channel_id=1, source_target_pairs={{0,6},{2,0},{4,2},{6,4},{1,7},{3,1},{5,3},{7,5},{8,14},{10,8},{12,... | collective-permute-start | bytes 1376264 | tf_op jit(solution)/shard_map/ppermute | solution.py:29
  112.2 23.8 %collective-permute-start.24 = (bf16[8,32,896]{2,1,0:T(8,128)(2,1)S(1)}, bf16[8,32,896]{2,1,0:T(8,128)(2,1)S(1)}, u32[]{:S(2)}, u32[]{:S(2)}) collective-permute-start(bf16[8,32,896]{2,1,0:T(8,128)(2,1)S(1)} %get-tuple-element.42), channel_id=1, source_target_pairs={{0,4},{2,6},{4,0},{6,2},{1,5},{3,7},{5,1},{7,3},{8,12},{10,14},{12... | collective-permute-start | bytes 1376264 | tf_op jit(solution)/shard_map/ppermute | solution.py:29
  112.2 23.8 %collective-permute-start.25 = (bf16[8,32,896]{2,1,0:T(8,128)(2,1)S(1)}, bf16[8,32,896]{2,1,0:T(8,128)(2,1)}, u32[]{:S(2)}, u32[]{:S(2)}) collective-permute-start(bf16[8,32,896]{2,1,0:T(8,128)(2,1)S(1)} %get-tuple-element.43), channel_id=1, source_target_pairs={{0,2},{2,4},{4,6},{6,0},{1,3},{3,5},{5,7},{7,1},{8,10},{10,12},{12... | collective-permute-start | bytes 1376264 | tf_op jit(solution)/shard_map/ppermute | solution.py:29
  113.2 56.9 %collective-permute-start.34 = (f32[64]{0:T(128)S(1)}, f32[64]{0:T(128)S(1)}, u32[]{:S(2)}, u32[]{:S(2)}) collective-permute-start(f32[64]{0:T(128)S(1)} %slice_bitcast_fusion.4), channel_id=1, source_target_pairs={{0,8},{8,0},{1,9},{9,1},{2,10},{10,2},{3,11},{11,3},{4,12},{12,4},... | collective-permute-start | bytes 776 | tf_op jit(solution)/shard_map/ppermute | solution.py:315
  129.5 1.0 copy-start.8
  137.4 10.6 %collective-permute-start.26 = (bf16[2,32,896]{2,1,0:T(8,128)(2,1)S(1)}, bf16[2,32,896]{2,1,0:T(8,128)(2,1)S(1)}, u32[]{:S(2)}, u32[]{:S(2)}) collective-permute-start(bf16[2,32,896]{2,1,0:T(8,128)(2,1)S(1)} %get-tuple-element.52), channel_id=1, source_target_pairs={{0,96},{16,112},{32,0},{48,16},{64,32},{80,48},{96,64},{112,80},{1... | collective-permute-start | bytes 344072 | tf_op jit(solution)/shard_map/ppermute | solution.py:29
  140.3 9.5 %collective-permute-start.27 = (bf16[2,32,896]{2,1,0:T(8,128)(2,1)S(1)}, bf16[2,32,896]{2,1,0:T(8,128)(2,1)S(1)}, u32[]{:S(2)}, u32[]{:S(2)}) collective-permute-start(bf16[2,32,896]{2,1,0:T(8,128)(2,1)S(1)} %get-tuple-element.53), channel_id=1, source_target_pairs={{0,32},{16,48},{32,64},{48,80},{64,96},{80,112},{96,0},{112,16},{1... | collective-permute-start | bytes 344072 | tf_op jit(solution)/shard_map/ppermute | solution.py:29
  141.4 17.3 %collective-permute-start.28 = (bf16[32,896]{1,0:T(8,128)(2,1)S(1)}, bf16[32,896]{1,0:T(8,128)(2,1)S(1)}, u32[]{:S(2)}, u32[]{:S(2)}) collective-permute-start(bf16[32,896]{1,0:T(8,128)(2,1)S(1)} %slice_bitcast_fusion), channel_id=1, source_target_pairs={{0,64},{16,80},{32,96},{48,112},{64,0},{80,16},{96,32},{112,48},{1... | collective-permute-start | bytes 172040 | tf_op jit(solution)/shard_map/ppermute | solution.py:29
  149.9 9.4 %collective-permute-start.29 = (bf16[32,896]{1,0:T(8,128)(2,1)S(1)}, bf16[32,896]{1,0:T(8,128)(2,1)S(1)}, u32[]{:S(2)}, u32[]{:S(2)}) collective-permute-start(bf16[32,896]{1,0:T(8,128)(2,1)S(1)} %get-tuple-element.50), channel_id=1, source_target_pairs={{0,112},{16,0},{32,16},{48,32},{64,48},{80,64},{96,80},{112,96},{1... | collective-permute-start | bytes 172040 | tf_op jit(solution)/shard_map/ppermute | solution.py:29
  152.3 7.4 %collective-permute-start.30 = (bf16[32,896]{1,0:T(8,128)(2,1)S(1)}, bf16[32,896]{1,0:T(8,128)(2,1)S(1)}, u32[]{:S(2)}, u32[]{:S(2)}) collective-permute-start(bf16[32,896]{1,0:T(8,128)(2,1)S(1)} %get-tuple-element.51), channel_id=1, source_target_pairs={{0,16},{16,32},{32,48},{48,64},{64,80},{80,96},{96,112},{112,0},{1... | collective-permute-start | bytes 172040 | tf_op jit(solution)/shard_map/ppermute | solution.py:29
  155.0 5.5 %collective-permute-start.20 = (bf16[32,896]{1,0:T(8,128)(2,1)S(1)}, bf16[32,896]{1,0:T(8,128)(2,1)S(1)}, u32[]{:S(2)}, u32[]{:S(2)}) collective-permute-start(bf16[32,896]{1,0:T(8,128)(2,1)S(1)} %get-tuple-element.54), channel_id=1, source_target_pairs={{0,6},{2,0},{4,2},{6,4},{1,7},{3,1},{5,3},{7,5},{8,14},{10,8},{12,... | collective-permute-start | bytes 172040 | tf_op jit(solution)/shard_map/ppermute | solution.py:29
  158.7 5.7 %collective-permute-start.21 = (bf16[32,896]{1,0:T(8,128)(2,1)S(1)}, bf16[32,896]{1,0:T(8,128)(2,1)S(1)}, u32[]{:S(2)}, u32[]{:S(2)}) collective-permute-start(bf16[32,896]{1,0:T(8,128)(2,1)S(1)} %get-tuple-element.56), channel_id=1, source_target_pairs={{0,4},{2,6},{4,0},{6,2},{1,5},{3,7},{5,1},{7,3},{8,12},{10,14},{12... | collective-permute-start | bytes 172040 | tf_op jit(solution)/shard_map/ppermute | solution.py:29
  159.2 5.8 %collective-permute-start.22 = (bf16[32,896]{1,0:T(8,128)(2,1)S(1)}, bf16[32,896]{1,0:T(8,128)(2,1)S(1)}, u32[]{:S(2)}, u32[]{:S(2)}) collective-permute-start(bf16[32,896]{1,0:T(8,128)(2,1)S(1)} %get-tuple-element.55), channel_id=1, source_target_pairs={{0,2},{2,4},{4,6},{6,0},{1,3},{3,5},{5,7},{7,1},{8,10},{10,12},{12... | collective-permute-start | bytes 172040 | tf_op jit(solution)/shard_map/ppermute | solution.py:29
  166.0 5.5 %collective-permute-start.32 = (bf16[2,16,448]{2,1,0:T(8,128)(2,1)S(1)}, bf16[2,16,448]{2,1,0:T(8,128)(2,1)S(1)}, u32[]{:S(2)}, u32[]{:S(2)}) collective-permute-start(bf16[2,16,448]{2,1,0:T(8,128)(2,1)S(1)} %get-tuple-element.57), channel_id=1, source_target_pairs={{0,128},{1,129},{128,0},{129,1},{2,130},{3,131},{130,2},{131,3},{4... | collective-permute-start | bytes 86024 | tf_op jit(solution)/shard_map/ppermute | solution.py:29
  168.0 3.9 %collective-permute-start.33 = (bf16[2,16,448]{2,1,0:T(8,128)(2,1)S(1)}, bf16[2,16,448]{2,1,0:T(8,128)(2,1)S(1)}, u32[]{:S(2)}, u32[]{:S(2)}) collective-permute-start(bf16[2,16,448]{2,1,0:T(8,128)(2,1)S(1)} %get-tuple-element.58), channel_id=1, source_target_pairs={{0,1},{1,128},{128,129},{129,0},{2,3},{3,130},{130,131},{131,2},{4... | collective-permute-start | bytes 86024 | tf_op jit(solution)/shard_map/ppermute | solution.py:29
  169.3 5.1 %collective-permute-start.31 = (bf16[2,16,448]{2,1,0:T(8,128)(2,1)S(1)}, bf16[2,16,448]{2,1,0:T(8,128)(2,1)S(1)}, u32[]{:S(2)}, u32[]{:S(2)}) collective-permute-start(bf16[2,16,448]{2,1,0:T(8,128)(2,1)S(1)} %get-tuple-element.45), channel_id=1, source_target_pairs={{0,129},{1,0},{128,1},{129,128},{2,131},{3,2},{130,3},{131,130},{4... | collective-permute-start | bytes 86024 | tf_op jit(solution)/shard_map/ppermute | solution.py:29
  (1 other events, 0.7 us)
Sparse Core Ops, SparseCore 0:
  30.3 50.2 all-gather.2
  107.7 45.0 reduce-scatter.1

commit v3 on v2

--- a/solution.py
+++ b/solution.py
@@ -33,6 +33,10 @@
     return functools.reduce(jnp.add, [v.astype(jnp.float32) for v in values]).astype(jnp.bfloat16)
 
 
+def after(value, *earlier):
+    return lax.optimization_barrier((value, earlier))[0]
+
+
 def gather_ring(value, axes):
     return [value] + [send(value, axes, k) for k in range(1, ring_size(axes))]
 
@@ -41,8 +45,9 @@
     return total([pieces[0]] + [send(piece, axes, -k) for k, piece in enumerate(pieces) if k])
 
 
-def gather_z(value):
-    back, ahead, far = send(value, "z", 1), send(value, "z", -1), send(value, "z", 4)
+def gather_z(value, beside):
+    first = [send(value, "z", 1), send(value, "z", -1), send(value, "z", 4)]
+    back, ahead, far = after(first, *beside)
     back2 = send(jnp.stack([value, back]), "z", 2)
     ahead2 = send(jnp.stack([value, ahead]), "z", -2)
     return run_join([value[None], back[None], back2, far[None], ahead2, ahead[None]])
@@ -78,15 +83,19 @@
 
 
 def ride_kernel(place, tokens_ref, routes_ref, gate_ref, out_ref):
-    labels = lax.broadcasted_iota(jnp.int32, (2, GROUP, LANES - WIDTH), 2)
-    gate = gate_ref[...]
-    part = jnp.where(lax.rem(place[3], 2) == 0, gate >> 8, gate & 255)
-    routes = routes_ref[...]
-    ride = jnp.zeros(labels.shape, jnp.int32)
-    for k in range(routes.shape[2]):
-        ride = ride + jnp.where(routes[:, :, k : k + 1] == labels, part[:, :, k : k + 1], 0)
-    ride = ride.astype(jnp.float32).astype(jnp.bfloat16)
-    out_ref[...] = jnp.concatenate([tokens_ref[...], ride], axis=2)
+    labels = lax.broadcasted_iota(jnp.int32, (LANES - WIDTH, GROUP), 0)
+    turn = (
+        lax.broadcasted_iota(jnp.int32, (GROUP, GROUP), 0) == lax.broadcasted_iota(jnp.int32, (GROUP, GROUP), 1)
+    ).astype(jnp.bfloat16)
+    for step in range(2):
+        gate, routes = gate_ref[step], routes_ref[step]
+        part = jnp.where(lax.rem(place[3], 2) == 0, gate >> 8, gate & 255)
+        ride = jnp.zeros(labels.shape, jnp.int32)
+        for k in range(routes.shape[0]):
+            ride = ride + jnp.where(routes[k : k + 1] == labels, part[k : k + 1], 0)
+        ride = ride.astype(jnp.float32).astype(jnp.bfloat16)
+        ride = lax.dot_general(turn, ride, (((1,), (1,)), ((), ())), preferred_element_type=jnp.float32)
+        out_ref[step] = jnp.concatenate([tokens_ref[step], ride.astype(jnp.bfloat16)], axis=1)
 
 
 def run_ride(place, tokens, routes, gate_fix):
@@ -98,7 +107,7 @@
         out_specs=vmem,
         compiler_params=SMALL,
         name="ride",
-    )(place, tokens, routes, gate_fix)
+    )(place, tokens, routes.transpose(0, 2, 1), gate_fix.transpose(0, 2, 1))
 
 
 def merge_kernel(place, *refs):
@@ -122,9 +131,11 @@
     )(place, *from_y)
 
 
-def handed_kernel(place, lower_ref, *refs):
-    ins = [pltpu.make_async_copy(refs[k].at[place[4]], refs[6 + k], refs[9].at[k]) for k in range(3)]
-    outs = [pltpu.make_async_copy(refs[6 + k], refs[3 + k], refs[9].at[3 + k]) for k in range(3)]
+def handed_kernel(place, slots, *refs):
+    count = (len(refs) - 2) // 3
+    slot, sems = slots[place[4]], refs[-1]
+    ins = [pltpu.make_async_copy(refs[k].at[slot], refs[2 * count + 1 + k], sems.at[k]) for k in range(count)]
+    outs = [pltpu.make_async_copy(refs[2 * count + 1 + k], refs[count + 1 + k], sems.at[count + k]) for k in range(count)]
     for copy in ins:
         copy.start()
     for copy_in, copy_out in zip(ins, outs):
@@ -134,22 +145,23 @@
         copy.wait()
 
 
-def run_handed(place, lower, panels):
-    hbm = pl.BlockSpec(memory_space=pltpu.HBM)
+def run_handed(place, slots, panels, earlier):
+    hbm, smem = pl.BlockSpec(memory_space=pltpu.HBM), pl.BlockSpec(memory_space=pltpu.SMEM)
     return pl.pallas_call(
         handed_kernel,
         out_shape=[jax.ShapeDtypeStruct(p.shape[1:], p.dtype) for p in panels],
-        in_specs=[pl.BlockSpec(memory_space=pltpu.SMEM), pl.BlockSpec(memory_space=pltpu.VMEM)] + [hbm] * 3,
-        out_specs=[hbm] * 3,
-        scratch_shapes=[pltpu.VMEM(p.shape[1:], p.dtype) for p in panels] + [pltpu.SemaphoreType.DMA((6,))],
+        in_specs=[smem, smem] + [hbm] * (len(panels) + 1),
+        out_specs=[hbm] * len(panels),
+        scratch_shapes=[pltpu.VMEM(p.shape[1:], p.dtype) for p in panels]
+        + [pltpu.SemaphoreType.DMA((2 * len(panels),))],
         compiler_params=LARGE,
-        cost_estimate=pl.CostEstimate(flops=0, bytes_accessed=6 * 2**20, transcendentals=0),
+        cost_estimate=pl.CostEstimate(flops=0, bytes_accessed=2 * len(panels) * 2**20, transcendentals=0),
         name="handed",
-    )(place, lower, *panels)
-
-
-def swapped_kernel(place, *refs):
-    slot = place[4]
+    )(place, slots, *panels, earlier)
+
+
+def swapped_kernel(place, slots, *refs):
+    slot = slots[place[4]]
     ins, outs = [], []
     for k in range(3):
         panel, taken, out, room = refs[k], refs[3 + k], refs[6 + k], refs[9 + k]
@@ -165,18 +177,18 @@
         copy.wait()
 
 
-def run_swapped(place, panels, taken):
+def run_swapped(place, slots, panels, taken):
     hbm = pl.BlockSpec(memory_space=pltpu.HBM)
     return pl.pallas_call(
         swapped_kernel,
         out_shape=[jax.ShapeDtypeStruct(p.shape, p.dtype) for p in panels],
-        in_specs=[pl.BlockSpec(memory_space=pltpu.SMEM)] + [hbm] * 6,
+        in_specs=[pl.BlockSpec(memory_space=pltpu.SMEM)] * 2 + [hbm] * 6,
         out_specs=[hbm] * 3,
         scratch_shapes=[pltpu.VMEM(p.shape, p.dtype) for p in panels] + [pltpu.SemaphoreType.DMA((12,))],
         compiler_params=LARGE,
         cost_estimate=pl.CostEstimate(flops=0, bytes_accessed=11 * 2**20, transcendentals=0),
         name="swapped",
-    )(place, *panels, *taken)
+    )(place, slots, *panels, *taken)
 
 
 def layer_kernel(place, position_ref, *refs):
@@ -199,9 +211,8 @@
         )
     copies.append([pltpu.make_async_copy(down_own, down_ref.at[:2], sems.at[8])])
     copies.append([pltpu.make_async_copy(down_other, down_ref.at[2:], sems.at[9])])
-    for group in copies:
-        for copy in group:
-            copy.start()
+    for copy in copies[0] + copies[1]:
+        copy.start()
 
     for q in range(4):
         panel_ref[q, :, WIDTH:, :] = jnp.zeros((8, LANES - WIDTH, 256), jnp.bfloat16)
@@ -223,6 +234,8 @@
         share = jnp.sum(jnp.where(positions == stored, gates, 0.0), axis=1, keepdims=True) * (1.0 / 65536.0)
         for copy in copies[q]:
             copy.wait()
+        for copy in copies[q + 2]:
+            copy.start()
         for step in range(2):
             at = slice(step * 256, (step + 1) * 256)
             act = jnp.zeros((256, 256), jnp.float32)
@@ -274,34 +287,31 @@
     return out[0], out[1:5], out[5]
 
 
-def after(value, *earlier):
-    return lax.optimization_barrier((value, earlier))[0]
-
-
 def on_device(tokens, routes, gate_fix, position, swap_slot, w_gate, w_up, w_down):
     yh, z, core = (lax.axis_index(a) for a in EXPERT_AXES)
     x, yl = (lax.axis_index(a) for a in DP_AXES)
     own_index = (yh * 8 + z) * 2 + core
     my_y = yh * 2 + yl
-    given_slot = lax.dynamic_index_in_dim(swap_slot, own_index, 0, keepdims=False)
-    place = jnp.stack([x, core, yh * 8 + z, my_y, given_slot]).astype(jnp.int32)
-
-    lower = run_ride(place, tokens, routes, gate_fix)
-    step_rows = run_merge(place, gather_ring(lower, Y))
-
+    place = jnp.stack([x, core, yh * 8 + z, my_y, own_index]).astype(jnp.int32)
     swap_core, swap_y = [(0, 1), (1, 0)], [(0, 1), (1, 0)]
+
     panels = (w_gate.reshape(2, 8, WIDTH, 128), w_up.reshape(2, 8, WIDTH, 128), w_down)
     other = tuple(lax.ppermute(w, "core", swap_core) for w in panels)
     weights = panels + other
-    gate_given, up_given, down_given = run_handed(place, lower, panels)
+
+    lower = run_ride(place, tokens, routes, gate_fix)
+    step_rows = run_merge(place, after(gather_ring(lower, Y), other[0]))
+    (gate_given,) = run_handed(place, swap_slot, panels[:1], lower)
+    from_x = after(gather_ring(step_rows[0], "x"), other[1], gate_given)
     gate_taken = lax.ppermute(after(gate_given, *step_rows), "yh", swap_y)
-    piece0 = lax.all_gather(jnp.stack(gather_ring(step_rows[0], "x")), "z")
-    over_z = gather_z(after(step_rows[1], *other))
+    piece0 = lax.all_gather(jnp.stack(from_x), "z")
+    up_given, down_given = run_handed(place, swap_slot, panels[1:], step_rows[1])
+    over_z = gather_z(step_rows[1], (up_given, down_given))
     up_taken = lax.ppermute(after(up_given, gate_taken, over_z), "yh", swap_y)
     down_taken = lax.ppermute(after(down_given, up_taken), "yh", swap_y)
     pieces1 = gather_ring(over_z, "x")
     out0, out1, counts = run_layer(after(place, up_taken), position.reshape(1, 64), piece0, pieces1, weights)
-    new = run_swapped(place, panels, (gate_taken, up_taken, down_taken))
+    new = run_swapped(place, swap_slot, panels, (gate_taken, up_taken, down_taken))
 
     back0 = lax.psum_scatter(out0, "z", scatter_dimension=0)
     back0 = after(back0, *new)

time: 184 us -> 176 us (0.957)
  waiting for transfers between devices: 77.8 us -> 68.8 us
  Pallas kernels: 23.1 us -> 25.8 us
  local copies, waits for them, and re-layouts: 7.65 us -> 5.79 us
    ppermute x28, waiting for transfers between devices: 40.8 us -> 34.9 us  [send(): lax.ppermute(value, axes, [(i, (i + amount) % count) for i in range(count)])]
    ppermute x3, waiting for transfers between devices: 4.82 us -> 0.01 us  [on_device(): other = tuple((lax.ppermute(w, 'core', swap_core) for w in panels))]
    ppermute x1, starting transfers between devices: 0.27 us -> 3.91 us  [on_device(): up_taken = lax.ppermute(after(up_given, gate_taken, over_z), 'yh', swap_y)]
    ppermute x1, starting transfers between devices: 3.25 us -> 0.68 us  [on_device(): down_taken = lax.ppermute(after(down_given, up_taken), 'yh', swap_y)]
    ppermute x1, waiting for transfers between devices: 16.2 us -> 18.6 us  [on_device(): down_taken = lax.ppermute(after(down_given, up_taken), 'yh', swap_y)]
    pallas_call x1 -> x2, Pallas kernels: 3.53 us -> 5.91 us  [run_handed(): pl.pallas_call(handed_kernel, out_shape=[jax.ShapeDtypeStruct(p.shape[1:]...]
    ppermute x28, starting transfers between devices: 49.1 us -> 46.9 us  [send(): lax.ppermute(value, axes, [(i, (i + amount) % count) for i in range(count)])]
    unnamed x26 -> x32, local copies, waits for them, and re-layouts: 4.77 us -> 4.79 us
  transfers between devices with their start and end apart: 37 -> 37, of which waited for: 20 -> 15; matrix products, arithmetic and copies ran while one was open for 2% -> 3% of each run, Pallas kernels for 5% -> 7%
where the time goes in v3:
time: 176 us; the launch traced here: 174 us
  waiting for transfers between devices  68.8 us (39%)
  starting transfers between devices  52.6 us (30%)
  Pallas kernels  25.8 us (15%)
  between operations  16.1 us (9%)
  local copies, waits for them, and re-layouts  5.79 us (3%)
  other arithmetic  5.28 us (3%)
    ppermute x28, starting transfers between devices, send(): lax.ppermute(value, axes, [(i, (i + amount) % count) for i in range(count)])  46.9 us
    ppermute x28, waiting for transfers between devices, send(): lax.ppermute(value, axes, [(i, (i + amount) % count) for i in range(count)])  34.9 us
    ppermute x1, waiting for transfers between devices, on_device(): down_taken = lax.ppermute(after(down_given, up_taken), 'yh', swap_y)  18.6 us
    ppermute x1, waiting for transfers between devices, on_device(): up_taken = lax.ppermute(after(up_given, gate_taken, over_z), 'yh', swap_y)  15.2 us
    pallas_call x1, Pallas kernels, run_layer(): pl.pallas_call(layer_kernel, out_shape=[jax.ShapeDtypeStruct((8, 4, 2 * G...  13 us
    pallas_call x2, Pallas kernels, run_handed(): pl.pallas_call(handed_kernel, out_shape=[jax.ShapeDtypeStruct(p.shape[1:]...  5.91 us
    pallas_call x1, Pallas kernels, run_swapped(): pl.pallas_call(swapped_kernel, out_shape=[jax.ShapeDtypeStruct(p.shape, p...  5.46 us
    unnamed x32, local copies, waits for them, and re-layouts  4.79 us
  transfers between devices with their start and end apart: 37, of which 15 were waited for; matrix products, arithmetic and copies ran while one was open for 3% of the time, Pallas kernels for 7%

profile of v3, /device:TPU:24, one launch (start us, length us, event | category | flops | bytes accessed | tf_op | source)
XLA Modules:
  0.0 174.4 jit_solution(3465549470217953629)
XLA Ops:
  7.9 0.8 copy-done.4
  8.7 0.7 copy-done.7
  9.4 0.7 copy-done.8
  10.0 0.8 ride.1.refs_0_.refs_1_
  10.9 2.0 %collective-permute-start = (bf16[2,16,512]{2,1,0:T(8,128)(2,1)S(1)}, bf16[2,16,512]{2,1,0:T(8,128)(2,1)S(1)}, u32[]{:S(2)}, u32[]{:S(2)}) collective-permute-start(bf16[2,16,512]{2,1,0:T(8,128)(2,1)S(1)} %ride.1.refs_0_.refs_1_), channel_id=1, source_target_pairs={{0,1},{1,128},{128,129},{129,0},{2,3},{3,130},{130,131},{131,2},{4... | collective-permute-start | bytes 98312 | tf_op jit(solution)/shard_map/ppermute | solution.py:29
  12.9 0.9 collective-permute-start.1
  13.9 1.3 collective-permute-done.refs_1_
  15.2 3.1 %collective-permute-done.1.refs_2_ = bf16[2,16,512]{2,1,0:T(8,128)(2,1)S(1)} collective-permute-done((bf16[2,16,512]{2,1,0:T(8,128)(2,1)S(1)}, bf16[2,16,512]{2,1,0:T(8,128)(2,1)S(1)}, u32[]{:S(2)}, u32[]{:S(2)}) %collective-permute-start.1) | collective-permute-done | bytes 32800 | tf_op jit(solution)/shard_map/ppermute | solution.py:29
  19.5 1.6 collective-permute-start.11
  21.0 2.7 %collective-permute-start.12 = (bf16[32,1024]{1,0:T(8,128)(2,1)S(1)}, bf16[32,1024]{1,0:T(8,128)(2,1)S(1)}, u32[]{:S(2)}, u32[]{:S(2)}) collective-permute-start(bf16[32,1024]{1,0:T(8,128)(2,1)S(1)} %get-tuple-element.48), channel_id=1, source_target_pairs={{0,4},{2,6},{4,0},{6,2},{1,5},{3,7},{5,1},{7,3},{8,12},{10,14},{12... | collective-permute-start | bytes 196616 | tf_op jit(solution)/shard_map/ppermute | solution.py:29
  23.8 1.4 collective-permute-start.13
  25.2 2.8 %handed.3 = bf16[8,448,128]{2,1,0:T(8,128)(2,1)} custom-call(s32[5]{0:T(128)} %copy-done.5, s32[32]{0:T(128)} %slots.5, bf16[2,8,448,128]{3,2,1,0:T(8,128)(2,1)} %bitcast.77, bf16[2,16,512]{2,1,0:T(8,128)(2,1)} %copy-done.3), custom_call_target="tpu_custom_call" | custom-call | bytes 2097152 | tf_op jit(solution)/shard_map/handed/pallas_call | solution.py:150
  28.1 0.7 pad_maximum_fusion
  29.3 1.9 %collective-permute-start.5 = (bf16[32,1024]{1,0:T(8,128)(2,1)S(1)}, bf16[32,1024]{1,0:T(8,128)(2,1)S(1)}, u32[]{:S(2)}, u32[]{:S(2)}) collective-permute-start(bf16[32,1024]{1,0:T(8,128)(2,1)S(1)} %get-tuple-element.38.refs_2_), channel_id=1, source_target_pairs={{0,16},{16,32},{32,48},{48,64},{64,80},{80,96},{96,112},{112,0},{1... | collective-permute-start | bytes 196616 | tf_op jit(solution)/shard_map/ppermute | solution.py:29
  31.2 4.0 %collective-permute-start.6 = (bf16[32,1024]{1,0:T(8,128)(2,1)S(1)}, bf16[32,1024]{1,0:T(8,128)(2,1)S(1)}, u32[]{:S(2)}, u32[]{:S(2)}) collective-permute-start(bf16[32,1024]{1,0:T(8,128)(2,1)S(1)} %get-tuple-element.38.refs_2_), channel_id=1, source_target_pairs={{0,112},{16,0},{32,16},{48,32},{64,48},{80,64},{96,80},{112,96},{1... | collective-permute-start | bytes 196616 | tf_op jit(solution)/shard_map/ppermute | solution.py:29
  35.2 4.5 %collective-permute-start.7 = (bf16[32,1024]{1,0:T(8,128)(2,1)S(1)}, bf16[32,1024]{1,0:T(8,128)(2,1)S(1)}, u32[]{:S(2)}, u32[]{:S(2)}) collective-permute-start(bf16[32,1024]{1,0:T(8,128)(2,1)S(1)} %get-tuple-element.38.refs_2_), channel_id=1, source_target_pairs={{0,64},{16,80},{32,96},{48,112},{64,0},{80,16},{96,32},{112,48},{1... | collective-permute-start | bytes 196616 | tf_op jit(solution)/shard_map/ppermute | solution.py:29
  39.7 3.1 %handed.2 = (bf16[8,448,128]{2,1,0:T(8,128)(2,1)}, bf16[128,3584]{1,0:T(8,128)(2,1)}) custom-call(s32[5]{0:T(128)} %copy-done.5, s32[32]{0:T(128)} %slots.5, bf16[2,8,448,128]{3,2,1,0:T(8,128)(2,1)} %bitcast.81, bf16[2,128,3584]{2,1,0:T(8,128)(2,1)} %refs_2_.1, bf16[32,1024]{1,0:T(8,128)(2,1)} %copy-done), custom_call_target="tpu_custom_call" | custom-call | bytes 4194304 | tf_op jit(solution)/shard_map/handed/pallas_call | solution.py:150
  43.4 0.9 pad_maximum_fusion.1
  44.4 4.1 %collective-permute-start.9 = (bf16[2,32,1024]{2,1,0:T(8,128)(2,1)S(1)}, bf16[2,32,1024]{2,1,0:T(8,128)(2,1)S(1)}, u32[]{:S(2)}, u32[]{:S(2)}) collective-permute-start(bf16[2,32,1024]{2,1,0:T(8,128)(2,1)S(1)} %get-tuple-element.77), channel_id=1, source_target_pairs={{0,96},{16,112},{32,0},{48,16},{64,32},{80,48},{96,64},{112,80},{1... | collective-permute-start | bytes 393224 | tf_op jit(solution)/shard_map/ppermute | solution.py:29
  48.5 8.9 %collective-permute-done.8.refs_2_ = bf16[2,32,1024]{2,1,0:T(8,128)(2,1)S(1)} collective-permute-done((bf16[2,32,1024]{2,1,0:T(8,128)(2,1)S(1)}, bf16[2,32,1024]{2,1,0:T(8,128)(2,1)S(1)}, u32[]{:S(2)}, u32[]{:S(2)}) %collective-permute-start.8) | collective-permute-done | bytes 131104 | tf_op jit(solution)/shard_map/ppermute | solution.py:29
  57.4 0.8 copy-done.1
  58.3 3.9 %collective-permute-start.10 = (bf16[8,448,128]{2,1,0:T(8,128)(2,1)}, bf16[8,448,128]{2,1,0:T(8,128)(2,1)S(1)}, u32[]{:S(2)}, u32[]{:S(2)}) collective-permute-start(bf16[8,448,128]{2,1,0:T(8,128)(2,1)} %get-tuple-element.46), channel_id=1, source_target_pairs={{0,128},{128,0},{1,129},{129,1},{2,130},{130,2},{3,131},{131,3},{4... | collective-permute-start | bytes 2752520 | tf_op jit(solution)/shard_map/ppermute | solution.py:310
  62.5 3.8 %collective-permute-start.16 = (bf16[8,32,1024]{2,1,0:T(8,128)(2,1)S(1)}, bf16[8,32,1024]{2,1,0:T(8,128)(2,1)S(1)}, u32[]{:S(2)}, u32[]{:S(2)}) collective-permute-start(bf16[8,32,1024]{2,1,0:T(8,128)(2,1)S(1)} %join.1.refs_1_), channel_id=1, source_target_pairs={{0,4},{2,6},{4,0},{6,2},{1,5},{3,7},{5,1},{7,3},{8,12},{10,14},{12... | collective-permute-start | bytes 1572872 | tf_op jit(solution)/shard_map/ppermute | solution.py:29
  66.3 15.2 %collective-permute-done.10.refs_4_ = bf16[8,448,128]{2,1,0:T(8,128)(2,1)S(1)} collective-permute-done((bf16[8,448,128]{2,1,0:T(8,128)(2,1)}, bf16[8,448,128]{2,1,0:T(8,128)(2,1)S(1)}, u32[]{:S(2)}, u32[]{:S(2)}) %collective-permute-start.10) | collective-permute-done | bytes 917536 | tf_op jit(solution)/shard_map/ppermute | solution.py:310
  81.6 5.8 %collective-permute-done.16.refs_3_ = bf16[8,32,1024]{2,1,0:T(8,128)(2,1)S(1)} collective-permute-done((bf16[8,32,1024]{2,1,0:T(8,128)(2,1)S(1)}, bf16[8,32,1024]{2,1,0:T(8,128)(2,1)S(1)}, u32[]{:S(2)}, u32[]{:S(2)}) %collective-permute-start.16) | collective-permute-done | bytes 524320 | tf_op jit(solution)/shard_map/ppermute | solution.py:29
  87.4 0.7 copy-done.15
  88.2 13.0 %layer.1 = (bf16[8,4,32,896]{3,2,1,0:T(8,128)(2,1)}, bf16[8,32,896]{2,1,0:T(8,128)(2,1)S(1)}, bf16[8,32,896]{2,1,0:T(8,128)(2,1)S(1)}, bf16[8,32,896]{2,1,0:T(8,...) custom-call(s32[5]{0:T(128)S(1)} %copy-done.6, s32[1,64]{1,0:T(1,128)S(1)} %bitcast.75, ...), custom_call_target="tpu_custom_call" | custom-call | flops 5637144576 | bytes 20971520 | tf_op jit(solution)/shard_map/layer/pallas_call | solution.py:266
  101.9 1.8 %collective-permute-start.23 = (bf16[8,32,896]{2,1,0:T(8,128)(2,1)S(1)}, bf16[8,32,896]{2,1,0:T(8,128)(2,1)S(1)}, u32[]{:S(2)}, u32[]{:S(2)}) collective-permute-start(bf16[8,32,896]{2,1,0:T(8,128)(2,1)S(1)} %get-tuple-element.59), channel_id=1, source_target_pairs={{0,6},{2,0},{4,2},{6,4},{1,7},{3,1},{5,3},{7,5},{8,14},{10,8},{12,... | collective-permute-start | bytes 1376264 | tf_op jit(solution)/shard_map/ppermute | solution.py:29
  103.7 0.8 collective-permute-start.24
  104.6 18.6 %collective-permute-done.19.refs_5_ = bf16[128,3584]{1,0:T(8,128)(2,1)S(1)} collective-permute-done((bf16[128,3584]{1,0:T(8,128)(2,1)}, bf16[128,3584]{1,0:T(8,128)(2,1)S(1)}, u32[]{:S(2)}, u32[]{:S(2)}) %collective-permute-start.19) | collective-permute-done | bytes 917536 | tf_op jit(solution)/shard_map/ppermute | solution.py:311
  123.3 1.0 copy-done.12
  124.3 5.5 %swapped.1 = (bf16[2,8,448,128]{3,2,1,0:T(8,128)(2,1)}, bf16[2,8,448,128]{3,2,1,0:T(8,128)(2,1)}, bf16[2,128,3584]{2,1,0:T(8,128)(2,1)}) custom-call(s32[5]{0:T(128)} %copy-done.5, s32[32]{0:T(128)} %slots.5, bf16[2,8,448,128]{3,2,1,0:T(8,128)(2,1)} %bitcast.79, bf16[2,8,448,128]{3,2,1,0:T(8,128)(2,1)} %bitcast.83, bf16[2,128,3584]{2,1,0:T(8,128)(2,1)} %refs_2_.1, ...), custom_call_target="tpu_custom_call" | custom-call | bytes 11534336 | tf_op jit(solution)/shard_map/swapped/pallas_call | solution.py:182
  129.9 1.3 add_convert_fusion
  131.2 3.6 %collective-permute-start.26 = (bf16[2,32,896]{2,1,0:T(8,128)(2,1)S(1)}, bf16[2,32,896]{2,1,0:T(8,128)(2,1)S(1)}, u32[]{:S(2)}, u32[]{:S(2)}) collective-permute-start(bf16[2,32,896]{2,1,0:T(8,128)(2,1)S(1)} %get-tuple-element.70), channel_id=1, source_target_pairs={{0,96},{16,112},{32,0},{48,16},{64,32},{80,48},{96,64},{112,80},{1... | collective-permute-start | bytes 344072 | tf_op jit(solution)/shard_map/ppermute | solution.py:29
  134.7 3.3 %collective-permute-start.28 = (bf16[32,896]{1,0:T(8,128)(2,1)S(1)}, bf16[32,896]{1,0:T(8,128)(2,1)S(1)}, u32[]{:S(2)}, u32[]{:S(2)}) collective-permute-start(bf16[32,896]{1,0:T(8,128)(2,1)S(1)} %slice_bitcast_fusion), channel_id=1, source_target_pairs={{0,64},{16,80},{32,96},{48,112},{64,0},{80,16},{96,32},{112,48},{1... | collective-permute-start | bytes 172040 | tf_op jit(solution)/shard_map/ppermute | solution.py:29
  138.0 4.9 %collective-permute-done.26 = bf16[2,32,896]{2,1,0:T(8,128)(2,1)S(1)} collective-permute-done((bf16[2,32,896]{2,1,0:T(8,128)(2,1)S(1)}, bf16[2,32,896]{2,1,0:T(8,128)(2,1)S(1)}, u32[]{:S(2)}, u32[]{:S(2)}) %collective-permute-start.26) | collective-permute-done | bytes 114720 | tf_op jit(solution)/shard_map/ppermute | solution.py:29
  143.0 1.4 collective-permute-done.27
  145.0 1.5 collective-permute-start.30
  146.5 0.9 slice_bitcast_fusion.3
  147.4 3.5 %collective-permute-start.20 = (bf16[32,896]{1,0:T(8,128)(2,1)S(1)}, bf16[32,896]{1,0:T(8,128)(2,1)S(1)}, u32[]{:S(2)}, u32[]{:S(2)}) collective-permute-start(bf16[32,896]{1,0:T(8,128)(2,1)S(1)} %get-tuple-element.72), channel_id=1, source_target_pairs={{0,6},{2,0},{4,2},{6,4},{1,7},{3,1},{5,3},{7,5},{8,14},{10,8},{12,... | collective-permute-start | bytes 172040 | tf_op jit(solution)/shard_map/ppermute | solution.py:29
  151.0 0.8 collective-permute-start.22
  151.9 0.8 collective-permute-done.20
  152.7 4.0 %collective-permute-done.21 = bf16[32,896]{1,0:T(8,128)(2,1)S(1)} collective-permute-done((bf16[32,896]{1,0:T(8,128)(2,1)S(1)}, bf16[32,896]{1,0:T(8,128)(2,1)S(1)}, u32[]{:S(2)}, u32[]{:S(2)}) %collective-permute-start.21) | collective-permute-done | bytes 57376 | tf_op jit(solution)/shard_map/ppermute | solution.py:29
  157.0 0.9 fusion.2
  158.0 1.4 collective-permute-start.32
  159.4 1.3 collective-permute-start.33
  162.7 0.9 collective-permute-done.32
  163.5 2.3 %collective-permute-done.31 = bf16[2,16,448]{2,1,0:T(8,128)(2,1)S(1)} collective-permute-done((bf16[2,16,448]{2,1,0:T(8,128)(2,1)S(1)}, bf16[2,16,448]{2,1,0:T(8,128)(2,1)S(1)}, u32[]{:S(2)}, u32[]{:S(2)}) %collective-permute-start.31) | collective-permute-done | bytes 28704 | tf_op jit(solution)/shard_map/ppermute | solution.py:29
  (84 shorter events, 7.7 us)
Async XLA Ops:
  7.2 80.2 %all-gather.3.cloned.1.call-start = ((), (), s32[]{:S(2)}) async-start(), calls=%async_computation.2 | async-start | bytes 2359296 | tf_op jit(solution)/shard_map/all_gather | solution.py:307
  7.2 11.7 %collective-permute-start.3 = (bf16[2,8,448,128]{3,2,1,0:T(8,128)(2,1)}, bf16[2,8,448,128]{3,2,1,0:T(8,128)(2,1)}, u32[]{:S(2)}, u32[]{:S(2)}) collective-permute-start(bf16[2,8,448,128]{3,2,1,0:T(8,128)(2,1)} %bitcast.76), channel_id=1, source_target_pairs={{0,8},{8,0},{1,9},{9,1},{2,10},{10,2},{3,11},{11,3},{4,12},{12,4},... | collective-permute-start | bytes 5505032 | tf_op jit(solution)/shard_map/ppermute | solution.py:299
  7.3 20.7 %collective-permute-start.14 = (bf16[2,8,448,128]{3,2,1,0:T(8,128)(2,1)}, bf16[2,8,448,128]{3,2,1,0:T(8,128)(2,1)}, u32[]{:S(2)}, u32[]{:S(2)}) collective-permute-start(bf16[2,8,448,128]{3,2,1,0:T(8,128)(2,1)} %bitcast.80), channel_id=1, source_target_pairs={{0,8},{8,0},{1,9},{9,1},{2,10},{10,2},{3,11},{11,3},{4,12},{12,4},... | collective-permute-start | bytes 5505032 | tf_op jit(solution)/shard_map/ppermute | solution.py:299
  7.9 17.3 %copy-start.5 = (s32[5]{0:T(128)}, s32[5]{0:T(128)S(1)}, u32[]{:S(2)}) copy-start(s32[5]{0:T(128)S(1)} %stack.59.place) | copy-start | bytes 64
  10.8 14.4 %copy-start.3 = (bf16[2,16,512]{2,1,0:T(8,128)(2,1)}, bf16[2,16,512]{2,1,0:T(8,128)(2,1)S(1)}, u32[]{:S(2)}) copy-start(bf16[2,16,512]{2,1,0:T(8,128)(2,1)S(1)} %ride.1.refs_0_.refs_1_) | copy-start | bytes 98308
  10.9 18.4 %copy-start.10 = (bf16[2,128,3584]{2,1,0:T(8,128)(2,1)S(1)}, bf16[2,128,3584]{2,1,0:T(8,128)(2,1)}, u32[]{:S(2)}) copy-start(bf16[2,128,3584]{2,1,0:T(8,128)(2,1)} %refs_2_.1) | copy-start | bytes 5505028
  10.9 4.3 %collective-permute-start = (bf16[2,16,512]{2,1,0:T(8,128)(2,1)S(1)}, bf16[2,16,512]{2,1,0:T(8,128)(2,1)S(1)}, u32[]{:S(2)}, u32[]{:S(2)}) collective-permute-start(bf16[2,16,512]{2,1,0:T(8,128)(2,1)S(1)} %ride.1.refs_0_.refs_1_), channel_id=1, source_target_pairs={{0,1},{1,128},{128,129},{129,0},{2,3},{3,130},{130,131},{131,2},{4... | collective-permute-start | bytes 98312 | tf_op jit(solution)/shard_map/ppermute | solution.py:29
  12.9 5.4 %collective-permute-start.1 = (bf16[2,16,512]{2,1,0:T(8,128)(2,1)S(1)}, bf16[2,16,512]{2,1,0:T(8,128)(2,1)S(1)}, u32[]{:S(2)}, u32[]{:S(2)}) collective-permute-start(bf16[2,16,512]{2,1,0:T(8,128)(2,1)S(1)} %ride.1.refs_0_.refs_1_), channel_id=1, source_target_pairs={{0,128},{1,129},{128,0},{129,1},{2,130},{3,131},{130,2},{131,3},{4... | collective-permute-start | bytes 98312 | tf_op jit(solution)/shard_map/ppermute | solution.py:29
  13.8 5.1 %collective-permute-start.2 = (bf16[2,16,512]{2,1,0:T(8,128)(2,1)S(1)}, bf16[2,16,512]{2,1,0:T(8,128)(2,1)S(1)}, u32[]{:S(2)}, u32[]{:S(2)}) collective-permute-start(bf16[2,16,512]{2,1,0:T(8,128)(2,1)S(1)} %ride.1.refs_0_.refs_1_), channel_id=1, source_target_pairs={{0,129},{1,0},{128,1},{129,128},{2,131},{3,2},{130,3},{131,130},{4... | collective-permute-start | bytes 98312 | tf_op jit(solution)/shard_map/ppermute | solution.py:29
  19.5 20.3 %copy-start = (bf16[32,1024]{1,0:T(8,128)(2,1)}, bf16[32,1024]{1,0:T(8,128)(2,1)S(1)}, u32[]{:S(2)}) copy-start(bf16[32,1024]{1,0:T(8,128)(2,1)S(1)} %get-tuple-element.38.refs_2_) | copy-start | bytes 196612
  19.5 8.6 %collective-permute-start.11 = (bf16[32,1024]{1,0:T(8,128)(2,1)S(1)}, bf16[32,1024]{1,0:T(8,128)(2,1)S(1)}, u32[]{:S(2)}, u32[]{:S(2)}) collective-permute-start(bf16[32,1024]{1,0:T(8,128)(2,1)S(1)} %get-tuple-element.48), channel_id=1, source_target_pairs={{0,2},{2,4},{4,6},{6,0},{1,3},{3,5},{5,7},{7,1},{8,10},{10,12},{12... | collective-permute-start | bytes 196616 | tf_op jit(solution)/shard_map/ppermute | solution.py:29
  21.0 7.0 %collective-permute-start.12 = (bf16[32,1024]{1,0:T(8,128)(2,1)S(1)}, bf16[32,1024]{1,0:T(8,128)(2,1)S(1)}, u32[]{:S(2)}, u32[]{:S(2)}) collective-permute-start(bf16[32,1024]{1,0:T(8,128)(2,1)S(1)} %get-tuple-element.48), channel_id=1, source_target_pairs={{0,4},{2,6},{4,0},{6,2},{1,5},{3,7},{5,1},{7,3},{8,12},{10,14},{12... | collective-permute-start | bytes 196616 | tf_op jit(solution)/shard_map/ppermute | solution.py:29
  23.8 4.3 %collective-permute-start.13 = (bf16[32,1024]{1,0:T(8,128)(2,1)S(1)}, bf16[32,1024]{1,0:T(8,128)(2,1)S(1)}, u32[]{:S(2)}, u32[]{:S(2)}) collective-permute-start(bf16[32,1024]{1,0:T(8,128)(2,1)S(1)} %get-tuple-element.48), channel_id=1, source_target_pairs={{0,6},{2,0},{4,2},{6,4},{1,7},{3,1},{5,3},{7,5},{8,14},{10,8},{12,... | collective-permute-start | bytes 196616 | tf_op jit(solution)/shard_map/ppermute | solution.py:29
  28.8 117.7 %reduce-scatter.2.cloned.1.call-start = ((), (), s32[]{:S(2)}) async-start(), calls=%async_computation.1 | async-start | bytes 2064384 | tf_op jit(solution)/shard_map/reduce_scatter | solution.py:316
  28.9 59.3 %copy-start.6 = (s32[5]{0:T(128)S(1)}, s32[5]{0:T(128)}, u32[]{:S(2)}) copy-start(s32[5]{0:T(128)} %copy-done.5) | copy-start | bytes 64
  28.9 59.3 %copy-start.9 = (s32[64]{0:T(128)S(1)}, s32[64]{0:T(128)}, u32[]{:S(2)}) copy-start(s32[64]{0:T(128)} %param.11) | copy-start | bytes 772
  28.9 29.4 %collective-permute-start.4 = (bf16[8,448,128]{2,1,0:T(8,128)(2,1)}, bf16[8,448,128]{2,1,0:T(8,128)(2,1)}, u32[]{:S(2)}, u32[]{:S(2)}) collective-permute-start(bf16[8,448,128]{2,1,0:T(8,128)(2,1)} %handed.3), channel_id=1, source_target_pairs={{0,128},{128,0},{1,129},{129,1},{2,130},{130,2},{3,131},{131,3},{4... | collective-permute-start | bytes 2752520 | tf_op jit(solution)/shard_map/ppermute | solution.py:306
  29.3 52.3 %collective-permute-start.18 = (bf16[2,128,3584]{2,1,0:T(8,128)(2,1)S(1)}, bf16[2,128,3584]{2,1,0:T(8,128)(2,1)}, u32[]{:S(2)}, u32[]{:S(2)}) collective-permute-start(bf16[2,128,3584]{2,1,0:T(8,128)(2,1)S(1)} %copy-done.10), channel_id=1, source_target_pairs={{0,8},{8,0},{1,9},{9,1},{2,10},{10,2},{3,11},{11,3},{4,12},{12,4},... | collective-permute-start | bytes 5505032 | tf_op jit(solution)/shard_map/ppermute | solution.py:299
  29.3 13.6 %collective-permute-start.5 = (bf16[32,1024]{1,0:T(8,128)(2,1)S(1)}, bf16[32,1024]{1,0:T(8,128)(2,1)S(1)}, u32[]{:S(2)}, u32[]{:S(2)}) collective-permute-start(bf16[32,1024]{1,0:T(8,128)(2,1)S(1)} %get-tuple-element.38.refs_2_), channel_id=1, source_target_pairs={{0,16},{16,32},{32,48},{48,64},{64,80},{80,96},{96,112},{112,0},{1... | collective-permute-start | bytes 196616 | tf_op jit(solution)/shard_map/ppermute | solution.py:29
  31.2 11.6 %collective-permute-start.6 = (bf16[32,1024]{1,0:T(8,128)(2,1)S(1)}, bf16[32,1024]{1,0:T(8,128)(2,1)S(1)}, u32[]{:S(2)}, u32[]{:S(2)}) collective-permute-start(bf16[32,1024]{1,0:T(8,128)(2,1)S(1)} %get-tuple-element.38.refs_2_), channel_id=1, source_target_pairs={{0,112},{16,0},{32,16},{48,32},{64,48},{80,64},{96,80},{112,96},{1... | collective-permute-start | bytes 196616 | tf_op jit(solution)/shard_map/ppermute | solution.py:29
  35.2 8.2 %collective-permute-start.7 = (bf16[32,1024]{1,0:T(8,128)(2,1)S(1)}, bf16[32,1024]{1,0:T(8,128)(2,1)S(1)}, u32[]{:S(2)}, u32[]{:S(2)}) collective-permute-start(bf16[32,1024]{1,0:T(8,128)(2,1)S(1)} %get-tuple-element.38.refs_2_), channel_id=1, source_target_pairs={{0,64},{16,80},{32,96},{48,112},{64,0},{80,16},{96,32},{112,48},{1... | collective-permute-start | bytes 196616 | tf_op jit(solution)/shard_map/ppermute | solution.py:29
  44.3 13.1 %collective-permute-start.8 = (bf16[2,32,1024]{2,1,0:T(8,128)(2,1)S(1)}, bf16[2,32,1024]{2,1,0:T(8,128)(2,1)S(1)}, u32[]{:S(2)}, u32[]{:S(2)}) collective-permute-start(bf16[2,32,1024]{2,1,0:T(8,128)(2,1)S(1)} %get-tuple-element.78), channel_id=1, source_target_pairs={{0,32},{16,48},{32,64},{48,80},{64,96},{80,112},{96,0},{112,16},{1... | collective-permute-start | bytes 393224 | tf_op jit(solution)/shard_map/ppermute | solution.py:29
  44.4 13.1 %collective-permute-start.9 = (bf16[2,32,1024]{2,1,0:T(8,128)(2,1)S(1)}, bf16[2,32,1024]{2,1,0:T(8,128)(2,1)S(1)}, u32[]{:S(2)}, u32[]{:S(2)}) collective-permute-start(bf16[2,32,1024]{2,1,0:T(8,128)(2,1)S(1)} %get-tuple-element.77), channel_id=1, source_target_pairs={{0,96},{16,112},{32,0},{48,16},{64,32},{80,48},{96,64},{112,80},{1... | collective-permute-start | bytes 393224 | tf_op jit(solution)/shard_map/ppermute | solution.py:29
  58.3 29.1 %copy-start.2 = (bf16[8,32,1024]{2,1,0:T(8,128)(2,1)}, bf16[8,32,1024]{2,1,0:T(8,128)(2,1)S(1)}, u32[]{:S(2)}) copy-start(bf16[8,32,1024]{2,1,0:T(8,128)(2,1)S(1)} %join.1.refs_1_) | copy-start | bytes 1572868
  58.3 23.3 %collective-permute-start.10 = (bf16[8,448,128]{2,1,0:T(8,128)(2,1)}, bf16[8,448,128]{2,1,0:T(8,128)(2,1)S(1)}, u32[]{:S(2)}, u32[]{:S(2)}) collective-permute-start(bf16[8,448,128]{2,1,0:T(8,128)(2,1)} %get-tuple-element.46), channel_id=1, source_target_pairs={{0,128},{128,0},{1,129},{129,1},{2,130},{130,2},{3,131},{131,3},{4... | collective-permute-start | bytes 2752520 | tf_op jit(solution)/shard_map/ppermute | solution.py:310
  62.2 19.4 %collective-permute-start.15 = (bf16[8,32,1024]{2,1,0:T(8,128)(2,1)S(1)}, bf16[8,32,1024]{2,1,0:T(8,128)(2,1)S(1)}, u32[]{:S(2)}, u32[]{:S(2)}) collective-permute-start(bf16[8,32,1024]{2,1,0:T(8,128)(2,1)S(1)} %join.1.refs_1_), channel_id=1, source_target_pairs={{0,2},{2,4},{4,6},{6,0},{1,3},{3,5},{5,7},{7,1},{8,10},{10,12},{12... | collective-permute-start | bytes 1572872 | tf_op jit(solution)/shard_map/ppermute | solution.py:29
  62.5 24.8 %collective-permute-start.16 = (bf16[8,32,1024]{2,1,0:T(8,128)(2,1)S(1)}, bf16[8,32,1024]{2,1,0:T(8,128)(2,1)S(1)}, u32[]{:S(2)}, u32[]{:S(2)}) collective-permute-start(bf16[8,32,1024]{2,1,0:T(8,128)(2,1)S(1)} %join.1.refs_1_), channel_id=1, source_target_pairs={{0,4},{2,6},{4,0},{6,2},{1,5},{3,7},{5,1},{7,3},{8,12},{10,14},{12... | collective-permute-start | bytes 1572872 | tf_op jit(solution)/shard_map/ppermute | solution.py:29
  66.3 21.1 %collective-permute-start.17 = (bf16[8,32,1024]{2,1,0:T(8,128)(2,1)S(1)}, bf16[8,32,1024]{2,1,0:T(8,128)(2,1)}, u32[]{:S(2)}, u32[]{:S(2)}) collective-permute-start(bf16[8,32,1024]{2,1,0:T(8,128)(2,1)S(1)} %join.1.refs_1_), channel_id=1, source_target_pairs={{0,6},{2,0},{4,2},{6,4},{1,7},{3,1},{5,3},{7,5},{8,14},{10,8},{12,... | collective-permute-start | bytes 1572872 | tf_op jit(solution)/shard_map/ppermute | solution.py:29
  81.6 5.8 %copy-start.11 = (bf16[8,448,128]{2,1,0:T(8,128)(2,1)}, bf16[8,448,128]{2,1,0:T(8,128)(2,1)S(1)}, u32[]{:S(2)}) copy-start(bf16[8,448,128]{2,1,0:T(8,128)(2,1)S(1)} %collective-permute-done.10.refs_4_) | copy-start | bytes 2752516
  81.6 5.8 %copy-start.14 = (bf16[8,32,1024]{2,1,0:T(8,128)(2,1)}, bf16[8,32,1024]{2,1,0:T(8,128)(2,1)S(1)}, u32[]{:S(2)}) copy-start(bf16[8,32,1024]{2,1,0:T(8,128)(2,1)S(1)} %collective-permute-done.15.refs_2_) | copy-start | bytes 1572868
  101.2 3.4 %copy-start.13 = (s32[32]{0:T(128)S(1)}, s32[32]{0:T(128)}, u32[]{:S(2)}) copy-start(s32[32]{0:T(128)} %slots.5) | copy-start | bytes 388
  101.2 22.0 %collective-permute-start.19 = (bf16[128,3584]{1,0:T(8,128)(2,1)}, bf16[128,3584]{1,0:T(8,128)(2,1)S(1)}, u32[]{:S(2)}, u32[]{:S(2)}) collective-permute-start(bf16[128,3584]{1,0:T(8,128)(2,1)} %get-tuple-element.53), channel_id=1, source_target_pairs={{0,128},{128,0},{1,129},{129,1},{2,130},{130,2},{3,131},{131,3},{4... | collective-permute-start | bytes 2752520 | tf_op jit(solution)/shard_map/ppermute | solution.py:311
  101.9 28.0 %collective-permute-start.23 = (bf16[8,32,896]{2,1,0:T(8,128)(2,1)S(1)}, bf16[8,32,896]{2,1,0:T(8,128)(2,1)S(1)}, u32[]{:S(2)}, u32[]{:S(2)}) collective-permute-start(bf16[8,32,896]{2,1,0:T(8,128)(2,1)S(1)} %get-tuple-element.59), channel_id=1, source_target_pairs={{0,6},{2,0},{4,2},{6,4},{1,7},{3,1},{5,3},{7,5},{8,14},{10,8},{12,... | collective-permute-start | bytes 1376264 | tf_op jit(solution)/shard_map/ppermute | solution.py:29
  103.7 26.2 %collective-permute-start.24 = (bf16[8,32,896]{2,1,0:T(8,128)(2,1)S(1)}, bf16[8,32,896]{2,1,0:T(8,128)(2,1)S(1)}, u32[]{:S(2)}, u32[]{:S(2)}) collective-permute-start(bf16[8,32,896]{2,1,0:T(8,128)(2,1)S(1)} %get-tuple-element.60), channel_id=1, source_target_pairs={{0,4},{2,6},{4,0},{6,2},{1,5},{3,7},{5,1},{7,3},{8,12},{10,14},{12... | collective-permute-start | bytes 1376264 | tf_op jit(solution)/shard_map/ppermute | solution.py:29
  104.4 25.4 %collective-permute-start.25 = (bf16[8,32,896]{2,1,0:T(8,128)(2,1)S(1)}, bf16[8,32,896]{2,1,0:T(8,128)(2,1)}, u32[]{:S(2)}, u32[]{:S(2)}) collective-permute-start(bf16[8,32,896]{2,1,0:T(8,128)(2,1)S(1)} %get-tuple-element.61), channel_id=1, source_target_pairs={{0,2},{2,4},{4,6},{6,0},{1,3},{3,5},{5,7},{7,1},{8,10},{10,12},{12... | collective-permute-start | bytes 1376264 | tf_op jit(solution)/shard_map/ppermute | solution.py:29
  123.3 1.0 copy-start.12
  129.7 31.6 %collective-permute-start.34 = (f32[64]{0:T(128)S(1)}, f32[64]{0:T(128)S(1)}, u32[]{:S(2)}, u32[]{:S(2)}) collective-permute-start(f32[64]{0:T(128)S(1)} %slice_bitcast_fusion.4), channel_id=1, source_target_pairs={{0,8},{8,0},{1,9},{9,1},{2,10},{10,2},{3,11},{11,3},{4,12},{12,4},... | collective-permute-start | bytes 776 | tf_op jit(solution)/shard_map/ppermute | solution.py:325
  131.2 11.8 %collective-permute-start.26 = (bf16[2,32,896]{2,1,0:T(8,128)(2,1)S(1)}, bf16[2,32,896]{2,1,0:T(8,128)(2,1)S(1)}, u32[]{:S(2)}, u32[]{:S(2)}) collective-permute-start(bf16[2,32,896]{2,1,0:T(8,128)(2,1)S(1)} %get-tuple-element.70), channel_id=1, source_target_pairs={{0,96},{16,112},{32,0},{48,16},{64,32},{80,48},{96,64},{112,80},{1... | collective-permute-start | bytes 344072 | tf_op jit(solution)/shard_map/ppermute | solution.py:29
  134.7 9.6 %collective-permute-start.27 = (bf16[2,32,896]{2,1,0:T(8,128)(2,1)S(1)}, bf16[2,32,896]{2,1,0:T(8,128)(2,1)S(1)}, u32[]{:S(2)}, u32[]{:S(2)}) collective-permute-start(bf16[2,32,896]{2,1,0:T(8,128)(2,1)S(1)} %get-tuple-element.71), channel_id=1, source_target_pairs={{0,32},{16,48},{32,64},{48,80},{64,96},{80,112},{96,0},{112,16},{1... | collective-permute-start | bytes 344072 | tf_op jit(solution)/shard_map/ppermute | solution.py:29
  134.7 16.2 %collective-permute-start.28 = (bf16[32,896]{1,0:T(8,128)(2,1)S(1)}, bf16[32,896]{1,0:T(8,128)(2,1)S(1)}, u32[]{:S(2)}, u32[]{:S(2)}) collective-permute-start(bf16[32,896]{1,0:T(8,128)(2,1)S(1)} %slice_bitcast_fusion), channel_id=1, source_target_pairs={{0,64},{16,80},{32,96},{48,112},{64,0},{80,16},{96,32},{112,48},{1... | collective-permute-start | bytes 172040 | tf_op jit(solution)/shard_map/ppermute | solution.py:29
  144.4 6.6 %collective-permute-start.29 = (bf16[32,896]{1,0:T(8,128)(2,1)S(1)}, bf16[32,896]{1,0:T(8,128)(2,1)S(1)}, u32[]{:S(2)}, u32[]{:S(2)}) collective-permute-start(bf16[32,896]{1,0:T(8,128)(2,1)S(1)} %get-tuple-element.68), channel_id=1, source_target_pairs={{0,112},{16,0},{32,16},{48,32},{64,48},{80,64},{96,80},{112,96},{1... | collective-permute-start | bytes 172040 | tf_op jit(solution)/shard_map/ppermute | solution.py:29
  145.0 6.9 %collective-permute-start.30 = (bf16[32,896]{1,0:T(8,128)(2,1)S(1)}, bf16[32,896]{1,0:T(8,128)(2,1)S(1)}, u32[]{:S(2)}, u32[]{:S(2)}) collective-permute-start(bf16[32,896]{1,0:T(8,128)(2,1)S(1)} %get-tuple-element.69), channel_id=1, source_target_pairs={{0,16},{16,32},{32,48},{48,64},{64,80},{80,96},{96,112},{112,0},{1... | collective-permute-start | bytes 172040 | tf_op jit(solution)/shard_map/ppermute | solution.py:29
  147.4 5.3 %collective-permute-start.20 = (bf16[32,896]{1,0:T(8,128)(2,1)S(1)}, bf16[32,896]{1,0:T(8,128)(2,1)S(1)}, u32[]{:S(2)}, u32[]{:S(2)}) collective-permute-start(bf16[32,896]{1,0:T(8,128)(2,1)S(1)} %get-tuple-element.72), channel_id=1, source_target_pairs={{0,6},{2,0},{4,2},{6,4},{1,7},{3,1},{5,3},{7,5},{8,14},{10,8},{12,... | collective-permute-start | bytes 172040 | tf_op jit(solution)/shard_map/ppermute | solution.py:29
  150.9 5.8 %collective-permute-start.21 = (bf16[32,896]{1,0:T(8,128)(2,1)S(1)}, bf16[32,896]{1,0:T(8,128)(2,1)S(1)}, u32[]{:S(2)}, u32[]{:S(2)}) collective-permute-start(bf16[32,896]{1,0:T(8,128)(2,1)S(1)} %get-tuple-element.74), channel_id=1, source_target_pairs={{0,4},{2,6},{4,0},{6,2},{1,5},{3,7},{5,1},{7,3},{8,12},{10,14},{12... | collective-permute-start | bytes 172040 | tf_op jit(solution)/shard_map/ppermute | solution.py:29
  151.0 6.0 %collective-permute-start.22 = (bf16[32,896]{1,0:T(8,128)(2,1)S(1)}, bf16[32,896]{1,0:T(8,128)(2,1)S(1)}, u32[]{:S(2)}, u32[]{:S(2)}) collective-permute-start(bf16[32,896]{1,0:T(8,128)(2,1)S(1)} %get-tuple-element.73), channel_id=1, source_target_pairs={{0,2},{2,4},{4,6},{6,0},{1,3},{3,5},{5,7},{7,1},{8,10},{10,12},{12... | collective-permute-start | bytes 172040 | tf_op jit(solution)/shard_map/ppermute | solution.py:29
  158.0 5.5 %collective-permute-start.32 = (bf16[2,16,448]{2,1,0:T(8,128)(2,1)S(1)}, bf16[2,16,448]{2,1,0:T(8,128)(2,1)S(1)}, u32[]{:S(2)}, u32[]{:S(2)}) collective-permute-start(bf16[2,16,448]{2,1,0:T(8,128)(2,1)S(1)} %get-tuple-element.75), channel_id=1, source_target_pairs={{0,128},{1,129},{128,0},{129,1},{2,130},{3,131},{130,2},{131,3},{4... | collective-permute-start | bytes 86024 | tf_op jit(solution)/shard_map/ppermute | solution.py:29
  159.4 4.2 %collective-permute-start.33 = (bf16[2,16,448]{2,1,0:T(8,128)(2,1)S(1)}, bf16[2,16,448]{2,1,0:T(8,128)(2,1)S(1)}, u32[]{:S(2)}, u32[]{:S(2)}) collective-permute-start(bf16[2,16,448]{2,1,0:T(8,128)(2,1)S(1)} %get-tuple-element.76), channel_id=1, source_target_pairs={{0,1},{1,128},{128,129},{129,0},{2,3},{3,130},{130,131},{131,2},{4... | collective-permute-start | bytes 86024 | tf_op jit(solution)/shard_map/ppermute | solution.py:29
  160.7 5.1 %collective-permute-start.31 = (bf16[2,16,448]{2,1,0:T(8,128)(2,1)S(1)}, bf16[2,16,448]{2,1,0:T(8,128)(2,1)S(1)}, u32[]{:S(2)}, u32[]{:S(2)}) collective-permute-start(bf16[2,16,448]{2,1,0:T(8,128)(2,1)S(1)} %get-tuple-element.63), channel_id=1, source_target_pairs={{0,129},{1,0},{128,1},{129,128},{2,131},{3,2},{130,3},{131,130},{4... | collective-permute-start | bytes 86024 | tf_op jit(solution)/shard_map/ppermute | solution.py:29
  (5 other events, 3.8 us)
Sparse Core Ops, SparseCore 0:
  28.9 47.5 all-gather.2
  101.3 41.5 reduce-scatter.1

commit v4 on v3

--- a/solution.py
+++ b/solution.py
@@ -45,12 +45,16 @@
     return total([pieces[0]] + [send(piece, axes, -k) for k, piece in enumerate(pieces) if k])
 
 
-def gather_z(value, beside):
+def gather_zx(value, beside):
     first = [send(value, "z", 1), send(value, "z", -1), send(value, "z", 4)]
     back, ahead, far = after(first, *beside)
     back2 = send(jnp.stack([value, back]), "z", 2)
     ahead2 = send(jnp.stack([value, ahead]), "z", -2)
-    return run_join([value[None], back[None], back2, far[None], ahead2, ahead[None]])
+    early = run_join([value[None], back[None], ahead[None], far[None]])
+    before, behind = send(early, "x", 1), send(early, "x", -1)
+    late = after(run_join([back2, ahead2]), before, behind)
+    both = run_join([early, late])
+    return both, ((both,), (before, send(late, "x", 1)), (send(both, "x", 2),), (behind, send(late, "x", -1)))
 
 
 def run_join(parts):
@@ -74,11 +78,11 @@
 
 
 def reduce_z(pieces):
-    back2 = send(pieces[2:4], "z", -2)
-    ahead2 = send(pieces[5:7], "z", 2)
-    far = send(pieces[4], "z", -4)
+    back2 = send(pieces[4:6], "z", -2)
+    ahead2 = send(pieces[6:8], "z", 2)
+    far = send(pieces[3], "z", -4)
     back = send(total([pieces[1], back2[1]]), "z", -1)
-    ahead = send(total([pieces[7], ahead2[1]]), "z", 1)
+    ahead = send(total([pieces[2], ahead2[1]]), "z", 1)
     return total([pieces[0], back2[0], ahead2[0], far, back, ahead])
 
 
@@ -192,10 +196,10 @@
 
 
 def layer_kernel(place, position_ref, *refs):
-    piece0, pieces1 = refs[0], refs[1:5]
-    gate_own, up_own, down_own, gate_other, up_other, down_other = refs[5:11]
-    out0, outs1, count_ref = refs[11], refs[12:16], refs[16]
-    rows_ref, panel_ref, down_ref, hidden_ref, result_ref, sems = refs[17:]
+    piece0, pieces1 = refs[0], ((refs[1],), refs[2:4], (refs[4],), refs[5:7])
+    gate_own, up_own, down_own, gate_other, up_other, down_other = refs[7:13]
+    out0, outs1, count_ref = refs[13], refs[14:18], refs[18]
+    rows_ref, gate_ref, up_ref, down_ref, hidden_ref, result_ref, sems = refs[19:]
     my_x, my_core, chip = place[0], place[1], place[2]
     span = 2 * GROUP
 
@@ -205,8 +209,8 @@
     ):
         copies.append(
             [
-                pltpu.make_async_copy(gate_w.at[slot], panel_ref.at[q, :, :WIDTH, :128], sems.at[2 * q]),
-                pltpu.make_async_copy(up_w.at[slot], panel_ref.at[q, :, :WIDTH, 128:], sems.at[2 * q + 1]),
+                pltpu.make_async_copy(gate_w.at[slot], gate_ref.at[q, :, :WIDTH], sems.at[2 * q]),
+                pltpu.make_async_copy(up_w.at[slot], up_ref.at[q, :, :WIDTH], sems.at[2 * q + 1]),
             ]
         )
     copies.append([pltpu.make_async_copy(down_own, down_ref.at[:2], sems.at[8])])
@@ -215,13 +219,15 @@
         copy.start()
 
     for q in range(4):
-        panel_ref[q, :, WIDTH:, :] = jnp.zeros((8, LANES - WIDTH, 256), jnp.bfloat16)
+        gate_ref[q, :, WIDTH:, :] = jnp.zeros((8, LANES - WIDTH, 128), jnp.bfloat16)
+        up_ref[q, :, WIDTH:, :] = jnp.zeros((8, LANES - WIDTH, 128), jnp.bfloat16)
     for xr in range(4):
         x_at = lax.rem(my_x - xr + 4, 4)
         lanes = pl.ds(pl.multiple_of(x_at * 2 * LANES, 2 * LANES), 2 * LANES)
         for zr in range(8):
             rows_ref[zr * span : (zr + 1) * span, lanes] = piece0[zr, xr]
-            rows_ref[(8 + zr) * span : (9 + zr) * span, lanes] = pieces1[xr][zr]
+            part = pieces1[xr][zr // pieces1[xr][0].shape[0]]
+            rows_ref[(8 + zr) * span : (9 + zr) * span, lanes] = part[zr % part.shape[0]]
 
     gates = rows_ref[:, WIDTH:LANES].astype(jnp.float32) * 256.0
     gates = gates + rows_ref[:, LANES + WIDTH : 2 * LANES].astype(jnp.float32)
@@ -242,7 +248,7 @@
             for block in range(8):
                 act = act + jnp.dot(
                     rows_ref[at, block * LANES : (block + 1) * LANES],
-                    panel_ref[q, block],
+                    jnp.concatenate([gate_ref[q, block], up_ref[q, block]], axis=1),
                     preferred_element_type=jnp.float32,
                 )
             value = jax.nn.silu(act[:, :128]) * act[:, 128:] * share[at]
@@ -269,12 +275,13 @@
         + [jax.ShapeDtypeStruct((8, 2 * GROUP, PAIR), jnp.bfloat16)] * 4
         + [jax.ShapeDtypeStruct((8, 64), jnp.float32)],
         in_specs=[pl.BlockSpec(memory_space=pltpu.SMEM)]
-        + [vmem] * 6
+        + [vmem] * 8
         + [pl.BlockSpec(memory_space=pltpu.HBM)] * 6,
         out_specs=[vmem] * 6,
         scratch_shapes=[
             pltpu.VMEM((512, 8 * LANES), jnp.bfloat16),
-            pltpu.VMEM((4, 8, LANES, 256), jnp.bfloat16),
+            pltpu.VMEM((4, 8, LANES, 128), jnp.bfloat16),
+            pltpu.VMEM((4, 8, LANES, 128), jnp.bfloat16),
             pltpu.VMEM((4, 128, 3584), jnp.bfloat16),
             pltpu.VMEM((512, 512), jnp.bfloat16),
             pltpu.VMEM((4, 512, PAIR), jnp.bfloat16),
@@ -283,7 +290,7 @@
         compiler_params=pltpu.CompilerParams(vmem_limit_bytes=52 * 2**20),
         cost_estimate=pl.CostEstimate(flops=2 * 512 * 3584 * 1536, bytes_accessed=20 * 2**20, transcendentals=0),
         name="layer",
-    )(place, position, piece0, *pieces1, *weights)
+    )(place, position, piece0, *sum(pieces1, ()), *weights)
     return out[0], out[1:5], out[5]
 
 
@@ -306,10 +313,9 @@
     gate_taken = lax.ppermute(after(gate_given, *step_rows), "yh", swap_y)
     piece0 = lax.all_gather(jnp.stack(from_x), "z")
     up_given, down_given = run_handed(place, swap_slot, panels[1:], step_rows[1])
-    over_z = gather_z(step_rows[1], (up_given, down_given))
+    over_z, pieces1 = gather_zx(step_rows[1], (up_given, down_given, other[2]))
     up_taken = lax.ppermute(after(up_given, gate_taken, over_z), "yh", swap_y)
     down_taken = lax.ppermute(after(down_given, up_taken), "yh", swap_y)
-    pieces1 = gather_ring(over_z, "x")
     out0, out1, counts = run_layer(after(place, up_taken), position.reshape(1, 64), piece0, pieces1, weights)
     new = run_swapped(place, swap_slot, panels, (gate_taken, up_taken, down_taken))
 

time: 176 us -> 170 us (0.966)
  waiting for transfers between devices: 68.8 us -> 62.9 us
  starting transfers between devices: 52.6 us -> 55 us
    ppermute x28 -> x30, waiting for transfers between devices: 34.9 us -> 32.2 us  [send(): lax.ppermute(value, axes, [(i, (i + amount) % count) for i in range(count)])]
    ppermute x1, starting transfers between devices: 0.68 us -> 3.34 us  [on_device(): down_taken = lax.ppermute(after(down_given, up_taken), 'yh', swap_y)]
    ppermute x1, waiting for transfers between devices: 15.2 us -> 12.8 us  [on_device(): up_taken = lax.ppermute(after(up_given, gate_taken, over_z), 'yh', swap_y)]
    ppermute x28 -> x30, starting transfers between devices: 46.9 us -> 47 us  [send(): lax.ppermute(value, axes, [(i, (i + amount) % count) for i in range(count)])]
  transfers between devices with their start and end apart: 37 -> 39, of which waited for: 15 -> 16; matrix products, arithmetic and copies ran while one was open for 3% -> 2% of each run, Pallas kernels for 7% -> 8%
where the time goes in v4:
time: 170 us
  waiting for transfers between devices  62.9 us (37%)
  starting transfers between devices  55 us (32%)
  Pallas kernels  26.4 us (16%)
  between operations  16.2 us (10%)
  local copies, waits for them, and re-layouts  5.05 us (3%)
  other arithmetic  4.23 us (2%)
    ppermute x30, starting transfers between devices, send(): lax.ppermute(value, axes, [(i, (i + amount) % count) for i in range(count)])  47 us
    ppermute x30, waiting for transfers between devices, send(): lax.ppermute(value, axes, [(i, (i + amount) % count) for i in range(count)])  32.2 us
    ppermute x1, waiting for transfers between devices, on_device(): down_taken = lax.ppermute(after(down_given, up_taken), 'yh', swap_y)  17.8 us
    pallas_call x1, Pallas kernels, run_layer(): pl.pallas_call(layer_kernel, out_shape=[jax.ShapeDtypeStruct((8, 4, 2 * G...  13.5 us
    ppermute x1, waiting for transfers between devices, on_device(): up_taken = lax.ppermute(after(up_given, gate_taken, over_z), 'yh', swap_y)  12.8 us
    pallas_call x2, Pallas kernels, run_handed(): pl.pallas_call(handed_kernel, out_shape=[jax.ShapeDtypeStruct(p.shape[1:]...  5.91 us
    pallas_call x1, Pallas kernels, run_swapped(): pl.pallas_call(swapped_kernel, out_shape=[jax.ShapeDtypeStruct(p.shape, p...  5.56 us
    unnamed x32, local copies, waits for them, and re-layouts  4.04 us
  transfers between devices with their start and end apart: 39, of which 16 were waited for; matrix products, arithmetic and copies ran while one was open for 2% of the time, Pallas kernels for 8%

profile of v4, /device:TPU:24, one launch (start us, length us, event | category | flops | bytes accessed | tf_op | source)
XLA Modules:
  0.0 169.8 jit_solution(14629619042382649479)
XLA Ops:
  7.9 0.8 copy-done.4
  10.0 0.8 ride.1.refs_0_.refs_1_
  10.9 2.0 %collective-permute-start = (bf16[2,16,512]{2,1,0:T(8,128)(2,1)S(1)}, bf16[2,16,512]{2,1,0:T(8,128)(2,1)S(1)}, u32[]{:S(2)}, u32[]{:S(2)}) collective-permute-start(bf16[2,16,512]{2,1,0:T(8,128)(2,1)S(1)} %ride.1.refs_0_.refs_1_), channel_id=1, source_target_pairs={{0,1},{1,128},{128,129},{129,0},{2,3},{3,130},{130,131},{131,2},{4... | collective-permute-start | bytes 98312 | tf_op jit(solution)/shard_map/ppermute | solution.py:29
  12.9 0.9 collective-permute-start.1
  13.9 1.3 collective-permute-done.refs_1_
  15.2 3.1 %collective-permute-done.1.refs_2_ = bf16[2,16,512]{2,1,0:T(8,128)(2,1)S(1)} collective-permute-done((bf16[2,16,512]{2,1,0:T(8,128)(2,1)S(1)}, bf16[2,16,512]{2,1,0:T(8,128)(2,1)S(1)}, u32[]{:S(2)}, u32[]{:S(2)}) %collective-permute-start.1) | collective-permute-done | bytes 32800 | tf_op jit(solution)/shard_map/ppermute | solution.py:29
  19.5 1.6 collective-permute-start.14
  21.0 2.7 %collective-permute-start.15 = (bf16[32,1024]{1,0:T(8,128)(2,1)S(1)}, bf16[32,1024]{1,0:T(8,128)(2,1)S(1)}, u32[]{:S(2)}, u32[]{:S(2)}) collective-permute-start(bf16[32,1024]{1,0:T(8,128)(2,1)S(1)} %get-tuple-element.50), channel_id=1, source_target_pairs={{0,4},{2,6},{4,0},{6,2},{1,5},{3,7},{5,1},{7,3},{8,12},{10,14},{12... | collective-permute-start | bytes 196616 | tf_op jit(solution)/shard_map/ppermute | solution.py:29
  23.8 1.4 collective-permute-start.16
  25.2 2.8 %handed.3 = bf16[8,448,128]{2,1,0:T(8,128)(2,1)} custom-call(s32[5]{0:T(128)} %copy-done.5, s32[32]{0:T(128)} %slots.5, bf16[2,8,448,128]{3,2,1,0:T(8,128)(2,1)} %bitcast.77, bf16[2,16,512]{2,1,0:T(8,128)(2,1)} %copy-done.3), custom_call_target="tpu_custom_call" | custom-call | bytes 2097152 | tf_op jit(solution)/shard_map/handed/pallas_call | solution.py:154
  29.4 1.9 %collective-permute-start.5 = (bf16[32,1024]{1,0:T(8,128)(2,1)S(1)}, bf16[32,1024]{1,0:T(8,128)(2,1)S(1)}, u32[]{:S(2)}, u32[]{:S(2)}) collective-permute-start(bf16[32,1024]{1,0:T(8,128)(2,1)S(1)} %get-tuple-element.39.refs_2_), channel_id=1, source_target_pairs={{0,16},{16,32},{32,48},{48,64},{64,80},{80,96},{96,112},{112,0},{1... | collective-permute-start | bytes 196616 | tf_op jit(solution)/shard_map/ppermute | solution.py:29
  31.3 3.9 %collective-permute-start.6 = (bf16[32,1024]{1,0:T(8,128)(2,1)S(1)}, bf16[32,1024]{1,0:T(8,128)(2,1)S(1)}, u32[]{:S(2)}, u32[]{:S(2)}) collective-permute-start(bf16[32,1024]{1,0:T(8,128)(2,1)S(1)} %get-tuple-element.39.refs_2_), channel_id=1, source_target_pairs={{0,112},{16,0},{32,16},{48,32},{64,48},{80,64},{96,80},{112,96},{1... | collective-permute-start | bytes 196616 | tf_op jit(solution)/shard_map/ppermute | solution.py:29
  35.2 4.6 %collective-permute-start.7 = (bf16[32,1024]{1,0:T(8,128)(2,1)S(1)}, bf16[32,1024]{1,0:T(8,128)(2,1)S(1)}, u32[]{:S(2)}, u32[]{:S(2)}) collective-permute-start(bf16[32,1024]{1,0:T(8,128)(2,1)S(1)} %get-tuple-element.39.refs_2_), channel_id=1, source_target_pairs={{0,64},{16,80},{32,96},{48,112},{64,0},{80,16},{96,32},{112,48},{1... | collective-permute-start | bytes 196616 | tf_op jit(solution)/shard_map/ppermute | solution.py:29
  39.8 3.1 %handed.2 = (bf16[8,448,128]{2,1,0:T(8,128)(2,1)}, bf16[128,3584]{1,0:T(8,128)(2,1)}) custom-call(s32[5]{0:T(128)} %copy-done.5, s32[32]{0:T(128)} %slots.5, bf16[2,8,448,128]{3,2,1,0:T(8,128)(2,1)} %bitcast.81, bf16[2,128,3584]{2,1,0:T(8,128)(2,1)} %refs_2_.1, bf16[32,1024]{1,0:T(8,128)(2,1)} %copy-done), custom_call_target="tpu_custom_call" | custom-call | bytes 4194304 | tf_op jit(solution)/shard_map/handed/pallas_call | solution.py:154
  43.0 1.1 collective-permute-done.7
  44.1 0.8 copy-done.1
  45.6 2.6 %collective-permute-start.12 = (bf16[4,32,1024]{2,1,0:T(8,128)(2,1)S(1)}, bf16[4,32,1024]{2,1,0:T(8,128)(2,1)S(1)}, u32[]{:S(2)}, u32[]{:S(2)}) collective-permute-start(bf16[4,32,1024]{2,1,0:T(8,128)(2,1)S(1)} %join.3.refs_0_), channel_id=1, source_target_pairs={{0,6},{2,0},{4,2},{6,4},{1,7},{3,1},{5,3},{7,5},{8,14},{10,8},{12,... | collective-permute-start | bytes 786440 | tf_op jit(solution)/shard_map/ppermute | solution.py:29
  48.3 0.9 pad_maximum_fusion.1
  49.1 1.9 %collective-permute-start.10 = (bf16[2,32,1024]{2,1,0:T(8,128)(2,1)S(1)}, bf16[2,32,1024]{2,1,0:T(8,128)(2,1)S(1)}, u32[]{:S(2)}, u32[]{:S(2)}) collective-permute-start(bf16[2,32,1024]{2,1,0:T(8,128)(2,1)S(1)} %get-tuple-element.79), channel_id=1, source_target_pairs={{0,96},{16,112},{32,0},{48,16},{64,32},{80,48},{96,64},{112,80},{1... | collective-permute-start | bytes 393224 | tf_op jit(solution)/shard_map/ppermute | solution.py:29
  51.0 1.2 collective-permute-start.9
  52.1 7.3 %collective-permute-done.10.refs_1_ = bf16[2,32,1024]{2,1,0:T(8,128)(2,1)S(1)} collective-permute-done((bf16[2,32,1024]{2,1,0:T(8,128)(2,1)S(1)}, bf16[2,32,1024]{2,1,0:T(8,128)(2,1)S(1)}, u32[]{:S(2)}, u32[]{:S(2)}) %collective-permute-start.10) | collective-permute-done | bytes 131104 | tf_op jit(solution)/shard_map/ppermute | solution.py:29
  59.5 3.5 %collective-permute-done.9.refs_0_ = bf16[2,32,1024]{2,1,0:T(8,128)(2,1)S(1)} collective-permute-done((bf16[2,32,1024]{2,1,0:T(8,128)(2,1)S(1)}, bf16[2,32,1024]{2,1,0:T(8,128)(2,1)S(1)}, u32[]{:S(2)}, u32[]{:S(2)}) %collective-permute-start.9) | collective-permute-done | bytes 131104 | tf_op jit(solution)/shard_map/ppermute | solution.py:29
  63.1 3.2 %collective-permute-start.13 = (bf16[8,448,128]{2,1,0:T(8,128)(2,1)S(1)}, bf16[8,448,128]{2,1,0:T(8,128)(2,1)S(1)}, u32[]{:S(2)}, u32[]{:S(2)}) collective-permute-start(bf16[8,448,128]{2,1,0:T(8,128)(2,1)S(1)} %copy-done.14), channel_id=1, source_target_pairs={{0,128},{128,0},{1,129},{129,1},{2,130},{130,2},{3,131},{131,3},{4... | collective-permute-start | bytes 2752520 | tf_op jit(solution)/shard_map/ppermute | solution.py:317
  66.3 1.1 collective-permute-start.19
  67.4 1.3 collective-permute-start.18
  68.7 1.9 %collective-permute-start.20 = (bf16[4,32,1024]{2,1,0:T(8,128)(2,1)S(1)}, bf16[4,32,1024]{2,1,0:T(8,128)(2,1)S(1)}, u32[]{:S(2)}, u32[]{:S(2)}) collective-permute-start(bf16[4,32,1024]{2,1,0:T(8,128)(2,1)S(1)} %join.4.refs_1_), channel_id=1, source_target_pairs={{0,6},{2,0},{4,2},{6,4},{1,7},{3,1},{5,3},{7,5},{8,14},{10,8},{12,... | collective-permute-start | bytes 786440 | tf_op jit(solution)/shard_map/ppermute | solution.py:29
  70.6 12.8 %collective-permute-done.13.refs_4_ = bf16[8,448,128]{2,1,0:T(8,128)(2,1)S(1)} collective-permute-done((bf16[8,448,128]{2,1,0:T(8,128)(2,1)S(1)}, bf16[8,448,128]{2,1,0:T(8,128)(2,1)S(1)}, u32[]{:S(2)}, u32[]{:S(2)}) %collective-permute-start.13) | collective-permute-done | bytes 917536 | tf_op jit(solution)/shard_map/ppermute | solution.py:317
  83.6 13.5 %layer.1 = (bf16[8,4,32,896]{3,2,1,0:T(8,128)(2,1)}, bf16[8,32,896]{2,1,0:T(8,128)(2,1)S(1)}, bf16[8,32,896]{2,1,0:T(8,128)(2,1)S(1)}, bf16[8,32,896]{2,1,0:T(8,...) custom-call(s32[5]{0:T(128)S(1)} %copy-done.6, s32[1,64]{1,0:T(1,128)S(1)} %bitcast.75, ...), custom_call_target="tpu_custom_call" | custom-call | flops 5637144576 | bytes 20971520 | tf_op jit(solution)/shard_map/layer/pallas_call | solution.py:272
  97.2 3.3 %collective-permute-start.21 = (bf16[128,3584]{1,0:T(8,128)(2,1)}, bf16[128,3584]{1,0:T(8,128)(2,1)S(1)}, u32[]{:S(2)}, u32[]{:S(2)}) collective-permute-start(bf16[128,3584]{1,0:T(8,128)(2,1)} %get-tuple-element.55), channel_id=1, source_target_pairs={{0,128},{128,0},{1,129},{129,1},{2,130},{130,2},{3,131},{131,3},{4... | collective-permute-start | bytes 2752520 | tf_op jit(solution)/shard_map/ppermute | solution.py:318
  100.5 1.9 %collective-permute-start.25 = (bf16[8,32,896]{2,1,0:T(8,128)(2,1)S(1)}, bf16[8,32,896]{2,1,0:T(8,128)(2,1)S(1)}, u32[]{:S(2)}, u32[]{:S(2)}) collective-permute-start(bf16[8,32,896]{2,1,0:T(8,128)(2,1)S(1)} %get-tuple-element.61), channel_id=1, source_target_pairs={{0,6},{2,0},{4,2},{6,4},{1,7},{3,1},{5,3},{7,5},{8,14},{10,8},{12,... | collective-permute-start | bytes 1376264 | tf_op jit(solution)/shard_map/ppermute | solution.py:29
  102.4 0.9 collective-permute-start.27
  103.4 17.8 %collective-permute-done.21.refs_5_ = bf16[128,3584]{1,0:T(8,128)(2,1)S(1)} collective-permute-done((bf16[128,3584]{1,0:T(8,128)(2,1)}, bf16[128,3584]{1,0:T(8,128)(2,1)S(1)}, u32[]{:S(2)}, u32[]{:S(2)}) %collective-permute-start.21) | collective-permute-done | bytes 917536 | tf_op jit(solution)/shard_map/ppermute | solution.py:318
  121.2 1.0 copy-done.12
  122.2 5.6 %swapped.1 = (bf16[2,8,448,128]{3,2,1,0:T(8,128)(2,1)}, bf16[2,8,448,128]{3,2,1,0:T(8,128)(2,1)}, bf16[2,128,3584]{2,1,0:T(8,128)(2,1)}) custom-call(s32[5]{0:T(128)} %copy-done.5, s32[32]{0:T(128)} %slots.5, bf16[2,8,448,128]{3,2,1,0:T(8,128)(2,1)} %bitcast.79, bf16[2,8,448,128]{3,2,1,0:T(8,128)(2,1)} %bitcast.83, bf16[2,128,3584]{2,1,0:T(8,128)(2,1)} %refs_2_.1, ...), custom_call_target="tpu_custom_call" | custom-call | bytes 11534336 | tf_op jit(solution)/shard_map/swapped/pallas_call | solution.py:186
  128.5 2.9 %collective-permute-start.29 = (bf16[2,32,896]{2,1,0:T(8,128)(2,1)S(1)}, bf16[2,32,896]{2,1,0:T(8,128)(2,1)S(1)}, u32[]{:S(2)}, u32[]{:S(2)}) collective-permute-start(bf16[2,32,896]{2,1,0:T(8,128)(2,1)S(1)} %get-tuple-element.73), channel_id=1, source_target_pairs={{0,32},{16,48},{32,64},{48,80},{64,96},{80,112},{96,0},{112,16},{1... | collective-permute-start | bytes 344072 | tf_op jit(solution)/shard_map/ppermute | solution.py:29
  131.4 1.9 %collective-permute-start.30 = (bf16[32,896]{1,0:T(8,128)(2,1)S(1)}, bf16[32,896]{1,0:T(8,128)(2,1)S(1)}, u32[]{:S(2)}, u32[]{:S(2)}) collective-permute-start(bf16[32,896]{1,0:T(8,128)(2,1)S(1)} %slice_bitcast_fusion), channel_id=1, source_target_pairs={{0,64},{16,80},{32,96},{48,112},{64,0},{80,16},{96,32},{112,48},{1... | collective-permute-start | bytes 172040 | tf_op jit(solution)/shard_map/ppermute | solution.py:29
  133.3 3.2 %collective-permute-done.28 = bf16[2,32,896]{2,1,0:T(8,128)(2,1)S(1)} collective-permute-done((bf16[2,32,896]{2,1,0:T(8,128)(2,1)S(1)}, bf16[2,32,896]{2,1,0:T(8,128)(2,1)S(1)}, u32[]{:S(2)}, u32[]{:S(2)}) %collective-permute-start.28) | collective-permute-done | bytes 114720 | tf_op jit(solution)/shard_map/ppermute | solution.py:29
  136.5 3.7 %collective-permute-done.29 = bf16[2,32,896]{2,1,0:T(8,128)(2,1)S(1)} collective-permute-done((bf16[2,32,896]{2,1,0:T(8,128)(2,1)S(1)}, bf16[2,32,896]{2,1,0:T(8,128)(2,1)S(1)}, u32[]{:S(2)}, u32[]{:S(2)}) %collective-permute-start.29) | collective-permute-done | bytes 114720 | tf_op jit(solution)/shard_map/ppermute | solution.py:29
  140.2 2.5 %collective-permute-start.31 = (bf16[32,896]{1,0:T(8,128)(2,1)S(1)}, bf16[32,896]{1,0:T(8,128)(2,1)S(1)}, u32[]{:S(2)}, u32[]{:S(2)}) collective-permute-start(bf16[32,896]{1,0:T(8,128)(2,1)S(1)} %get-tuple-element.70), channel_id=1, source_target_pairs={{0,112},{16,0},{32,16},{48,32},{64,48},{80,64},{96,80},{112,96},{1... | collective-permute-start | bytes 172040 | tf_op jit(solution)/shard_map/ppermute | solution.py:29
  142.8 0.9 slice_bitcast_fusion.3
  143.7 2.4 %collective-permute-start.22 = (bf16[32,896]{1,0:T(8,128)(2,1)S(1)}, bf16[32,896]{1,0:T(8,128)(2,1)S(1)}, u32[]{:S(2)}, u32[]{:S(2)}) collective-permute-start(bf16[32,896]{1,0:T(8,128)(2,1)S(1)} %get-tuple-element.74), channel_id=1, source_target_pairs={{0,6},{2,0},{4,2},{6,4},{1,7},{3,1},{5,3},{7,5},{8,14},{10,8},{12,... | collective-permute-start | bytes 172040 | tf_op jit(solution)/shard_map/ppermute | solution.py:29
  146.4 1.3 collective-permute-start.24
  148.2 3.6 %collective-permute-done.23 = bf16[32,896]{1,0:T(8,128)(2,1)S(1)} collective-permute-done((bf16[32,896]{1,0:T(8,128)(2,1)S(1)}, bf16[32,896]{1,0:T(8,128)(2,1)S(1)}, u32[]{:S(2)}, u32[]{:S(2)}) %collective-permute-start.23) | collective-permute-done | bytes 57376 | tf_op jit(solution)/shard_map/ppermute | solution.py:29
  152.4 0.9 fusion.2
  153.3 1.0 collective-permute-start.34
  154.3 1.7 collective-permute-start.35
  157.6 1.2 collective-permute-done.34
  158.8 2.3 %collective-permute-done.33 = bf16[2,16,448]{2,1,0:T(8,128)(2,1)S(1)} collective-permute-done((bf16[2,16,448]{2,1,0:T(8,128)(2,1)S(1)}, bf16[2,16,448]{2,1,0:T(8,128)(2,1)S(1)}, u32[]{:S(2)}, u32[]{:S(2)}) %collective-permute-start.33) | collective-permute-done | bytes 28704 | tf_op jit(solution)/shard_map/ppermute | solution.py:29
  (90 shorter events, 9.6 us)
Async XLA Ops:
  7.2 76.4 %all-gather.3.cloned.1.call-start = ((), (), s32[]{:S(2)}) async-start(), calls=%async_computation.2 | async-start | bytes 2359296 | tf_op jit(solution)/shard_map/all_gather | solution.py:314
  7.2 11.7 %collective-permute-start.3 = (bf16[2,8,448,128]{3,2,1,0:T(8,128)(2,1)}, bf16[2,8,448,128]{3,2,1,0:T(8,128)(2,1)}, u32[]{:S(2)}, u32[]{:S(2)}) collective-permute-start(bf16[2,8,448,128]{3,2,1,0:T(8,128)(2,1)} %bitcast.76), channel_id=1, source_target_pairs={{0,8},{8,0},{1,9},{9,1},{2,10},{10,2},{3,11},{11,3},{4,12},{12,4},... | collective-permute-start | bytes 5505032 | tf_op jit(solution)/shard_map/ppermute | solution.py:306
  7.3 20.7 %collective-permute-start.17 = (bf16[2,8,448,128]{3,2,1,0:T(8,128)(2,1)}, bf16[2,8,448,128]{3,2,1,0:T(8,128)(2,1)}, u32[]{:S(2)}, u32[]{:S(2)}) collective-permute-start(bf16[2,8,448,128]{3,2,1,0:T(8,128)(2,1)} %bitcast.80), channel_id=1, source_target_pairs={{0,8},{8,0},{1,9},{9,1},{2,10},{10,2},{3,11},{11,3},{4,12},{12,4},... | collective-permute-start | bytes 5505032 | tf_op jit(solution)/shard_map/ppermute | solution.py:306
  7.9 17.3 %copy-start.5 = (s32[5]{0:T(128)}, s32[5]{0:T(128)S(1)}, u32[]{:S(2)}) copy-start(s32[5]{0:T(128)S(1)} %stack.57.place) | copy-start | bytes 64
  10.8 14.4 %copy-start.3 = (bf16[2,16,512]{2,1,0:T(8,128)(2,1)}, bf16[2,16,512]{2,1,0:T(8,128)(2,1)S(1)}, u32[]{:S(2)}) copy-start(bf16[2,16,512]{2,1,0:T(8,128)(2,1)S(1)} %ride.1.refs_0_.refs_1_) | copy-start | bytes 98308
  10.9 18.0 %copy-start.10 = (bf16[2,128,3584]{2,1,0:T(8,128)(2,1)S(1)}, bf16[2,128,3584]{2,1,0:T(8,128)(2,1)}, u32[]{:S(2)}) copy-start(bf16[2,128,3584]{2,1,0:T(8,128)(2,1)} %refs_2_.1) | copy-start | bytes 5505028
  10.9 4.3 %collective-permute-start = (bf16[2,16,512]{2,1,0:T(8,128)(2,1)S(1)}, bf16[2,16,512]{2,1,0:T(8,128)(2,1)S(1)}, u32[]{:S(2)}, u32[]{:S(2)}) collective-permute-start(bf16[2,16,512]{2,1,0:T(8,128)(2,1)S(1)} %ride.1.refs_0_.refs_1_), channel_id=1, source_target_pairs={{0,1},{1,128},{128,129},{129,0},{2,3},{3,130},{130,131},{131,2},{4... | collective-permute-start | bytes 98312 | tf_op jit(solution)/shard_map/ppermute | solution.py:29
  12.9 5.4 %collective-permute-start.1 = (bf16[2,16,512]{2,1,0:T(8,128)(2,1)S(1)}, bf16[2,16,512]{2,1,0:T(8,128)(2,1)S(1)}, u32[]{:S(2)}, u32[]{:S(2)}) collective-permute-start(bf16[2,16,512]{2,1,0:T(8,128)(2,1)S(1)} %ride.1.refs_0_.refs_1_), channel_id=1, source_target_pairs={{0,128},{1,129},{128,0},{129,1},{2,130},{3,131},{130,2},{131,3},{4... | collective-permute-start | bytes 98312 | tf_op jit(solution)/shard_map/ppermute | solution.py:29
  13.8 5.1 %collective-permute-start.2 = (bf16[2,16,512]{2,1,0:T(8,128)(2,1)S(1)}, bf16[2,16,512]{2,1,0:T(8,128)(2,1)S(1)}, u32[]{:S(2)}, u32[]{:S(2)}) collective-permute-start(bf16[2,16,512]{2,1,0:T(8,128)(2,1)S(1)} %ride.1.refs_0_.refs_1_), channel_id=1, source_target_pairs={{0,129},{1,0},{128,1},{129,128},{2,131},{3,2},{130,3},{131,130},{4... | collective-permute-start | bytes 98312 | tf_op jit(solution)/shard_map/ppermute | solution.py:29
  19.5 20.3 %copy-start = (bf16[32,1024]{1,0:T(8,128)(2,1)}, bf16[32,1024]{1,0:T(8,128)(2,1)S(1)}, u32[]{:S(2)}) copy-start(bf16[32,1024]{1,0:T(8,128)(2,1)S(1)} %get-tuple-element.39.refs_2_) | copy-start | bytes 196612
  19.5 8.6 %collective-permute-start.14 = (bf16[32,1024]{1,0:T(8,128)(2,1)S(1)}, bf16[32,1024]{1,0:T(8,128)(2,1)S(1)}, u32[]{:S(2)}, u32[]{:S(2)}) collective-permute-start(bf16[32,1024]{1,0:T(8,128)(2,1)S(1)} %get-tuple-element.50), channel_id=1, source_target_pairs={{0,2},{2,4},{4,6},{6,0},{1,3},{3,5},{5,7},{7,1},{8,10},{10,12},{12... | collective-permute-start | bytes 196616 | tf_op jit(solution)/shard_map/ppermute | solution.py:29
  21.0 7.0 %collective-permute-start.15 = (bf16[32,1024]{1,0:T(8,128)(2,1)S(1)}, bf16[32,1024]{1,0:T(8,128)(2,1)S(1)}, u32[]{:S(2)}, u32[]{:S(2)}) collective-permute-start(bf16[32,1024]{1,0:T(8,128)(2,1)S(1)} %get-tuple-element.50), channel_id=1, source_target_pairs={{0,4},{2,6},{4,0},{6,2},{1,5},{3,7},{5,1},{7,3},{8,12},{10,14},{12... | collective-permute-start | bytes 196616 | tf_op jit(solution)/shard_map/ppermute | solution.py:29
  23.8 4.3 %collective-permute-start.16 = (bf16[32,1024]{1,0:T(8,128)(2,1)S(1)}, bf16[32,1024]{1,0:T(8,128)(2,1)S(1)}, u32[]{:S(2)}, u32[]{:S(2)}) collective-permute-start(bf16[32,1024]{1,0:T(8,128)(2,1)S(1)} %get-tuple-element.50), channel_id=1, source_target_pairs={{0,6},{2,0},{4,2},{6,4},{1,7},{3,1},{5,3},{7,5},{8,14},{10,8},{12,... | collective-permute-start | bytes 196616 | tf_op jit(solution)/shard_map/ppermute | solution.py:29
  28.8 114.0 %reduce-scatter.2.cloned.1.call-start = ((), (), s32[]{:S(2)}) async-start(), calls=%async_computation.1 | async-start | bytes 2064384 | tf_op jit(solution)/shard_map/reduce_scatter | solution.py:322
  28.9 14.1 %collective-permute-start.8 = (bf16[2,128,3584]{2,1,0:T(8,128)(2,1)S(1)}, bf16[2,128,3584]{2,1,0:T(8,128)(2,1)}, u32[]{:S(2)}, u32[]{:S(2)}) collective-permute-start(bf16[2,128,3584]{2,1,0:T(8,128)(2,1)S(1)} %copy-done.10), channel_id=1, source_target_pairs={{0,8},{8,0},{1,9},{9,1},{2,10},{10,2},{3,11},{11,3},{4,12},{12,4},... | collective-permute-start | bytes 5505032 | tf_op jit(solution)/shard_map/ppermute | solution.py:306
  29.0 34.1 %collective-permute-start.4 = (bf16[8,448,128]{2,1,0:T(8,128)(2,1)}, bf16[8,448,128]{2,1,0:T(8,128)(2,1)}, u32[]{:S(2)}, u32[]{:S(2)}) collective-permute-start(bf16[8,448,128]{2,1,0:T(8,128)(2,1)} %handed.3), channel_id=1, source_target_pairs={{0,128},{128,0},{1,129},{129,1},{2,130},{130,2},{3,131},{131,3},{4... | collective-permute-start | bytes 2752520 | tf_op jit(solution)/shard_map/ppermute | solution.py:313
  29.4 13.6 %collective-permute-start.5 = (bf16[32,1024]{1,0:T(8,128)(2,1)S(1)}, bf16[32,1024]{1,0:T(8,128)(2,1)S(1)}, u32[]{:S(2)}, u32[]{:S(2)}) collective-permute-start(bf16[32,1024]{1,0:T(8,128)(2,1)S(1)} %get-tuple-element.39.refs_2_), channel_id=1, source_target_pairs={{0,16},{16,32},{32,48},{48,64},{64,80},{80,96},{96,112},{112,0},{1... | collective-permute-start | bytes 196616 | tf_op jit(solution)/shard_map/ppermute | solution.py:29
  31.3 11.7 %collective-permute-start.6 = (bf16[32,1024]{1,0:T(8,128)(2,1)S(1)}, bf16[32,1024]{1,0:T(8,128)(2,1)S(1)}, u32[]{:S(2)}, u32[]{:S(2)}) collective-permute-start(bf16[32,1024]{1,0:T(8,128)(2,1)S(1)} %get-tuple-element.39.refs_2_), channel_id=1, source_target_pairs={{0,112},{16,0},{32,16},{48,32},{64,48},{80,64},{96,80},{112,96},{1... | collective-permute-start | bytes 196616 | tf_op jit(solution)/shard_map/ppermute | solution.py:29
  35.2 8.9 %collective-permute-start.7 = (bf16[32,1024]{1,0:T(8,128)(2,1)S(1)}, bf16[32,1024]{1,0:T(8,128)(2,1)S(1)}, u32[]{:S(2)}, u32[]{:S(2)}) collective-permute-start(bf16[32,1024]{1,0:T(8,128)(2,1)S(1)} %get-tuple-element.39.refs_2_), channel_id=1, source_target_pairs={{0,64},{16,80},{32,96},{48,112},{64,0},{80,16},{96,32},{112,48},{1... | collective-permute-start | bytes 196616 | tf_op jit(solution)/shard_map/ppermute | solution.py:29
  42.9 40.7 %copy-start.6 = (s32[5]{0:T(128)S(1)}, s32[5]{0:T(128)}, u32[]{:S(2)}) copy-start(s32[5]{0:T(128)} %copy-done.5) | copy-start | bytes 64
  42.9 40.7 %copy-start.9 = (s32[64]{0:T(128)S(1)}, s32[64]{0:T(128)}, u32[]{:S(2)}) copy-start(s32[64]{0:T(128)} %param.11) | copy-start | bytes 772
  44.9 18.2 %copy-start.14 = (bf16[8,448,128]{2,1,0:T(8,128)(2,1)S(1)}, bf16[8,448,128]{2,1,0:T(8,128)(2,1)}, u32[]{:S(2)}) copy-start(bf16[8,448,128]{2,1,0:T(8,128)(2,1)} %get-tuple-element.48) | copy-start | bytes 2752516
  45.0 18.0 %collective-permute-start.11 = (bf16[4,32,1024]{2,1,0:T(8,128)(2,1)S(1)}, bf16[4,32,1024]{2,1,0:T(8,128)(2,1)S(1)}, u32[]{:S(2)}, u32[]{:S(2)}) collective-permute-start(bf16[4,32,1024]{2,1,0:T(8,128)(2,1)S(1)} %join.3.refs_0_), channel_id=1, source_target_pairs={{0,2},{2,4},{4,6},{6,0},{1,3},{3,5},{5,7},{7,1},{8,10},{10,12},{12... | collective-permute-start | bytes 786440 | tf_op jit(solution)/shard_map/ppermute | solution.py:29
  45.6 17.4 %collective-permute-start.12 = (bf16[4,32,1024]{2,1,0:T(8,128)(2,1)S(1)}, bf16[4,32,1024]{2,1,0:T(8,128)(2,1)S(1)}, u32[]{:S(2)}, u32[]{:S(2)}) collective-permute-start(bf16[4,32,1024]{2,1,0:T(8,128)(2,1)S(1)} %join.3.refs_0_), channel_id=1, source_target_pairs={{0,6},{2,0},{4,2},{6,4},{1,7},{3,1},{5,3},{7,5},{8,14},{10,8},{12,... | collective-permute-start | bytes 786440 | tf_op jit(solution)/shard_map/ppermute | solution.py:29
  49.1 10.3 %collective-permute-start.10 = (bf16[2,32,1024]{2,1,0:T(8,128)(2,1)S(1)}, bf16[2,32,1024]{2,1,0:T(8,128)(2,1)S(1)}, u32[]{:S(2)}, u32[]{:S(2)}) collective-permute-start(bf16[2,32,1024]{2,1,0:T(8,128)(2,1)S(1)} %get-tuple-element.79), channel_id=1, source_target_pairs={{0,96},{16,112},{32,0},{48,16},{64,32},{80,48},{96,64},{112,80},{1... | collective-permute-start | bytes 393224 | tf_op jit(solution)/shard_map/ppermute | solution.py:29
  51.0 12.0 %collective-permute-start.9 = (bf16[2,32,1024]{2,1,0:T(8,128)(2,1)S(1)}, bf16[2,32,1024]{2,1,0:T(8,128)(2,1)S(1)}, u32[]{:S(2)}, u32[]{:S(2)}) collective-permute-start(bf16[2,32,1024]{2,1,0:T(8,128)(2,1)S(1)} %get-tuple-element.80), channel_id=1, source_target_pairs={{0,32},{16,48},{32,64},{48,80},{64,96},{80,112},{96,0},{112,16},{1... | collective-permute-start | bytes 393224 | tf_op jit(solution)/shard_map/ppermute | solution.py:29
  63.1 20.6 %copy-start.2 = (bf16[8,32,1024]{2,1,0:T(8,128)(2,1)}, bf16[8,32,1024]{2,1,0:T(8,128)(2,1)S(1)}, u32[]{:S(2)}) copy-start(bf16[8,32,1024]{2,1,0:T(8,128)(2,1)S(1)} %join.5.refs_1_) | copy-start | bytes 1572868
  63.1 20.3 %collective-permute-start.13 = (bf16[8,448,128]{2,1,0:T(8,128)(2,1)S(1)}, bf16[8,448,128]{2,1,0:T(8,128)(2,1)S(1)}, u32[]{:S(2)}, u32[]{:S(2)}) collective-permute-start(bf16[8,448,128]{2,1,0:T(8,128)(2,1)S(1)} %copy-done.14), channel_id=1, source_target_pairs={{0,128},{128,0},{1,129},{129,1},{2,130},{130,2},{3,131},{131,3},{4... | collective-permute-start | bytes 2752520 | tf_op jit(solution)/shard_map/ppermute | solution.py:317
  66.3 17.3 %collective-permute-start.19 = (bf16[8,32,1024]{2,1,0:T(8,128)(2,1)S(1)}, bf16[8,32,1024]{2,1,0:T(8,128)(2,1)}, u32[]{:S(2)}, u32[]{:S(2)}) collective-permute-start(bf16[8,32,1024]{2,1,0:T(8,128)(2,1)S(1)} %join.5.refs_1_), channel_id=1, source_target_pairs={{0,4},{2,6},{4,0},{6,2},{1,5},{3,7},{5,1},{7,3},{8,12},{10,14},{12... | collective-permute-start | bytes 1572872 | tf_op jit(solution)/shard_map/ppermute | solution.py:29
  67.4 16.2 %collective-permute-start.18 = (bf16[4,32,1024]{2,1,0:T(8,128)(2,1)S(1)}, bf16[4,32,1024]{2,1,0:T(8,128)(2,1)S(1)}, u32[]{:S(2)}, u32[]{:S(2)}) collective-permute-start(bf16[4,32,1024]{2,1,0:T(8,128)(2,1)S(1)} %join.4.refs_1_), channel_id=1, source_target_pairs={{0,2},{2,4},{4,6},{6,0},{1,3},{3,5},{5,7},{7,1},{8,10},{10,12},{12... | collective-permute-start | bytes 786440 | tf_op jit(solution)/shard_map/ppermute | solution.py:29
  68.7 14.9 %collective-permute-start.20 = (bf16[4,32,1024]{2,1,0:T(8,128)(2,1)S(1)}, bf16[4,32,1024]{2,1,0:T(8,128)(2,1)S(1)}, u32[]{:S(2)}, u32[]{:S(2)}) collective-permute-start(bf16[4,32,1024]{2,1,0:T(8,128)(2,1)S(1)} %join.4.refs_1_), channel_id=1, source_target_pairs={{0,6},{2,0},{4,2},{6,4},{1,7},{3,1},{5,3},{7,5},{8,14},{10,8},{12,... | collective-permute-start | bytes 786440 | tf_op jit(solution)/shard_map/ppermute | solution.py:29
  83.4 13.7 %copy-start.11 = (bf16[8,448,128]{2,1,0:T(8,128)(2,1)}, bf16[8,448,128]{2,1,0:T(8,128)(2,1)S(1)}, u32[]{:S(2)}) copy-start(bf16[8,448,128]{2,1,0:T(8,128)(2,1)S(1)} %collective-permute-done.13.refs_4_) | copy-start | bytes 2752516
  97.2 24.0 %collective-permute-start.21 = (bf16[128,3584]{1,0:T(8,128)(2,1)}, bf16[128,3584]{1,0:T(8,128)(2,1)S(1)}, u32[]{:S(2)}, u32[]{:S(2)}) collective-permute-start(bf16[128,3584]{1,0:T(8,128)(2,1)} %get-tuple-element.55), channel_id=1, source_target_pairs={{0,128},{128,0},{1,129},{129,1},{2,130},{130,2},{3,131},{131,3},{4... | collective-permute-start | bytes 2752520 | tf_op jit(solution)/shard_map/ppermute | solution.py:318
  100.5 27.6 %collective-permute-start.25 = (bf16[8,32,896]{2,1,0:T(8,128)(2,1)S(1)}, bf16[8,32,896]{2,1,0:T(8,128)(2,1)S(1)}, u32[]{:S(2)}, u32[]{:S(2)}) collective-permute-start(bf16[8,32,896]{2,1,0:T(8,128)(2,1)S(1)} %get-tuple-element.61), channel_id=1, source_target_pairs={{0,6},{2,0},{4,2},{6,4},{1,7},{3,1},{5,3},{7,5},{8,14},{10,8},{12,... | collective-permute-start | bytes 1376264 | tf_op jit(solution)/shard_map/ppermute | solution.py:29
  102.4 25.7 %collective-permute-start.26 = (bf16[8,32,896]{2,1,0:T(8,128)(2,1)}, bf16[8,32,896]{2,1,0:T(8,128)(2,1)S(1)}, u32[]{:S(2)}, u32[]{:S(2)}) collective-permute-start(bf16[8,32,896]{2,1,0:T(8,128)(2,1)} %get-tuple-element.62), channel_id=1, source_target_pairs={{0,4},{2,6},{4,0},{6,2},{1,5},{3,7},{5,1},{7,3},{8,12},{10,14},{12... | collective-permute-start | bytes 1376264 | tf_op jit(solution)/shard_map/ppermute | solution.py:29
  102.4 25.7 %collective-permute-start.27 = (bf16[8,32,896]{2,1,0:T(8,128)(2,1)S(1)}, bf16[8,32,896]{2,1,0:T(8,128)(2,1)S(1)}, u32[]{:S(2)}, u32[]{:S(2)}) collective-permute-start(bf16[8,32,896]{2,1,0:T(8,128)(2,1)S(1)} %copy-done.15), channel_id=1, source_target_pairs={{0,2},{2,4},{4,6},{6,0},{1,3},{3,5},{5,7},{7,1},{8,10},{10,12},{12... | collective-permute-start | bytes 1376264 | tf_op jit(solution)/shard_map/ppermute | solution.py:29
  127.7 28.6 %collective-permute-start.36 = (f32[64]{0:T(128)S(1)}, f32[64]{0:T(128)S(1)}, u32[]{:S(2)}, u32[]{:S(2)}) collective-permute-start(f32[64]{0:T(128)S(1)} %slice_bitcast_fusion.4), channel_id=1, source_target_pairs={{0,8},{8,0},{1,9},{9,1},{2,10},{10,2},{3,11},{11,3},{4,12},{12,4},... | collective-permute-start | bytes 776 | tf_op jit(solution)/shard_map/ppermute | solution.py:331
  128.4 8.1 %collective-permute-start.28 = (bf16[2,32,896]{2,1,0:T(8,128)(2,1)S(1)}, bf16[2,32,896]{2,1,0:T(8,128)(2,1)S(1)}, u32[]{:S(2)}, u32[]{:S(2)}) collective-permute-start(bf16[2,32,896]{2,1,0:T(8,128)(2,1)S(1)} %get-tuple-element.72), channel_id=1, source_target_pairs={{0,96},{16,112},{32,0},{48,16},{64,32},{80,48},{96,64},{112,80},{1... | collective-permute-start | bytes 344072 | tf_op jit(solution)/shard_map/ppermute | solution.py:29
  128.5 11.7 %collective-permute-start.29 = (bf16[2,32,896]{2,1,0:T(8,128)(2,1)S(1)}, bf16[2,32,896]{2,1,0:T(8,128)(2,1)S(1)}, u32[]{:S(2)}, u32[]{:S(2)}) collective-permute-start(bf16[2,32,896]{2,1,0:T(8,128)(2,1)S(1)} %get-tuple-element.73), channel_id=1, source_target_pairs={{0,32},{16,48},{32,64},{48,80},{64,96},{80,112},{96,0},{112,16},{1... | collective-permute-start | bytes 344072 | tf_op jit(solution)/shard_map/ppermute | solution.py:29
  131.4 14.7 %collective-permute-start.30 = (bf16[32,896]{1,0:T(8,128)(2,1)S(1)}, bf16[32,896]{1,0:T(8,128)(2,1)S(1)}, u32[]{:S(2)}, u32[]{:S(2)}) collective-permute-start(bf16[32,896]{1,0:T(8,128)(2,1)S(1)} %slice_bitcast_fusion), channel_id=1, source_target_pairs={{0,64},{16,80},{32,96},{48,112},{64,0},{80,16},{96,32},{112,48},{1... | collective-permute-start | bytes 172040 | tf_op jit(solution)/shard_map/ppermute | solution.py:29
  140.2 6.1 %collective-permute-start.31 = (bf16[32,896]{1,0:T(8,128)(2,1)S(1)}, bf16[32,896]{1,0:T(8,128)(2,1)S(1)}, u32[]{:S(2)}, u32[]{:S(2)}) collective-permute-start(bf16[32,896]{1,0:T(8,128)(2,1)S(1)} %get-tuple-element.70), channel_id=1, source_target_pairs={{0,112},{16,0},{32,16},{48,32},{64,48},{80,64},{96,80},{112,96},{1... | collective-permute-start | bytes 172040 | tf_op jit(solution)/shard_map/ppermute | solution.py:29
  142.8 5.4 %collective-permute-start.32 = (bf16[32,896]{1,0:T(8,128)(2,1)S(1)}, bf16[32,896]{1,0:T(8,128)(2,1)S(1)}, u32[]{:S(2)}, u32[]{:S(2)}) collective-permute-start(bf16[32,896]{1,0:T(8,128)(2,1)S(1)} %get-tuple-element.71), channel_id=1, source_target_pairs={{0,16},{16,32},{32,48},{48,64},{64,80},{80,96},{96,112},{112,0},{1... | collective-permute-start | bytes 172040 | tf_op jit(solution)/shard_map/ppermute | solution.py:29
  143.7 4.5 %collective-permute-start.22 = (bf16[32,896]{1,0:T(8,128)(2,1)S(1)}, bf16[32,896]{1,0:T(8,128)(2,1)S(1)}, u32[]{:S(2)}, u32[]{:S(2)}) collective-permute-start(bf16[32,896]{1,0:T(8,128)(2,1)S(1)} %get-tuple-element.74), channel_id=1, source_target_pairs={{0,6},{2,0},{4,2},{6,4},{1,7},{3,1},{5,3},{7,5},{8,14},{10,8},{12,... | collective-permute-start | bytes 172040 | tf_op jit(solution)/shard_map/ppermute | solution.py:29
  146.1 5.7 %collective-permute-start.23 = (bf16[32,896]{1,0:T(8,128)(2,1)S(1)}, bf16[32,896]{1,0:T(8,128)(2,1)S(1)}, u32[]{:S(2)}, u32[]{:S(2)}) collective-permute-start(bf16[32,896]{1,0:T(8,128)(2,1)S(1)} %get-tuple-element.76), channel_id=1, source_target_pairs={{0,4},{2,6},{4,0},{6,2},{1,5},{3,7},{5,1},{7,3},{8,12},{10,14},{12... | collective-permute-start | bytes 172040 | tf_op jit(solution)/shard_map/ppermute | solution.py:29
  146.4 6.0 %collective-permute-start.24 = (bf16[32,896]{1,0:T(8,128)(2,1)S(1)}, bf16[32,896]{1,0:T(8,128)(2,1)S(1)}, u32[]{:S(2)}, u32[]{:S(2)}) collective-permute-start(bf16[32,896]{1,0:T(8,128)(2,1)S(1)} %get-tuple-element.75), channel_id=1, source_target_pairs={{0,2},{2,4},{4,6},{6,0},{1,3},{3,5},{5,7},{7,1},{8,10},{10,12},{12... | collective-permute-start | bytes 172040 | tf_op jit(solution)/shard_map/ppermute | solution.py:29
  153.3 5.5 %collective-permute-start.34 = (bf16[2,16,448]{2,1,0:T(8,128)(2,1)S(1)}, bf16[2,16,448]{2,1,0:T(8,128)(2,1)S(1)}, u32[]{:S(2)}, u32[]{:S(2)}) collective-permute-start(bf16[2,16,448]{2,1,0:T(8,128)(2,1)S(1)} %get-tuple-element.77), channel_id=1, source_target_pairs={{0,128},{1,129},{128,0},{129,1},{2,130},{3,131},{130,2},{131,3},{4... | collective-permute-start | bytes 86024 | tf_op jit(solution)/shard_map/ppermute | solution.py:29
  154.3 4.5 %collective-permute-start.35 = (bf16[2,16,448]{2,1,0:T(8,128)(2,1)S(1)}, bf16[2,16,448]{2,1,0:T(8,128)(2,1)S(1)}, u32[]{:S(2)}, u32[]{:S(2)}) collective-permute-start(bf16[2,16,448]{2,1,0:T(8,128)(2,1)S(1)} %get-tuple-element.78), channel_id=1, source_target_pairs={{0,1},{1,128},{128,129},{129,0},{2,3},{3,130},{130,131},{131,2},{4... | collective-permute-start | bytes 86024 | tf_op jit(solution)/shard_map/ppermute | solution.py:29
  156.0 5.1 %collective-permute-start.33 = (bf16[2,16,448]{2,1,0:T(8,128)(2,1)S(1)}, bf16[2,16,448]{2,1,0:T(8,128)(2,1)S(1)}, u32[]{:S(2)}, u32[]{:S(2)}) collective-permute-start(bf16[2,16,448]{2,1,0:T(8,128)(2,1)S(1)} %get-tuple-element.65), channel_id=1, source_target_pairs={{0,129},{1,0},{128,1},{129,128},{2,131},{3,2},{130,3},{131,130},{4... | collective-permute-start | bytes 86024 | tf_op jit(solution)/shard_map/ppermute | solution.py:29
  (7 other events, 15.4 us)
Sparse Core Ops, SparseCore 0:
  28.9 47.0 all-gather.2
  97.3 42.0 reduce-scatter.1

commit v5 on v4

--- a/solution.py
+++ b/solution.py
@@ -77,13 +77,16 @@
     )(*parts)
 
 
-def reduce_z(pieces):
-    back2 = send(pieces[4:6], "z", -2)
-    ahead2 = send(pieces[6:8], "z", 2)
-    far = send(pieces[3], "z", -4)
-    back = send(total([pieces[1], back2[1]]), "z", -1)
-    ahead = send(total([pieces[2], ahead2[1]]), "z", 1)
-    return total([pieces[0], back2[0], ahead2[0], far, back, ahead])
+def reduce_zx(pieces):
+    own, (near1, far1), (middle,), (near3, far3) = pieces
+    far1, far3, middle_in = send(far1, "x", -1), send(far3, "x", 1), send(middle, "x", -2)
+    late = total([own[3:], far1, middle_in[3:], far3])
+    near1, near3 = send(after(near1, far1, far3), "x", -1), send(after(near3, far1, far3), "x", 1)
+    back2, ahead2, far = send(late[1:3], "z", -2), send(late[3:], "z", 2), send(late[0], "z", -4)
+    early = total([own[:3], near1, middle_in[:3], near3])
+    back = send(total([early[1], back2[1]]), "z", -1)
+    ahead = send(total([early[2], ahead2[1]]), "z", 1)
+    return total([early[0], back2[0], ahead2[0], far, back, ahead]), late
 
 
 def ride_kernel(place, tokens_ref, routes_ref, gate_ref, out_ref):
@@ -198,8 +201,8 @@
 def layer_kernel(place, position_ref, *refs):
     piece0, pieces1 = refs[0], ((refs[1],), refs[2:4], (refs[4],), refs[5:7])
     gate_own, up_own, down_own, gate_other, up_other, down_other = refs[7:13]
-    out0, outs1, count_ref = refs[13], refs[14:18], refs[18]
-    rows_ref, gate_ref, up_ref, down_ref, hidden_ref, result_ref, sems = refs[19:]
+    out0, outs1, count_ref = refs[13], ((refs[14],), refs[15:17], (refs[17],), refs[18:20]), refs[20]
+    rows_ref, gate_ref, up_ref, down_ref, hidden_ref, result_ref, sems = refs[21:]
     my_x, my_core, chip = place[0], place[1], place[2]
     span = 2 * GROUP
 
@@ -264,7 +267,9 @@
         x_at = lax.rem(my_x - xr + 4, 4)
         for zr in range(8):
             out0[zr, xr] = result_ref[x_at, zr * span : (zr + 1) * span, :]
-            outs1[xr][zr] = result_ref[x_at, (8 + zr) * span : (9 + zr) * span, :]
+            whole = len(outs1[xr]) == 1
+            out = outs1[xr][0 if whole or zr < 3 else 1]
+            out[zr if whole or zr < 3 else zr - 3] = result_ref[x_at, (8 + zr) * span : (9 + zr) * span, :]
 
 
 def run_layer(place, position, piece0, pieces1, weights):
@@ -272,12 +277,12 @@
     out = pl.pallas_call(
         layer_kernel,
         out_shape=[jax.ShapeDtypeStruct((8, 4, 2 * GROUP, PAIR), jnp.bfloat16)]
-        + [jax.ShapeDtypeStruct((8, 2 * GROUP, PAIR), jnp.bfloat16)] * 4
+        + [jax.ShapeDtypeStruct((n, 2 * GROUP, PAIR), jnp.bfloat16) for n in (8, 3, 5, 8, 3, 5)]
         + [jax.ShapeDtypeStruct((8, 64), jnp.float32)],
         in_specs=[pl.BlockSpec(memory_space=pltpu.SMEM)]
         + [vmem] * 8
         + [pl.BlockSpec(memory_space=pltpu.HBM)] * 6,
-        out_specs=[vmem] * 6,
+        out_specs=[vmem] * 8,
         scratch_shapes=[
             pltpu.VMEM((512, 8 * LANES), jnp.bfloat16),
             pltpu.VMEM((4, 8, LANES, 128), jnp.bfloat16),
@@ -291,7 +296,7 @@
         cost_estimate=pl.CostEstimate(flops=2 * 512 * 3584 * 1536, bytes_accessed=20 * 2**20, transcendentals=0),
         name="layer",
     )(place, position, piece0, *sum(pieces1, ()), *weights)
-    return out[0], out[1:5], out[5]
+    return out[0], (out[1], out[2:4], out[4:5], out[5:7]), out[7]
 
 
 def on_device(tokens, routes, gate_fix, position, swap_slot, w_gate, w_up, w_down):
@@ -317,12 +322,11 @@
     up_taken = lax.ppermute(after(up_given, gate_taken, over_z), "yh", swap_y)
     down_taken = lax.ppermute(after(down_given, up_taken), "yh", swap_y)
     out0, out1, counts = run_layer(after(place, up_taken), position.reshape(1, 64), piece0, pieces1, weights)
-    new = run_swapped(place, swap_slot, panels, (gate_taken, up_taken, down_taken))
+    back1, late = reduce_zx(out1)
+    new = run_swapped(place, swap_slot, panels, (gate_taken, up_taken, after(down_taken, late)))
 
     back0 = lax.psum_scatter(out0, "z", scatter_dimension=0)
     back0 = after(back0, *new)
-    back1 = reduce_ring(out1, "x")
-    back1 = reduce_z(back1)
     back0 = reduce_ring([back0[k] for k in range(4)], "x")
     back = jnp.stack([back0, back1]).reshape(2, 2, GROUP, PAIR)
     halves = [back[:, 0, :, :WIDTH], back[:, 0, :, WIDTH:], back[:, 1, :, :WIDTH], back[:, 1, :, WIDTH:]]

time: 170 us -> 174 us (1.024)
    ppermute x1, waiting for transfers between devices: 17.8 us -> 0.01 us  [on_device(): down_taken = lax.ppermute(after(down_given, up_taken), 'yh', swap_y)]
    ppermute x30 -> x32, waiting for transfers between devices: 32.2 us -> 46.5 us  [send(): lax.ppermute(value, axes, [(i, (i + amount) % count) for i in range(count)])]
    reduce_scatter x1, waiting for transfers between devices: 0.01 us -> 2.75 us  [on_device(): back0 = lax.psum_scatter(out0, 'z', scatter_dimension=0)]
    ppermute x30 -> x32, starting transfers between devices: 47 us -> 48.9 us  [send(): lax.ppermute(value, axes, [(i, (i + amount) % count) for i in range(count)])]
    unnamed x32 -> x38, local copies, waits for them, and re-layouts: 4.04 us -> 5.65 us
  transfers between devices with their start and end apart: 39 -> 41, of which waited for: 16 -> 18; matrix products, arithmetic and copies ran while one was open for 2% -> 3% of each run, Pallas kernels for 8% -> 7%
where the time goes in v5:
time: 174 us; the launch traced here: 173 us
  waiting for transfers between devices  62.1 us (36%)
  starting transfers between devices  56.6 us (33%)
  Pallas kernels  26.3 us (15%)
  between operations  16.2 us (9%)
  local copies, waits for them, and re-layouts  6.65 us (4%)
  other arithmetic  5.21 us (3%)
    ppermute x32, starting transfers between devices, send(): lax.ppermute(value, axes, [(i, (i + amount) % count) for i in range(count)])  48.9 us
    ppermute x32, waiting for transfers between devices, send(): lax.ppermute(value, axes, [(i, (i + amount) % count) for i in range(count)])  46.5 us
    pallas_call x1, Pallas kernels, run_layer(): pl.pallas_call(layer_kernel, out_shape=[jax.ShapeDtypeStruct((8, 4, 2 * G...  13.4 us
    ppermute x1, waiting for transfers between devices, on_device(): up_taken = lax.ppermute(after(up_given, gate_taken, over_z), 'yh', swap_y)  12.8 us
    pallas_call x2, Pallas kernels, run_handed(): pl.pallas_call(handed_kernel, out_shape=[jax.ShapeDtypeStruct(p.shape[1:]...  5.91 us
    unnamed x38, local copies, waits for them, and re-layouts  5.65 us
    pallas_call x1, Pallas kernels, run_swapped(): pl.pallas_call(swapped_kernel, out_shape=[jax.ShapeDtypeStruct(p.shape, p...  5.49 us
  transfers between devices with their start and end apart: 41, of which 18 were waited for; matrix products, arithmetic and copies ran while one was open for 3% of the time, Pallas kernels for 7%

profile of v5, /device:TPU:24, one launch (start us, length us, event | category | flops | bytes accessed | tf_op | source)
XLA Modules:
  0.0 173.0 jit_solution(4642023155162548550)
XLA Ops:
  10.9 2.0 %collective-permute-start = (bf16[2,16,512]{2,1,0:T(8,128)(2,1)S(1)}, bf16[2,16,512]{2,1,0:T(8,128)(2,1)S(1)}, u32[]{:S(2)}, u32[]{:S(2)}) collective-permute-start(bf16[2,16,512]{2,1,0:T(8,128)(2,1)S(1)} %ride.1.refs_0_.refs_1_), channel_id=1, source_target_pairs={{0,1},{1,128},{128,129},{129,0},{2,3},{3,130},{130,131},{131,2},{4... | collective-permute-start | bytes 98312 | tf_op jit(solution)/shard_map/ppermute | solution.py:29
  13.9 1.3 collective-permute-done.refs_1_
  15.2 3.1 %collective-permute-done.1.refs_2_ = bf16[2,16,512]{2,1,0:T(8,128)(2,1)S(1)} collective-permute-done((bf16[2,16,512]{2,1,0:T(8,128)(2,1)S(1)}, bf16[2,16,512]{2,1,0:T(8,128)(2,1)S(1)}, u32[]{:S(2)}, u32[]{:S(2)}) %collective-permute-start.1) | collective-permute-done | bytes 32800 | tf_op jit(solution)/shard_map/ppermute | solution.py:29
  19.5 1.6 collective-permute-start.14
  21.0 2.7 %collective-permute-start.15 = (bf16[32,1024]{1,0:T(8,128)(2,1)S(1)}, bf16[32,1024]{1,0:T(8,128)(2,1)S(1)}, u32[]{:S(2)}, u32[]{:S(2)}) collective-permute-start(bf16[32,1024]{1,0:T(8,128)(2,1)S(1)} %get-tuple-element.55), channel_id=1, source_target_pairs={{0,4},{2,6},{4,0},{6,2},{1,5},{3,7},{5,1},{7,3},{8,12},{10,14},{12... | collective-permute-start | bytes 196616 | tf_op jit(solution)/shard_map/ppermute | solution.py:29
  23.8 1.4 collective-permute-start.16
  25.2 2.8 %handed.3 = bf16[8,448,128]{2,1,0:T(8,128)(2,1)} custom-call(s32[5]{0:T(128)} %copy-done.5, s32[32]{0:T(128)} %slots.5, bf16[2,8,448,128]{3,2,1,0:T(8,128)(2,1)} %bitcast.77, bf16[2,16,512]{2,1,0:T(8,128)(2,1)} %copy-done.3), custom_call_target="tpu_custom_call" | custom-call | bytes 2097152 | tf_op jit(solution)/shard_map/handed/pallas_call | solution.py:157
  29.4 1.9 %collective-permute-start.5 = (bf16[32,1024]{1,0:T(8,128)(2,1)S(1)}, bf16[32,1024]{1,0:T(8,128)(2,1)S(1)}, u32[]{:S(2)}, u32[]{:S(2)}) collective-permute-start(bf16[32,1024]{1,0:T(8,128)(2,1)S(1)} %get-tuple-element.44.refs_2_), channel_id=1, source_target_pairs={{0,16},{16,32},{32,48},{48,64},{64,80},{80,96},{96,112},{112,0},{1... | collective-permute-start | bytes 196616 | tf_op jit(solution)/shard_map/ppermute | solution.py:29
  31.3 3.9 %collective-permute-start.6 = (bf16[32,1024]{1,0:T(8,128)(2,1)S(1)}, bf16[32,1024]{1,0:T(8,128)(2,1)S(1)}, u32[]{:S(2)}, u32[]{:S(2)}) collective-permute-start(bf16[32,1024]{1,0:T(8,128)(2,1)S(1)} %get-tuple-element.44.refs_2_), channel_id=1, source_target_pairs={{0,112},{16,0},{32,16},{48,32},{64,48},{80,64},{96,80},{112,96},{1... | collective-permute-start | bytes 196616 | tf_op jit(solution)/shard_map/ppermute | solution.py:29
  35.2 4.6 %collective-permute-start.7 = (bf16[32,1024]{1,0:T(8,128)(2,1)S(1)}, bf16[32,1024]{1,0:T(8,128)(2,1)S(1)}, u32[]{:S(2)}, u32[]{:S(2)}) collective-permute-start(bf16[32,1024]{1,0:T(8,128)(2,1)S(1)} %get-tuple-element.44.refs_2_), channel_id=1, source_target_pairs={{0,64},{16,80},{32,96},{48,112},{64,0},{80,16},{96,32},{112,48},{1... | collective-permute-start | bytes 196616 | tf_op jit(solution)/shard_map/ppermute | solution.py:29
  39.8 3.1 %handed.2 = (bf16[8,448,128]{2,1,0:T(8,128)(2,1)}, bf16[128,3584]{1,0:T(8,128)(2,1)}) custom-call(s32[5]{0:T(128)} %copy-done.5, s32[32]{0:T(128)} %slots.5, bf16[2,8,448,128]{3,2,1,0:T(8,128)(2,1)} %bitcast.81, bf16[2,128,3584]{2,1,0:T(8,128)(2,1)} %refs_2_.1, bf16[32,1024]{1,0:T(8,128)(2,1)} %copy-done), custom_call_target="tpu_custom_call" | custom-call | bytes 4194304 | tf_op jit(solution)/shard_map/handed/pallas_call | solution.py:157
  43.0 1.1 collective-permute-done.7
  45.6 2.6 %collective-permute-start.12 = (bf16[4,32,1024]{2,1,0:T(8,128)(2,1)S(1)}, bf16[4,32,1024]{2,1,0:T(8,128)(2,1)S(1)}, u32[]{:S(2)}, u32[]{:S(2)}) collective-permute-start(bf16[4,32,1024]{2,1,0:T(8,128)(2,1)S(1)} %join.3.refs_0_), channel_id=1, source_target_pairs={{0,6},{2,0},{4,2},{6,4},{1,7},{3,1},{5,3},{7,5},{8,14},{10,8},{12,... | collective-permute-start | bytes 786440 | tf_op jit(solution)/shard_map/ppermute | solution.py:29
  48.3 0.9 pad_maximum_fusion.1
  49.2 1.9 %collective-permute-start.10 = (bf16[2,32,1024]{2,1,0:T(8,128)(2,1)S(1)}, bf16[2,32,1024]{2,1,0:T(8,128)(2,1)S(1)}, u32[]{:S(2)}, u32[]{:S(2)}) collective-permute-start(bf16[2,32,1024]{2,1,0:T(8,128)(2,1)S(1)} %get-tuple-element.89), channel_id=1, source_target_pairs={{0,96},{16,112},{32,0},{48,16},{64,32},{80,48},{96,64},{112,80},{1... | collective-permute-start | bytes 393224 | tf_op jit(solution)/shard_map/ppermute | solution.py:29
  51.0 1.2 collective-permute-start.9
  52.2 7.3 %collective-permute-done.10.refs_1_ = bf16[2,32,1024]{2,1,0:T(8,128)(2,1)S(1)} collective-permute-done((bf16[2,32,1024]{2,1,0:T(8,128)(2,1)S(1)}, bf16[2,32,1024]{2,1,0:T(8,128)(2,1)S(1)}, u32[]{:S(2)}, u32[]{:S(2)}) %collective-permute-start.10) | collective-permute-done | bytes 131104 | tf_op jit(solution)/shard_map/ppermute | solution.py:29
  59.5 3.5 %collective-permute-done.9.refs_0_ = bf16[2,32,1024]{2,1,0:T(8,128)(2,1)S(1)} collective-permute-done((bf16[2,32,1024]{2,1,0:T(8,128)(2,1)S(1)}, bf16[2,32,1024]{2,1,0:T(8,128)(2,1)S(1)}, u32[]{:S(2)}, u32[]{:S(2)}) %collective-permute-start.9) | collective-permute-done | bytes 131104 | tf_op jit(solution)/shard_map/ppermute | solution.py:29
  63.1 3.2 %collective-permute-start.13 = (bf16[8,448,128]{2,1,0:T(8,128)(2,1)S(1)}, bf16[8,448,128]{2,1,0:T(8,128)(2,1)S(1)}, u32[]{:S(2)}, u32[]{:S(2)}) collective-permute-start(bf16[8,448,128]{2,1,0:T(8,128)(2,1)S(1)} %copy-done.17), channel_id=1, source_target_pairs={{0,128},{128,0},{1,129},{129,1},{2,130},{130,2},{3,131},{131,3},{4... | collective-permute-start | bytes 2752520 | tf_op jit(solution)/shard_map/ppermute | solution.py:322
  66.3 1.1 collective-permute-start.19
  67.4 1.3 collective-permute-start.18
  68.8 1.9 %collective-permute-start.20 = (bf16[4,32,1024]{2,1,0:T(8,128)(2,1)S(1)}, bf16[4,32,1024]{2,1,0:T(8,128)(2,1)S(1)}, u32[]{:S(2)}, u32[]{:S(2)}) collective-permute-start(bf16[4,32,1024]{2,1,0:T(8,128)(2,1)S(1)} %join.4.refs_1_), channel_id=1, source_target_pairs={{0,6},{2,0},{4,2},{6,4},{1,7},{3,1},{5,3},{7,5},{8,14},{10,8},{12,... | collective-permute-start | bytes 786440 | tf_op jit(solution)/shard_map/ppermute | solution.py:29
  70.7 12.8 %collective-permute-done.13.refs_4_ = bf16[8,448,128]{2,1,0:T(8,128)(2,1)S(1)} collective-permute-done((bf16[8,448,128]{2,1,0:T(8,128)(2,1)S(1)}, bf16[8,448,128]{2,1,0:T(8,128)(2,1)S(1)}, u32[]{:S(2)}, u32[]{:S(2)}) %collective-permute-start.13) | collective-permute-done | bytes 917536 | tf_op jit(solution)/shard_map/ppermute | solution.py:322
  85.2 13.4 %layer.1 = (bf16[8,4,32,896]{3,2,1,0:T(8,128)(2,1)}, bf16[8,32,896]{2,1,0:T(8,128)(2,1)}, bf16[3,32,896]{2,1,0:T(8,128)(2,1)S(1)}, bf16[5,32,896]{2,1,0:T(8,128)...) custom-call(s32[5]{0:T(128)S(1)} %copy-done.6, ...), custom_call_target="tpu_custom_call" | custom-call | flops 5637144576 | bytes 20971520 | tf_op jit(solution)/shard_map/layer/pallas_call | solution.py:277
  98.8 1.5 collective-permute-start.23
  100.2 0.9 collective-permute-start.22
  101.2 1.2 collective-permute-start.24
  102.4 3.3 %collective-permute-start.21 = (bf16[128,3584]{1,0:T(8,128)(2,1)S(1)}, bf16[128,3584]{1,0:T(8,128)(2,1)S(1)}, u32[]{:S(2)}, u32[]{:S(2)}) collective-permute-start(bf16[128,3584]{1,0:T(8,128)(2,1)S(1)} %copy-done.16), channel_id=1, source_target_pairs={{0,128},{128,0},{1,129},{129,1},{2,130},{130,2},{3,131},{131,3},{4... | collective-permute-start | bytes 2752520 | tf_op jit(solution)/shard_map/ppermute | solution.py:323
  105.8 11.8 %collective-permute-done.22 = bf16[5,32,896]{2,1,0:T(8,128)(2,1)S(1)} collective-permute-done((bf16[5,32,896]{2,1,0:T(8,128)(2,1)S(1)}, bf16[5,32,896]{2,1,0:T(8,128)(2,1)S(1)}, u32[]{:S(2)}, u32[]{:S(2)}) %collective-permute-start.22) | collective-permute-done | bytes 286752 | tf_op jit(solution)/shard_map/ppermute | solution.py:29
  118.4 1.5 collective-permute-start.28
  120.7 4.0 %collective-permute-done.28 = bf16[3,32,896]{2,1,0:T(8,128)(2,1)S(1)} collective-permute-done((bf16[3,32,896]{2,1,0:T(8,128)(2,1)S(1)}, bf16[3,32,896]{2,1,0:T(8,128)(2,1)S(1)}, u32[]{:S(2)}, u32[]{:S(2)}) %collective-permute-start.28) | collective-permute-done | bytes 172064 | tf_op jit(solution)/shard_map/ppermute | solution.py:29
  124.7 2.1 %collective-permute-done.29 = bf16[3,32,896]{2,1,0:T(8,128)(2,1)S(1)} collective-permute-done((bf16[3,32,896]{2,1,0:T(8,128)(2,1)S(1)}, bf16[3,32,896]{2,1,0:T(8,128)(2,1)S(1)}, u32[]{:S(2)}, u32[]{:S(2)}) %collective-permute-start.29) | collective-permute-done | bytes 172064 | tf_op jit(solution)/shard_map/ppermute | solution.py:29
  126.7 1.2 collective-permute-start.32
  128.0 1.0 add_convert_fusion.1
  129.0 1.0 copy-done.13
  130.0 5.5 %swapped.1 = (bf16[2,8,448,128]{3,2,1,0:T(8,128)(2,1)}, bf16[2,8,448,128]{3,2,1,0:T(8,128)(2,1)}, bf16[2,128,3584]{2,1,0:T(8,128)(2,1)}) custom-call(s32[5]{0:T(128)} %copy-done.5, s32[32]{0:T(128)} %slots.5, bf16[2,8,448,128]{3,2,1,0:T(8,128)(2,1)} %bitcast.79, bf16[2,8,448,128]{3,2,1,0:T(8,128)(2,1)} %bitcast.83, bf16[2,128,3584]{2,1,0:T(8,128)(2,1)} %refs_2_.1, ...), custom_call_target="tpu_custom_call" | custom-call | bytes 11534336 | tf_op jit(solution)/shard_map/swapped/pallas_call | solution.py:189
  135.5 2.8 %collective-permute-done.31 = bf16[2,32,896]{2,1,0:T(8,128)(2,1)S(1)} collective-permute-done((bf16[2,32,896]{2,1,0:T(8,128)(2,1)S(1)}, bf16[2,32,896]{2,1,0:T(8,128)(2,1)S(1)}, u32[]{:S(2)}, u32[]{:S(2)}) %collective-permute-start.31) | collective-permute-done | bytes 114720 | tf_op jit(solution)/shard_map/ppermute | solution.py:29
  139.0 1.4 collective-permute-start.34
  140.4 2.7 %reduce-scatter.2.cloned.1.call-done = bf16[1,4,32,896]{3,2,1,0:T(8,128)(2,1)} async-done(((bf16[8,4,32,896]{3,2,1,0:T(8,128)(2,1)}), bf16[1,4,32,896]{3,2,1,0:T(8,128)(2,1)}) %reduce-scatter.2.cloned.1.call-update) | async-done | bytes 229392 | tf_op jit(solution)/shard_map/reduce_scatter | solution.py:328
  143.2 0.9 slice_bitcast_fusion.3
  144.1 3.4 %collective-permute-start.25 = (bf16[32,896]{1,0:T(8,128)(2,1)S(1)}, bf16[32,896]{1,0:T(8,128)(2,1)S(1)}, u32[]{:S(2)}, u32[]{:S(2)}) collective-permute-start(bf16[32,896]{1,0:T(8,128)(2,1)S(1)} %get-tuple-element.82), channel_id=1, source_target_pairs={{0,6},{2,0},{4,2},{6,4},{1,7},{3,1},{5,3},{7,5},{8,14},{10,8},{12,... | collective-permute-start | bytes 172040 | tf_op jit(solution)/shard_map/ppermute | solution.py:29
  147.4 1.1 collective-permute-start.26
  148.5 1.2 collective-permute-start.27
  149.8 3.3 %collective-permute-done.26 = bf16[32,896]{1,0:T(8,128)(2,1)S(1)} collective-permute-done((bf16[32,896]{1,0:T(8,128)(2,1)S(1)}, bf16[32,896]{1,0:T(8,128)(2,1)S(1)}, u32[]{:S(2)}, u32[]{:S(2)}) %collective-permute-start.26) | collective-permute-done | bytes 57376 | tf_op jit(solution)/shard_map/ppermute | solution.py:29
  153.9 0.9 fusion.2
  154.9 1.7 collective-permute-start.36
  156.6 2.7 %collective-permute-start.37 = (bf16[2,16,448]{2,1,0:T(8,128)(2,1)S(1)}, bf16[2,16,448]{2,1,0:T(8,128)(2,1)S(1)}, u32[]{:S(2)}, u32[]{:S(2)}) collective-permute-start(bf16[2,16,448]{2,1,0:T(8,128)(2,1)S(1)} %get-tuple-element.88), channel_id=1, source_target_pairs={{0,1},{1,128},{128,129},{129,0},{2,3},{3,130},{130,131},{131,2},{4... | collective-permute-start | bytes 86024 | tf_op jit(solution)/shard_map/ppermute | solution.py:29
  160.9 3.5 %collective-permute-done.35 = bf16[2,16,448]{2,1,0:T(8,128)(2,1)S(1)} collective-permute-done((bf16[2,16,448]{2,1,0:T(8,128)(2,1)S(1)}, bf16[2,16,448]{2,1,0:T(8,128)(2,1)S(1)}, u32[]{:S(2)}, u32[]{:S(2)}) %collective-permute-start.35) | collective-permute-done | bytes 28704 | tf_op jit(solution)/shard_map/ppermute | solution.py:29
  (101 shorter events, 15.4 us)
Async XLA Ops:
  7.2 77.3 %all-gather.3.cloned.1.call-start = ((), (), s32[]{:S(2)}) async-start(), calls=%async_computation.2 | async-start | bytes 2359296 | tf_op jit(solution)/shard_map/all_gather | solution.py:319
  7.2 11.7 %collective-permute-start.3 = (bf16[2,8,448,128]{3,2,1,0:T(8,128)(2,1)}, bf16[2,8,448,128]{3,2,1,0:T(8,128)(2,1)}, u32[]{:S(2)}, u32[]{:S(2)}) collective-permute-start(bf16[2,8,448,128]{3,2,1,0:T(8,128)(2,1)} %bitcast.76), channel_id=1, source_target_pairs={{0,8},{8,0},{1,9},{9,1},{2,10},{10,2},{3,11},{11,3},{4,12},{12,4},... | collective-permute-start | bytes 5505032 | tf_op jit(solution)/shard_map/ppermute | solution.py:311
  7.3 20.7 %collective-permute-start.17 = (bf16[2,8,448,128]{3,2,1,0:T(8,128)(2,1)}, bf16[2,8,448,128]{3,2,1,0:T(8,128)(2,1)}, u32[]{:S(2)}, u32[]{:S(2)}) collective-permute-start(bf16[2,8,448,128]{3,2,1,0:T(8,128)(2,1)} %bitcast.80), channel_id=1, source_target_pairs={{0,8},{8,0},{1,9},{9,1},{2,10},{10,2},{3,11},{11,3},{4,12},{12,4},... | collective-permute-start | bytes 5505032 | tf_op jit(solution)/shard_map/ppermute | solution.py:311
  10.9 4.3 %collective-permute-start = (bf16[2,16,512]{2,1,0:T(8,128)(2,1)S(1)}, bf16[2,16,512]{2,1,0:T(8,128)(2,1)S(1)}, u32[]{:S(2)}, u32[]{:S(2)}) collective-permute-start(bf16[2,16,512]{2,1,0:T(8,128)(2,1)S(1)} %ride.1.refs_0_.refs_1_), channel_id=1, source_target_pairs={{0,1},{1,128},{128,129},{129,0},{2,3},{3,130},{130,131},{131,2},{4... | collective-permute-start | bytes 98312 | tf_op jit(solution)/shard_map/ppermute | solution.py:29
  12.9 5.4 %collective-permute-start.1 = (bf16[2,16,512]{2,1,0:T(8,128)(2,1)S(1)}, bf16[2,16,512]{2,1,0:T(8,128)(2,1)S(1)}, u32[]{:S(2)}, u32[]{:S(2)}) collective-permute-start(bf16[2,16,512]{2,1,0:T(8,128)(2,1)S(1)} %ride.1.refs_0_.refs_1_), channel_id=1, source_target_pairs={{0,128},{1,129},{128,0},{129,1},{2,130},{3,131},{130,2},{131,3},{4... | collective-permute-start | bytes 98312 | tf_op jit(solution)/shard_map/ppermute | solution.py:29
  13.8 5.1 %collective-permute-start.2 = (bf16[2,16,512]{2,1,0:T(8,128)(2,1)S(1)}, bf16[2,16,512]{2,1,0:T(8,128)(2,1)S(1)}, u32[]{:S(2)}, u32[]{:S(2)}) collective-permute-start(bf16[2,16,512]{2,1,0:T(8,128)(2,1)S(1)} %ride.1.refs_0_.refs_1_), channel_id=1, source_target_pairs={{0,129},{1,0},{128,1},{129,128},{2,131},{3,2},{130,3},{131,130},{4... | collective-permute-start | bytes 98312 | tf_op jit(solution)/shard_map/ppermute | solution.py:29
  19.5 20.4 %copy-start = (bf16[32,1024]{1,0:T(8,128)(2,1)}, bf16[32,1024]{1,0:T(8,128)(2,1)S(1)}, u32[]{:S(2)}) copy-start(bf16[32,1024]{1,0:T(8,128)(2,1)S(1)} %get-tuple-element.44.refs_2_) | copy-start | bytes 196612
  19.5 8.6 %collective-permute-start.14 = (bf16[32,1024]{1,0:T(8,128)(2,1)S(1)}, bf16[32,1024]{1,0:T(8,128)(2,1)S(1)}, u32[]{:S(2)}, u32[]{:S(2)}) collective-permute-start(bf16[32,1024]{1,0:T(8,128)(2,1)S(1)} %get-tuple-element.55), channel_id=1, source_target_pairs={{0,2},{2,4},{4,6},{6,0},{1,3},{3,5},{5,7},{7,1},{8,10},{10,12},{12... | collective-permute-start | bytes 196616 | tf_op jit(solution)/shard_map/ppermute | solution.py:29
  21.0 7.0 %collective-permute-start.15 = (bf16[32,1024]{1,0:T(8,128)(2,1)S(1)}, bf16[32,1024]{1,0:T(8,128)(2,1)S(1)}, u32[]{:S(2)}, u32[]{:S(2)}) collective-permute-start(bf16[32,1024]{1,0:T(8,128)(2,1)S(1)} %get-tuple-element.55), channel_id=1, source_target_pairs={{0,4},{2,6},{4,0},{6,2},{1,5},{3,7},{5,1},{7,3},{8,12},{10,14},{12... | collective-permute-start | bytes 196616 | tf_op jit(solution)/shard_map/ppermute | solution.py:29
  23.8 4.3 %collective-permute-start.16 = (bf16[32,1024]{1,0:T(8,128)(2,1)S(1)}, bf16[32,1024]{1,0:T(8,128)(2,1)S(1)}, u32[]{:S(2)}, u32[]{:S(2)}) collective-permute-start(bf16[32,1024]{1,0:T(8,128)(2,1)S(1)} %get-tuple-element.55), channel_id=1, source_target_pairs={{0,6},{2,0},{4,2},{6,4},{1,7},{3,1},{5,3},{7,5},{8,14},{10,8},{12,... | collective-permute-start | bytes 196616 | tf_op jit(solution)/shard_map/ppermute | solution.py:29
  28.8 114.3 %reduce-scatter.2.cloned.1.call-start = ((), (), s32[]{:S(2)}) async-start(), calls=%async_computation.1 | async-start | bytes 2064384 | tf_op jit(solution)/shard_map/reduce_scatter | solution.py:328
  28.9 14.1 %collective-permute-start.8 = (bf16[2,128,3584]{2,1,0:T(8,128)(2,1)S(1)}, bf16[2,128,3584]{2,1,0:T(8,128)(2,1)}, u32[]{:S(2)}, u32[]{:S(2)}) collective-permute-start(bf16[2,128,3584]{2,1,0:T(8,128)(2,1)S(1)} %copy-done.10), channel_id=1, source_target_pairs={{0,8},{8,0},{1,9},{9,1},{2,10},{10,2},{3,11},{11,3},{4,12},{12,4},... | collective-permute-start | bytes 5505032 | tf_op jit(solution)/shard_map/ppermute | solution.py:311
  29.0 34.1 %collective-permute-start.4 = (bf16[8,448,128]{2,1,0:T(8,128)(2,1)}, bf16[8,448,128]{2,1,0:T(8,128)(2,1)S(1)}, u32[]{:S(2)}, u32[]{:S(2)}) collective-permute-start(bf16[8,448,128]{2,1,0:T(8,128)(2,1)} %handed.3), channel_id=1, source_target_pairs={{0,128},{128,0},{1,129},{129,1},{2,130},{130,2},{3,131},{131,3},{4... | collective-permute-start | bytes 2752520 | tf_op jit(solution)/shard_map/ppermute | solution.py:318
  29.4 13.6 %collective-permute-start.5 = (bf16[32,1024]{1,0:T(8,128)(2,1)S(1)}, bf16[32,1024]{1,0:T(8,128)(2,1)S(1)}, u32[]{:S(2)}, u32[]{:S(2)}) collective-permute-start(bf16[32,1024]{1,0:T(8,128)(2,1)S(1)} %get-tuple-element.44.refs_2_), channel_id=1, source_target_pairs={{0,16},{16,32},{32,48},{48,64},{64,80},{80,96},{96,112},{112,0},{1... | collective-permute-start | bytes 196616 | tf_op jit(solution)/shard_map/ppermute | solution.py:29
  31.3 11.7 %collective-permute-start.6 = (bf16[32,1024]{1,0:T(8,128)(2,1)S(1)}, bf16[32,1024]{1,0:T(8,128)(2,1)S(1)}, u32[]{:S(2)}, u32[]{:S(2)}) collective-permute-start(bf16[32,1024]{1,0:T(8,128)(2,1)S(1)} %get-tuple-element.44.refs_2_), channel_id=1, source_target_pairs={{0,112},{16,0},{32,16},{48,32},{64,48},{80,64},{96,80},{112,96},{1... | collective-permute-start | bytes 196616 | tf_op jit(solution)/shard_map/ppermute | solution.py:29
  35.2 8.9 %collective-permute-start.7 = (bf16[32,1024]{1,0:T(8,128)(2,1)S(1)}, bf16[32,1024]{1,0:T(8,128)(2,1)S(1)}, u32[]{:S(2)}, u32[]{:S(2)}) collective-permute-start(bf16[32,1024]{1,0:T(8,128)(2,1)S(1)} %get-tuple-element.44.refs_2_), channel_id=1, source_target_pairs={{0,64},{16,80},{32,96},{48,112},{64,0},{80,16},{96,32},{112,48},{1... | collective-permute-start | bytes 196616 | tf_op jit(solution)/shard_map/ppermute | solution.py:29
  42.9 42.3 %copy-start.6 = (s32[5]{0:T(128)S(1)}, s32[5]{0:T(128)}, u32[]{:S(2)}) copy-start(s32[5]{0:T(128)} %copy-done.5) | copy-start | bytes 64
  42.9 42.3 %copy-start.9 = (s32[64]{0:T(128)S(1)}, s32[64]{0:T(128)}, u32[]{:S(2)}) copy-start(s32[64]{0:T(128)} %param.11) | copy-start | bytes 772
  45.0 18.2 %copy-start.17 = (bf16[8,448,128]{2,1,0:T(8,128)(2,1)S(1)}, bf16[8,448,128]{2,1,0:T(8,128)(2,1)}, u32[]{:S(2)}) copy-start(bf16[8,448,128]{2,1,0:T(8,128)(2,1)} %get-tuple-element.53) | copy-start | bytes 2752516
  45.0 18.1 %collective-permute-start.11 = (bf16[4,32,1024]{2,1,0:T(8,128)(2,1)S(1)}, bf16[4,32,1024]{2,1,0:T(8,128)(2,1)S(1)}, u32[]{:S(2)}, u32[]{:S(2)}) collective-permute-start(bf16[4,32,1024]{2,1,0:T(8,128)(2,1)S(1)} %join.3.refs_0_), channel_id=1, source_target_pairs={{0,2},{2,4},{4,6},{6,0},{1,3},{3,5},{5,7},{7,1},{8,10},{10,12},{12... | collective-permute-start | bytes 786440 | tf_op jit(solution)/shard_map/ppermute | solution.py:29
  45.6 17.4 %collective-permute-start.12 = (bf16[4,32,1024]{2,1,0:T(8,128)(2,1)S(1)}, bf16[4,32,1024]{2,1,0:T(8,128)(2,1)S(1)}, u32[]{:S(2)}, u32[]{:S(2)}) collective-permute-start(bf16[4,32,1024]{2,1,0:T(8,128)(2,1)S(1)} %join.3.refs_0_), channel_id=1, source_target_pairs={{0,6},{2,0},{4,2},{6,4},{1,7},{3,1},{5,3},{7,5},{8,14},{10,8},{12,... | collective-permute-start | bytes 786440 | tf_op jit(solution)/shard_map/ppermute | solution.py:29
  49.2 10.3 %collective-permute-start.10 = (bf16[2,32,1024]{2,1,0:T(8,128)(2,1)S(1)}, bf16[2,32,1024]{2,1,0:T(8,128)(2,1)S(1)}, u32[]{:S(2)}, u32[]{:S(2)}) collective-permute-start(bf16[2,32,1024]{2,1,0:T(8,128)(2,1)S(1)} %get-tuple-element.89), channel_id=1, source_target_pairs={{0,96},{16,112},{32,0},{48,16},{64,32},{80,48},{96,64},{112,80},{1... | collective-permute-start | bytes 393224 | tf_op jit(solution)/shard_map/ppermute | solution.py:29
  51.0 12.0 %collective-permute-start.9 = (bf16[2,32,1024]{2,1,0:T(8,128)(2,1)S(1)}, bf16[2,32,1024]{2,1,0:T(8,128)(2,1)S(1)}, u32[]{:S(2)}, u32[]{:S(2)}) collective-permute-start(bf16[2,32,1024]{2,1,0:T(8,128)(2,1)S(1)} %get-tuple-element.90), channel_id=1, source_target_pairs={{0,32},{16,48},{32,64},{48,80},{64,96},{80,112},{96,0},{112,16},{1... | collective-permute-start | bytes 393224 | tf_op jit(solution)/shard_map/ppermute | solution.py:29
  63.1 22.1 %copy-start.2 = (bf16[8,32,1024]{2,1,0:T(8,128)(2,1)}, bf16[8,32,1024]{2,1,0:T(8,128)(2,1)S(1)}, u32[]{:S(2)}) copy-start(bf16[8,32,1024]{2,1,0:T(8,128)(2,1)S(1)} %join.5.refs_1_) | copy-start | bytes 1572868
  63.1 35.5 %copy-start.11 = (bf16[8,448,128]{2,1,0:T(8,128)(2,1)}, bf16[8,448,128]{2,1,0:T(8,128)(2,1)S(1)}, u32[]{:S(2)}) copy-start(bf16[8,448,128]{2,1,0:T(8,128)(2,1)S(1)} %collective-permute-done.4.refs_3_) | copy-start | bytes 2752516
  63.1 20.4 %collective-permute-start.13 = (bf16[8,448,128]{2,1,0:T(8,128)(2,1)S(1)}, bf16[8,448,128]{2,1,0:T(8,128)(2,1)S(1)}, u32[]{:S(2)}, u32[]{:S(2)}) collective-permute-start(bf16[8,448,128]{2,1,0:T(8,128)(2,1)S(1)} %copy-done.17), channel_id=1, source_target_pairs={{0,128},{128,0},{1,129},{129,1},{2,130},{130,2},{3,131},{131,3},{4... | collective-permute-start | bytes 2752520 | tf_op jit(solution)/shard_map/ppermute | solution.py:322
  66.3 18.1 %collective-permute-start.19 = (bf16[8,32,1024]{2,1,0:T(8,128)(2,1)S(1)}, bf16[8,32,1024]{2,1,0:T(8,128)(2,1)S(1)}, u32[]{:S(2)}, u32[]{:S(2)}) collective-permute-start(bf16[8,32,1024]{2,1,0:T(8,128)(2,1)S(1)} %join.5.refs_1_), channel_id=1, source_target_pairs={{0,4},{2,6},{4,0},{6,2},{1,5},{3,7},{5,1},{7,3},{8,12},{10,14},{12... | collective-permute-start | bytes 1572872 | tf_op jit(solution)/shard_map/ppermute | solution.py:29
  67.4 16.2 %collective-permute-start.18 = (bf16[4,32,1024]{2,1,0:T(8,128)(2,1)S(1)}, bf16[4,32,1024]{2,1,0:T(8,128)(2,1)S(1)}, u32[]{:S(2)}, u32[]{:S(2)}) collective-permute-start(bf16[4,32,1024]{2,1,0:T(8,128)(2,1)S(1)} %join.4.refs_1_), channel_id=1, source_target_pairs={{0,2},{2,4},{4,6},{6,0},{1,3},{3,5},{5,7},{7,1},{8,10},{10,12},{12... | collective-permute-start | bytes 786440 | tf_op jit(solution)/shard_map/ppermute | solution.py:29
  68.8 14.9 %collective-permute-start.20 = (bf16[4,32,1024]{2,1,0:T(8,128)(2,1)S(1)}, bf16[4,32,1024]{2,1,0:T(8,128)(2,1)S(1)}, u32[]{:S(2)}, u32[]{:S(2)}) collective-permute-start(bf16[4,32,1024]{2,1,0:T(8,128)(2,1)S(1)} %join.4.refs_1_), channel_id=1, source_target_pairs={{0,6},{2,0},{4,2},{6,4},{1,7},{3,1},{5,3},{7,5},{8,14},{10,8},{12,... | collective-permute-start | bytes 786440 | tf_op jit(solution)/shard_map/ppermute | solution.py:29
  98.7 21.7 %copy-start.14 = (bf16[8,32,896]{2,1,0:T(8,128)(2,1)S(1)}, bf16[8,32,896]{2,1,0:T(8,128)(2,1)}, u32[]{:S(2)}) copy-start(bf16[8,32,896]{2,1,0:T(8,128)(2,1)} %get-tuple-element.61) | copy-start | bytes 1376260
  98.8 21.6 %collective-permute-start.23 = (bf16[8,32,896]{2,1,0:T(8,128)(2,1)}, bf16[8,32,896]{2,1,0:T(8,128)(2,1)S(1)}, u32[]{:S(2)}, u32[]{:S(2)}) collective-permute-start(bf16[8,32,896]{2,1,0:T(8,128)(2,1)} %get-tuple-element.63), channel_id=1, source_target_pairs={{0,4},{2,6},{4,0},{6,2},{1,5},{3,7},{5,1},{7,3},{8,12},{10,14},{12... | collective-permute-start | bytes 1376264 | tf_op jit(solution)/shard_map/ppermute | solution.py:29
  100.2 17.3 %collective-permute-start.22 = (bf16[5,32,896]{2,1,0:T(8,128)(2,1)S(1)}, bf16[5,32,896]{2,1,0:T(8,128)(2,1)S(1)}, u32[]{:S(2)}, u32[]{:S(2)}) collective-permute-start(bf16[5,32,896]{2,1,0:T(8,128)(2,1)S(1)} %get-tuple-element.62), channel_id=1, source_target_pairs={{0,6},{2,0},{4,2},{6,4},{1,7},{3,1},{5,3},{7,5},{8,14},{10,8},{12,... | collective-permute-start | bytes 860168 | tf_op jit(solution)/shard_map/ppermute | solution.py:29
  101.2 17.2 %collective-permute-start.24 = (bf16[5,32,896]{2,1,0:T(8,128)(2,1)S(1)}, bf16[5,32,896]{2,1,0:T(8,128)(2,1)S(1)}, u32[]{:S(2)}, u32[]{:S(2)}) collective-permute-start(bf16[5,32,896]{2,1,0:T(8,128)(2,1)S(1)} %get-tuple-element.64), channel_id=1, source_target_pairs={{0,2},{2,4},{4,6},{6,0},{1,3},{3,5},{5,7},{7,1},{8,10},{10,12},{12... | collective-permute-start | bytes 860168 | tf_op jit(solution)/shard_map/ppermute | solution.py:29
  102.4 26.5 %collective-permute-start.21 = (bf16[128,3584]{1,0:T(8,128)(2,1)S(1)}, bf16[128,3584]{1,0:T(8,128)(2,1)S(1)}, u32[]{:S(2)}, u32[]{:S(2)}) collective-permute-start(bf16[128,3584]{1,0:T(8,128)(2,1)S(1)} %copy-done.16), channel_id=1, source_target_pairs={{0,128},{128,0},{1,129},{129,1},{2,130},{130,2},{3,131},{131,3},{4... | collective-permute-start | bytes 2752520 | tf_op jit(solution)/shard_map/ppermute | solution.py:323
  105.8 53.5 %collective-permute-start.38 = (f32[64]{0:T(128)S(1)}, f32[64]{0:T(128)S(1)}, u32[]{:S(2)}, u32[]{:S(2)}) collective-permute-start(f32[64]{0:T(128)S(1)} %slice_bitcast_fusion.4), channel_id=1, source_target_pairs={{0,8},{8,0},{1,9},{9,1},{2,10},{10,2},{3,11},{11,3},{4,12},{12,4},... | collective-permute-start | bytes 776 | tf_op jit(solution)/shard_map/ppermute | solution.py:335
  118.4 6.3 %collective-permute-start.28 = (bf16[3,32,896]{2,1,0:T(8,128)(2,1)S(1)}, bf16[3,32,896]{2,1,0:T(8,128)(2,1)S(1)}, u32[]{:S(2)}, u32[]{:S(2)}) collective-permute-start(bf16[3,32,896]{2,1,0:T(8,128)(2,1)S(1)} %get-tuple-element.71), channel_id=1, source_target_pairs={{0,6},{2,0},{4,2},{6,4},{1,7},{3,1},{5,3},{7,5},{8,14},{10,8},{12,... | collective-permute-start | bytes 516104 | tf_op jit(solution)/shard_map/ppermute | solution.py:29
  119.8 6.9 %collective-permute-start.29 = (bf16[3,32,896]{2,1,0:T(8,128)(2,1)S(1)}, bf16[3,32,896]{2,1,0:T(8,128)(2,1)S(1)}, u32[]{:S(2)}, u32[]{:S(2)}) collective-permute-start(bf16[3,32,896]{2,1,0:T(8,128)(2,1)S(1)} %get-tuple-element.73), channel_id=1, source_target_pairs={{0,2},{2,4},{4,6},{6,0},{1,3},{3,5},{5,7},{7,1},{8,10},{10,12},{12... | collective-permute-start | bytes 516104 | tf_op jit(solution)/shard_map/ppermute | solution.py:29
  120.6 14.9 %collective-permute-start.30 = (bf16[2,32,896]{2,1,0:T(8,128)(2,1)S(1)}, bf16[2,32,896]{2,1,0:T(8,128)(2,1)S(1)}, u32[]{:S(2)}, u32[]{:S(2)}) collective-permute-start(bf16[2,32,896]{2,1,0:T(8,128)(2,1)S(1)} %get-tuple-element.80), channel_id=1, source_target_pairs={{0,96},{16,112},{32,0},{48,16},{64,32},{80,48},{96,64},{112,80},{1... | collective-permute-start | bytes 344072 | tf_op jit(solution)/shard_map/ppermute | solution.py:29
  124.7 13.6 %collective-permute-start.31 = (bf16[2,32,896]{2,1,0:T(8,128)(2,1)S(1)}, bf16[2,32,896]{2,1,0:T(8,128)(2,1)S(1)}, u32[]{:S(2)}, u32[]{:S(2)}) collective-permute-start(bf16[2,32,896]{2,1,0:T(8,128)(2,1)S(1)} %get-tuple-element.81), channel_id=1, source_target_pairs={{0,32},{16,48},{32,64},{48,80},{64,96},{80,112},{96,0},{112,16},{1... | collective-permute-start | bytes 344072 | tf_op jit(solution)/shard_map/ppermute | solution.py:29
  126.7 20.7 %collective-permute-start.32 = (bf16[32,896]{1,0:T(8,128)(2,1)S(1)}, bf16[32,896]{1,0:T(8,128)(2,1)S(1)}, u32[]{:S(2)}, u32[]{:S(2)}) collective-permute-start(bf16[32,896]{1,0:T(8,128)(2,1)S(1)} %slice_bitcast_fusion), channel_id=1, source_target_pairs={{0,64},{16,80},{32,96},{48,112},{64,0},{80,16},{96,32},{112,48},{1... | collective-permute-start | bytes 172040 | tf_op jit(solution)/shard_map/ppermute | solution.py:29
  138.3 10.2 %collective-permute-start.33 = (bf16[32,896]{1,0:T(8,128)(2,1)S(1)}, bf16[32,896]{1,0:T(8,128)(2,1)S(1)}, u32[]{:S(2)}, u32[]{:S(2)}) collective-permute-start(bf16[32,896]{1,0:T(8,128)(2,1)S(1)} %get-tuple-element.85), channel_id=1, source_target_pairs={{0,112},{16,0},{32,16},{48,32},{64,48},{80,64},{96,80},{112,96},{1... | collective-permute-start | bytes 172040 | tf_op jit(solution)/shard_map/ppermute | solution.py:29
  139.0 10.8 %collective-permute-start.34 = (bf16[32,896]{1,0:T(8,128)(2,1)S(1)}, bf16[32,896]{1,0:T(8,128)(2,1)S(1)}, u32[]{:S(2)}, u32[]{:S(2)}) collective-permute-start(bf16[32,896]{1,0:T(8,128)(2,1)S(1)} %get-tuple-element.86), channel_id=1, source_target_pairs={{0,16},{16,32},{32,48},{48,64},{64,80},{80,96},{96,112},{112,0},{1... | collective-permute-start | bytes 172040 | tf_op jit(solution)/shard_map/ppermute | solution.py:29
  144.1 5.7 %collective-permute-start.25 = (bf16[32,896]{1,0:T(8,128)(2,1)S(1)}, bf16[32,896]{1,0:T(8,128)(2,1)S(1)}, u32[]{:S(2)}, u32[]{:S(2)}) collective-permute-start(bf16[32,896]{1,0:T(8,128)(2,1)S(1)} %get-tuple-element.82), channel_id=1, source_target_pairs={{0,6},{2,0},{4,2},{6,4},{1,7},{3,1},{5,3},{7,5},{8,14},{10,8},{12,... | collective-permute-start | bytes 172040 | tf_op jit(solution)/shard_map/ppermute | solution.py:29
  147.4 5.7 %collective-permute-start.26 = (bf16[32,896]{1,0:T(8,128)(2,1)S(1)}, bf16[32,896]{1,0:T(8,128)(2,1)S(1)}, u32[]{:S(2)}, u32[]{:S(2)}) collective-permute-start(bf16[32,896]{1,0:T(8,128)(2,1)S(1)} %get-tuple-element.84), channel_id=1, source_target_pairs={{0,4},{2,6},{4,0},{6,2},{1,5},{3,7},{5,1},{7,3},{8,12},{10,14},{12... | collective-permute-start | bytes 172040 | tf_op jit(solution)/shard_map/ppermute | solution.py:29
  148.5 5.4 %collective-permute-start.27 = (bf16[32,896]{1,0:T(8,128)(2,1)S(1)}, bf16[32,896]{1,0:T(8,128)(2,1)S(1)}, u32[]{:S(2)}, u32[]{:S(2)}) collective-permute-start(bf16[32,896]{1,0:T(8,128)(2,1)S(1)} %get-tuple-element.83), channel_id=1, source_target_pairs={{0,2},{2,4},{4,6},{6,0},{1,3},{3,5},{5,7},{7,1},{8,10},{10,12},{12... | collective-permute-start | bytes 172040 | tf_op jit(solution)/shard_map/ppermute | solution.py:29
  154.9 5.6 %collective-permute-start.36 = (bf16[2,16,448]{2,1,0:T(8,128)(2,1)S(1)}, bf16[2,16,448]{2,1,0:T(8,128)(2,1)S(1)}, u32[]{:S(2)}, u32[]{:S(2)}) collective-permute-start(bf16[2,16,448]{2,1,0:T(8,128)(2,1)S(1)} %get-tuple-element.87), channel_id=1, source_target_pairs={{0,128},{1,129},{128,0},{129,1},{2,130},{3,131},{130,2},{131,3},{4... | collective-permute-start | bytes 86024 | tf_op jit(solution)/shard_map/ppermute | solution.py:29
  156.6 4.3 %collective-permute-start.37 = (bf16[2,16,448]{2,1,0:T(8,128)(2,1)S(1)}, bf16[2,16,448]{2,1,0:T(8,128)(2,1)S(1)}, u32[]{:S(2)}, u32[]{:S(2)}) collective-permute-start(bf16[2,16,448]{2,1,0:T(8,128)(2,1)S(1)} %get-tuple-element.88), channel_id=1, source_target_pairs={{0,1},{1,128},{128,129},{129,0},{2,3},{3,130},{130,131},{131,2},{4... | collective-permute-start | bytes 86024 | tf_op jit(solution)/shard_map/ppermute | solution.py:29
  159.3 5.1 %collective-permute-start.35 = (bf16[2,16,448]{2,1,0:T(8,128)(2,1)S(1)}, bf16[2,16,448]{2,1,0:T(8,128)(2,1)S(1)}, u32[]{:S(2)}, u32[]{:S(2)}) collective-permute-start(bf16[2,16,448]{2,1,0:T(8,128)(2,1)S(1)} %get-tuple-element.75), channel_id=1, source_target_pairs={{0,129},{1,0},{128,1},{129,128},{2,131},{3,2},{130,3},{131,130},{4... | collective-permute-start | bytes 86024 | tf_op jit(solution)/shard_map/ppermute | solution.py:29
  (12 other events, 62.9 us)
Sparse Core Ops, SparseCore 0:
  29.0 47.2 all-gather.2
  98.8 44.2 reduce-scatter.1

commit v6 on v5

--- a/solution.py
+++ b/solution.py
@@ -51,10 +51,9 @@
     back2 = send(jnp.stack([value, back]), "z", 2)
     ahead2 = send(jnp.stack([value, ahead]), "z", -2)
     early = run_join([value[None], back[None], ahead[None], far[None]])
-    before, behind = send(early, "x", 1), send(early, "x", -1)
-    late = after(run_join([back2, ahead2]), before, behind)
-    both = run_join([early, late])
-    return both, ((both,), (before, send(late, "x", 1)), (send(both, "x", 2),), (behind, send(late, "x", -1)))
+    over_x = gather_ring(early, "x")
+    late = after(run_join([back2, ahead2]), *over_x)
+    return late, tuple(zip(over_x, gather_ring(late, "x")))
 
 
 def run_join(parts):
@@ -138,71 +137,79 @@
     )(place, *from_y)
 
 
-def handed_kernel(place, slots, *refs):
-    count = (len(refs) - 2) // 3
-    slot, sems = slots[place[4]], refs[-1]
-    ins = [pltpu.make_async_copy(refs[k].at[slot], refs[2 * count + 1 + k], sems.at[k]) for k in range(count)]
-    outs = [pltpu.make_async_copy(refs[2 * count + 1 + k], refs[count + 1 + k], sems.at[count + k]) for k in range(count)]
-    for copy in ins:
+def swap_views(gate, up, down, slot, room):
+    views = [(gate.at[slot], room.at[:3584]), (up.at[slot], room.at[3584:7168])]
+    for c in range(28):
+        views.append((down.at[slot, :, c * 128 : (c + 1) * 128], room.at[7168 + c * 128 : 7296 + c * 128]))
+    return views
+
+
+def handed_kernel(place, slots, gate, up, down, earlier_ref, out, room, sems):
+    views = swap_views(gate, up, down, slots[place[4]], room)
+    copies = [pltpu.make_async_copy(source, to, sems.at[k]) for k, (source, to) in enumerate(views)]
+    for copy in copies:
         copy.start()
-    for copy_in, copy_out in zip(ins, outs):
-        copy_in.wait()
-        copy_out.start()
-    for copy in outs:
+    for copy in copies:
         copy.wait()
+    copy = pltpu.make_async_copy(room, out, sems.at[30])
+    copy.start()
+    copy.wait()
 
 
 def run_handed(place, slots, panels, earlier):
     hbm, smem = pl.BlockSpec(memory_space=pltpu.HBM), pl.BlockSpec(memory_space=pltpu.SMEM)
+    shape = (3 * 3584, 128)
     return pl.pallas_call(
         handed_kernel,
-        out_shape=[jax.ShapeDtypeStruct(p.shape[1:], p.dtype) for p in panels],
-        in_specs=[smem, smem] + [hbm] * (len(panels) + 1),
-        out_specs=[hbm] * len(panels),
-        scratch_shapes=[pltpu.VMEM(p.shape[1:], p.dtype) for p in panels]
-        + [pltpu.SemaphoreType.DMA((2 * len(panels),))],
+        out_shape=jax.ShapeDtypeStruct(shape, jnp.bfloat16),
+        in_specs=[smem, smem] + [hbm] * 4,
+        out_specs=hbm,
+        scratch_shapes=[pltpu.VMEM(shape, jnp.bfloat16), pltpu.SemaphoreType.DMA((31,))],
         compiler_params=LARGE,
-        cost_estimate=pl.CostEstimate(flops=0, bytes_accessed=2 * len(panels) * 2**20, transcendentals=0),
+        cost_estimate=pl.CostEstimate(flops=0, bytes_accessed=6 * 2**20, transcendentals=0),
         name="handed",
     )(place, slots, *panels, earlier)
 
 
-def swapped_kernel(place, slots, *refs):
+def swapped_kernel(place, slots, gate, up, down, taken, *refs):
+    outs, kept_rooms, room, sems = refs[:3], refs[3:6], refs[6], refs[7]
     slot = slots[place[4]]
-    ins, outs = [], []
-    for k in range(3):
-        panel, taken, out, room = refs[k], refs[3 + k], refs[6 + k], refs[9 + k]
-        for j, source, at in ((0, panel.at[1 - slot], 1 - slot), (1, taken, slot)):
-            ins.append(pltpu.make_async_copy(source, room.at[j], refs[12].at[2 * k + j]))
-            outs.append(pltpu.make_async_copy(room.at[j], out.at[at], refs[12].at[6 + 2 * k + j]))
-    for copy in ins:
+    arrive = [pltpu.make_async_copy(taken, room, sems.at[0])]
+    leave = [[pltpu.make_async_copy(r, o, sems.at[7 + k]) for k, (o, r) in enumerate(swap_views(*outs, slot, room))]]
+    for k, (panel, out, kept) in enumerate(zip((gate, up, down), outs, kept_rooms)):
+        arrive.append(pltpu.make_async_copy(panel.at[1 - slot], kept, sems.at[1 + k]))
+        leave.append([pltpu.make_async_copy(kept, out.at[1 - slot], sems.at[4 + k])])
+    for copy in arrive:
         copy.start()
-    for copy_in, copy_out in zip(ins, outs):
+    for copy_in, copies_out in zip(arrive, leave):
         copy_in.wait()
-        copy_out.start()
-    for copy in outs:
-        copy.wait()
+        for copy in copies_out:
+            copy.start()
+    for copies_out in leave:
+        for copy in copies_out:
+            copy.wait()
 
 
 def run_swapped(place, slots, panels, taken):
-    hbm = pl.BlockSpec(memory_space=pltpu.HBM)
+    hbm, smem = pl.BlockSpec(memory_space=pltpu.HBM), pl.BlockSpec(memory_space=pltpu.SMEM)
     return pl.pallas_call(
         swapped_kernel,
         out_shape=[jax.ShapeDtypeStruct(p.shape, p.dtype) for p in panels],
-        in_specs=[pl.BlockSpec(memory_space=pltpu.SMEM)] * 2 + [hbm] * 6,
+        in_specs=[smem, smem] + [hbm] * 4,
         out_specs=[hbm] * 3,
-        scratch_shapes=[pltpu.VMEM(p.shape, p.dtype) for p in panels] + [pltpu.SemaphoreType.DMA((12,))],
+        scratch_shapes=[pltpu.VMEM(p.shape[1:], p.dtype) for p in panels]
+        + [pltpu.VMEM(taken.shape, taken.dtype), pltpu.SemaphoreType.DMA((37,))],
         compiler_params=LARGE,
         cost_estimate=pl.CostEstimate(flops=0, bytes_accessed=11 * 2**20, transcendentals=0),
         name="swapped",
-    )(place, slots, *panels, *taken)
+    )(place, slots, *panels, taken)
 
 
 def layer_kernel(place, position_ref, *refs):
-    piece0, pieces1 = refs[0], ((refs[1],), refs[2:4], (refs[4],), refs[5:7])
-    gate_own, up_own, down_own, gate_other, up_other, down_other = refs[7:13]
-    out0, outs1, count_ref = refs[13], ((refs[14],), refs[15:17], (refs[17],), refs[18:20]), refs[20]
-    rows_ref, gate_ref, up_ref, down_ref, hidden_ref, result_ref, sems = refs[21:]
+    piece0, pieces1 = refs[0], (refs[1:3], refs[3:5], refs[5:7], refs[7:9])
+    gate_own, up_own, down_own, gate_other, up_other, down_other = refs[9:15]
+    out0, outs1, count_ref = refs[15], ((refs[16],), refs[17:19], (refs[19],), refs[20:22]), refs[22]
+    rows_ref, gate_ref, up_ref, down_ref, hidden_ref, result_ref, sems = refs[23:]
     my_x, my_core, chip = place[0], place[1], place[2]
     span = 2 * GROUP
 
@@ -280,7 +287,7 @@
         + [jax.ShapeDtypeStruct((n, 2 * GROUP, PAIR), jnp.bfloat16) for n in (8, 3, 5, 8, 3, 5)]
         + [jax.ShapeDtypeStruct((8, 64), jnp.float32)],
         in_specs=[pl.BlockSpec(memory_space=pltpu.SMEM)]
-        + [vmem] * 8
+        + [vmem] * 10
         + [pl.BlockSpec(memory_space=pltpu.HBM)] * 6,
         out_specs=[vmem] * 8,
         scratch_shapes=[
@@ -313,17 +320,15 @@
 
     lower = run_ride(place, tokens, routes, gate_fix)
     step_rows = run_merge(place, after(gather_ring(lower, Y), other[0]))
-    (gate_given,) = run_handed(place, swap_slot, panels[:1], lower)
-    from_x = after(gather_ring(step_rows[0], "x"), other[1], gate_given)
-    gate_taken = lax.ppermute(after(gate_given, *step_rows), "yh", swap_y)
+    whole = (w_gate, w_up, w_down)
+    given = run_handed(place, swap_slot, whole, step_rows[1])
+    from_x = after(gather_ring(step_rows[0], "x"), other[1])
     piece0 = lax.all_gather(jnp.stack(from_x), "z")
-    up_given, down_given = run_handed(place, swap_slot, panels[1:], step_rows[1])
-    over_z, pieces1 = gather_zx(step_rows[1], (up_given, down_given, other[2]))
-    up_taken = lax.ppermute(after(up_given, gate_taken, over_z), "yh", swap_y)
-    down_taken = lax.ppermute(after(down_given, up_taken), "yh", swap_y)
-    out0, out1, counts = run_layer(after(place, up_taken), position.reshape(1, 64), piece0, pieces1, weights)
+    over_z, pieces1 = gather_zx(step_rows[1], (given, other[2]))
+    taken = lax.ppermute(after(given, over_z), "yh", swap_y)
+    out0, out1, counts = run_layer(place, position.reshape(1, 64), piece0, pieces1, weights)
     back1, late = reduce_zx(out1)
-    new = run_swapped(place, swap_slot, panels, (gate_taken, up_taken, after(down_taken, late)))
+    new = run_swapped(place, swap_slot, whole, after(taken, back1))
 
     back0 = lax.psum_scatter(out0, "z", scatter_dimension=0)
     back0 = after(back0, *new)

time: 174 us -> 188 us (1.080)
  waiting for transfers between devices: 62.1 us -> 76.1 us
  Pallas kernels: 26.3 us -> 24.1 us
  starting transfers between devices: 56.6 us -> 58.6 us
    ppermute x32 -> x33, waiting for transfers between devices: 46.5 us -> 59.7 us  [send(): lax.ppermute(value, axes, [(i, (i + amount) % count) for i in range(count)])]
    ppermute x32 -> x33, starting transfers between devices: 48.9 us -> 56.3 us  [send(): lax.ppermute(value, axes, [(i, (i + amount) % count) for i in range(count)])]
    ppermute x3 -> x1, starting transfers between devices: 6.91 us -> 1.55 us  [on_device(): taken = lax.ppermute(after(given, over_z), 'yh', swap_y)]
    ppermute x3 -> x1, waiting for transfers between devices: 12.8 us -> 15.7 us  [on_device(): taken = lax.ppermute(after(given, over_z), 'yh', swap_y)]
    reduce_scatter x1, waiting for transfers between devices: 2.75 us -> 0.02 us  [on_device(): back0 = lax.psum_scatter(out0, 'z', scatter_dimension=0)]
    pallas_call x2 -> x1, Pallas kernels: 5.91 us -> 4.09 us  [run_handed(): pl.pallas_call(handed_kernel, out_shape=jax.ShapeDtypeStruct(shape, jnp.b...]
    unnamed x38 -> x26, local copies, waits for them, and re-layouts: 5.65 us -> 5.2 us
  transfers between devices with their start and end apart: 41 -> 40, of which waited for: 18 -> 22; matrix products, arithmetic and copies ran while one was open for 3% -> 3% of each run, Pallas kernels for 7% -> 6%
where the time goes in v6:
time: 188 us
  waiting for transfers between devices  76.1 us (40%)
  starting transfers between devices  58.6 us (31%)
  Pallas kernels  24.1 us (13%)
  between operations  16.1 us (9%)
  other arithmetic  6.43 us (3%)
  local copies, waits for them, and re-layouts  6.21 us (3%)
    ppermute x33, waiting for transfers between devices, send(): lax.ppermute(value, axes, [(i, (i + amount) % count) for i in range(count)])  59.7 us
    ppermute x33, starting transfers between devices, send(): lax.ppermute(value, axes, [(i, (i + amount) % count) for i in range(count)])  56.3 us
    ppermute x1, waiting for transfers between devices, on_device(): taken = lax.ppermute(after(given, over_z), 'yh', swap_y)  15.7 us
    pallas_call x1, Pallas kernels, run_layer(): pl.pallas_call(layer_kernel, out_shape=[jax.ShapeDtypeStruct((8, 4, 2 * G...  13.4 us
    unnamed x26, local copies, waits for them, and re-layouts  5.2 us
    pallas_call x1, Pallas kernels, run_swapped(): pl.pallas_call(swapped_kernel, out_shape=[jax.ShapeDtypeStruct(p.shape, p...  5.2 us
    pallas_call x1, Pallas kernels, run_handed(): pl.pallas_call(handed_kernel, out_shape=jax.ShapeDtypeStruct(shape, jnp.b...  4.09 us
    convert_element_type x6, other arithmetic, total(): functools.reduce(jnp.add, [v.astype(jnp.float32) for v in values])  4.01 us
  transfers between devices with their start and end apart: 40, of which 22 were waited for; matrix products, arithmetic and copies ran while one was open for 3% of the time, Pallas kernels for 6%

profile of v6, /device:TPU:24, one launch (start us, length us, event | category | flops | bytes accessed | tf_op | source)
XLA Modules:
  0.0 187.5 jit_solution(12596757254394681792)
XLA Ops:
  10.8 2.0 %collective-permute-start = (bf16[2,16,512]{2,1,0:T(8,128)(2,1)S(1)}, bf16[2,16,512]{2,1,0:T(8,128)(2,1)S(1)}, u32[]{:S(2)}, u32[]{:S(2)}) collective-permute-start(bf16[2,16,512]{2,1,0:T(8,128)(2,1)S(1)} %ride.1.refs_0_), channel_id=1, source_target_pairs={{0,1},{1,128},{128,129},{129,0},{2,3},{3,130},{130,131},{131,2},{4... | collective-permute-start | bytes 98312 | tf_op jit(solution)/shard_map/ppermute | solution.py:29
  12.8 0.9 collective-permute-start.1
  13.8 1.3 collective-permute-done.refs_1_
  15.1 3.1 %collective-permute-done.1.refs_2_ = bf16[2,16,512]{2,1,0:T(8,128)(2,1)S(1)} collective-permute-done((bf16[2,16,512]{2,1,0:T(8,128)(2,1)S(1)}, bf16[2,16,512]{2,1,0:T(8,128)(2,1)S(1)}, u32[]{:S(2)}, u32[]{:S(2)}) %collective-permute-start.1) | collective-permute-done | bytes 32800 | tf_op jit(solution)/shard_map/ppermute | solution.py:29
  19.4 1.6 collective-permute-start.4
  21.0 2.7 %collective-permute-start.5 = (bf16[32,1024]{1,0:T(8,128)(2,1)S(1)}, bf16[32,1024]{1,0:T(8,128)(2,1)S(1)}, u32[]{:S(2)}, u32[]{:S(2)}) collective-permute-start(bf16[32,1024]{1,0:T(8,128)(2,1)S(1)} %get-tuple-element.40), channel_id=1, source_target_pairs={{0,4},{2,6},{4,0},{6,2},{1,5},{3,7},{5,1},{7,3},{8,12},{10,14},{12... | collective-permute-start | bytes 196616 | tf_op jit(solution)/shard_map/ppermute | solution.py:29
  23.7 1.4 collective-permute-start.6
  25.1 1.6 collective-permute-done.5
  26.7 1.2 collective-permute-done.6
  28.9 7.3 %collective-permute-start.10 = (bf16[32,1024]{1,0:T(8,128)(2,1)S(1)}, bf16[32,1024]{1,0:T(8,128)(2,1)S(1)}, u32[]{:S(2)}, u32[]{:S(2)}) collective-permute-start(bf16[32,1024]{1,0:T(8,128)(2,1)S(1)} %get-tuple-element.44.earlier_ref), channel_id=1, source_target_pairs={{0,64},{16,80},{32,96},{48,112},{64,0},{80,16},{96,32},{112,48},{1... | collective-permute-start | bytes 196616 | tf_op jit(solution)/shard_map/ppermute | solution.py:29
  36.2 1.0 collective-permute-start.8
  37.2 2.2 %collective-permute-start.9 = (bf16[32,1024]{1,0:T(8,128)(2,1)S(1)}, bf16[32,1024]{1,0:T(8,128)(2,1)S(1)}, u32[]{:S(2)}, u32[]{:S(2)}) collective-permute-start(bf16[32,1024]{1,0:T(8,128)(2,1)S(1)} %get-tuple-element.44.earlier_ref), channel_id=1, source_target_pairs={{0,112},{16,0},{32,16},{48,32},{64,48},{80,64},{96,80},{112,96},{1... | collective-permute-start | bytes 196616 | tf_op jit(solution)/shard_map/ppermute | solution.py:29
  39.4 4.1 %handed.1 = bf16[10752,128]{1,0:T(8,128)(2,1)} custom-call(s32[5]{0:T(128)} %copy-done.3, s32[32]{0:T(128)} %slots.3, bf16[2,3584,128]{2,1,0:T(8,128)(2,1)} %gate.3, bf16[2,3584,128]{2,1,0:T(8,128)(2,1)} %up.3, bf16[2,128,3584]{2,1,0:T(8,128)(2,1)} %down.3, bf16[32,1024]{1,0:T(8,128)(2,1)} %copy-done), custom_call_target="tpu_custom_call" | custom-call | bytes 6291456 | tf_op jit(solution)/shard_map/handed/pallas_call | solution.py:162
  45.1 3.5 %collective-permute-start.15 = (bf16[4,32,1024]{2,1,0:T(8,128)(2,1)S(1)}, bf16[4,32,1024]{2,1,0:T(8,128)(2,1)S(1)}, u32[]{:S(2)}, u32[]{:S(2)}) collective-permute-start(bf16[4,32,1024]{2,1,0:T(8,128)(2,1)S(1)} %join.2.refs_1_), channel_id=1, source_target_pairs={{0,4},{2,6},{4,0},{6,2},{1,5},{3,7},{5,1},{7,3},{8,12},{10,14},{12... | collective-permute-start | bytes 786440 | tf_op jit(solution)/shard_map/ppermute | solution.py:29
  48.7 0.9 pad_maximum_fusion.1
  49.9 3.9 %collective-permute-start.13 = (bf16[2,32,1024]{2,1,0:T(8,128)(2,1)S(1)}, bf16[2,32,1024]{2,1,0:T(8,128)(2,1)S(1)}, u32[]{:S(2)}, u32[]{:S(2)}) collective-permute-start(bf16[2,32,1024]{2,1,0:T(8,128)(2,1)S(1)} %get-tuple-element.79), channel_id=1, source_target_pairs={{0,96},{16,112},{32,0},{48,16},{64,32},{80,48},{96,64},{112,80},{1... | collective-permute-start | bytes 393224 | tf_op jit(solution)/shard_map/ppermute | solution.py:29
  53.8 8.4 %collective-permute-done.12.refs_0_ = bf16[2,32,1024]{2,1,0:T(8,128)(2,1)S(1)} collective-permute-done((bf16[2,32,1024]{2,1,0:T(8,128)(2,1)S(1)}, bf16[2,32,1024]{2,1,0:T(8,128)(2,1)S(1)}, u32[]{:S(2)}, u32[]{:S(2)}) %collective-permute-start.12) | collective-permute-done | bytes 131104 | tf_op jit(solution)/shard_map/ppermute | solution.py:29
  62.2 1.9 %collective-permute-start.17 = (bf16[4,32,1024]{2,1,0:T(8,128)(2,1)S(1)}, bf16[4,32,1024]{2,1,0:T(8,128)(2,1)S(1)}, u32[]{:S(2)}, u32[]{:S(2)}) collective-permute-start(bf16[4,32,1024]{2,1,0:T(8,128)(2,1)S(1)} %join.3.refs_2_), channel_id=1, source_target_pairs={{0,2},{2,4},{4,6},{6,0},{1,3},{3,5},{5,7},{7,1},{8,10},{10,12},{12... | collective-permute-start | bytes 786440 | tf_op jit(solution)/shard_map/ppermute | solution.py:29
  64.5 2.5 %collective-permute-start.19 = (bf16[4,32,1024]{2,1,0:T(8,128)(2,1)S(1)}, bf16[4,32,1024]{2,1,0:T(8,128)(2,1)S(1)}, u32[]{:S(2)}, u32[]{:S(2)}) collective-permute-start(bf16[4,32,1024]{2,1,0:T(8,128)(2,1)S(1)} %join.3.refs_2_), channel_id=1, source_target_pairs={{0,6},{2,0},{4,2},{6,4},{1,7},{3,1},{5,3},{7,5},{8,14},{10,8},{12,... | collective-permute-start | bytes 786440 | tf_op jit(solution)/shard_map/ppermute | solution.py:29
  67.0 4.1 %collective-permute-done.17.refs_4_ = bf16[4,32,1024]{2,1,0:T(8,128)(2,1)S(1)} collective-permute-done((bf16[4,32,1024]{2,1,0:T(8,128)(2,1)S(1)}, bf16[4,32,1024]{2,1,0:T(8,128)(2,1)S(1)}, u32[]{:S(2)}, u32[]{:S(2)}) %collective-permute-start.17) | collective-permute-done | bytes 262176 | tf_op jit(solution)/shard_map/ppermute | solution.py:29
  71.2 4.6 %collective-permute-done.18.refs_6_ = bf16[4,32,1024]{2,1,0:T(8,128)(2,1)S(1)} collective-permute-done((bf16[4,32,1024]{2,1,0:T(8,128)(2,1)S(1)}, bf16[4,32,1024]{2,1,0:T(8,128)(2,1)S(1)}, u32[]{:S(2)}, u32[]{:S(2)}) %collective-permute-start.18) | collective-permute-done | bytes 262176 | tf_op jit(solution)/shard_map/ppermute | solution.py:29
  77.5 13.4 %layer.1 = (bf16[8,4,32,896]{3,2,1,0:T(8,128)(2,1)}, bf16[8,32,896]{2,1,0:T(8,128)(2,1)}, bf16[3,32,896]{2,1,0:T(8,128)(2,1)S(1)}, bf16[5,32,896]{2,1,0:T(8,128)...) custom-call(s32[5]{0:T(128)S(1)} %copy-done.4, ...), custom_call_target="tpu_custom_call" | custom-call | flops 5637144576 | bytes 20971520 | tf_op jit(solution)/shard_map/layer/pallas_call | solution.py:284
  91.0 1.5 collective-permute-start.20
  92.5 2.3 %collective-permute-start.24 = (bf16[8,32,896]{2,1,0:T(8,128)(2,1)}, bf16[8,32,896]{2,1,0:T(8,128)(2,1)}, u32[]{:S(2)}, u32[]{:S(2)}) collective-permute-start(bf16[8,32,896]{2,1,0:T(8,128)(2,1)} %get-tuple-element.56), channel_id=1, source_target_pairs={{0,4},{2,6},{4,0},{6,2},{1,5},{3,7},{5,1},{7,3},{8,12},{10,14},{12... | collective-permute-start | bytes 1376264 | tf_op jit(solution)/shard_map/ppermute | solution.py:29
  94.8 1.9 %collective-permute-start.21 = (bf16[5,32,896]{2,1,0:T(8,128)(2,1)}, bf16[5,32,896]{2,1,0:T(8,128)(2,1)S(1)}, u32[]{:S(2)}, u32[]{:S(2)}) collective-permute-start(bf16[5,32,896]{2,1,0:T(8,128)(2,1)} %get-tuple-element.53), channel_id=1, source_target_pairs={{0,6},{2,0},{4,2},{6,4},{1,7},{3,1},{5,3},{7,5},{8,14},{10,8},{12,... | collective-permute-start | bytes 860168 | tf_op jit(solution)/shard_map/ppermute | solution.py:29
  96.9 13.9 %collective-permute-done.21 = bf16[5,32,896]{2,1,0:T(8,128)(2,1)S(1)} collective-permute-done((bf16[5,32,896]{2,1,0:T(8,128)(2,1)}, bf16[5,32,896]{2,1,0:T(8,128)(2,1)S(1)}, u32[]{:S(2)}, u32[]{:S(2)}) %collective-permute-start.21) | collective-permute-done | bytes 286752 | tf_op jit(solution)/shard_map/ppermute | solution.py:29
  110.8 2.6 %collective-permute-start.23 = (bf16[3,32,896]{2,1,0:T(8,128)(2,1)S(1)}, bf16[3,32,896]{2,1,0:T(8,128)(2,1)S(1)}, u32[]{:S(2)}, u32[]{:S(2)}) collective-permute-start(bf16[3,32,896]{2,1,0:T(8,128)(2,1)S(1)} %get-tuple-element.55), channel_id=1, source_target_pairs={{0,6},{2,0},{4,2},{6,4},{1,7},{3,1},{5,3},{7,5},{8,14},{10,8},{12,... | collective-permute-start | bytes 516104 | tf_op jit(solution)/shard_map/ppermute | solution.py:29
  113.4 1.3 add_convert_fusion
  114.8 5.0 %collective-permute-start.26 = (bf16[2,32,896]{2,1,0:T(8,128)(2,1)S(1)}, bf16[2,32,896]{2,1,0:T(8,128)(2,1)S(1)}, u32[]{:S(2)}, u32[]{:S(2)}) collective-permute-start(bf16[2,32,896]{2,1,0:T(8,128)(2,1)S(1)} %get-tuple-element.70), channel_id=1, source_target_pairs={{0,96},{16,112},{32,0},{48,16},{64,32},{80,48},{96,64},{112,80},{1... | collective-permute-start | bytes 344072 | tf_op jit(solution)/shard_map/ppermute | solution.py:29
  119.8 2.5 %collective-permute-start.28 = (bf16[32,896]{1,0:T(8,128)(2,1)S(1)}, bf16[32,896]{1,0:T(8,128)(2,1)S(1)}, u32[]{:S(2)}, u32[]{:S(2)}) collective-permute-start(bf16[32,896]{1,0:T(8,128)(2,1)S(1)} %slice_bitcast_fusion), channel_id=1, source_target_pairs={{0,64},{16,80},{32,96},{48,112},{64,0},{80,16},{96,32},{112,48},{1... | collective-permute-start | bytes 172040 | tf_op jit(solution)/shard_map/ppermute | solution.py:29
  122.4 1.1 add_convert_fusion.1
  123.5 5.6 %collective-permute-done.26 = bf16[2,32,896]{2,1,0:T(8,128)(2,1)S(1)} collective-permute-done((bf16[2,32,896]{2,1,0:T(8,128)(2,1)S(1)}, bf16[2,32,896]{2,1,0:T(8,128)(2,1)S(1)}, u32[]{:S(2)}, u32[]{:S(2)}) %collective-permute-start.26) | collective-permute-done | bytes 114720 | tf_op jit(solution)/shard_map/ppermute | solution.py:29
  129.0 1.5 collective-permute-done.27
  130.6 2.0 %collective-permute-start.30 = (bf16[32,896]{1,0:T(8,128)(2,1)S(1)}, bf16[32,896]{1,0:T(8,128)(2,1)S(1)}, u32[]{:S(2)}, u32[]{:S(2)}) collective-permute-start(bf16[32,896]{1,0:T(8,128)(2,1)S(1)} %get-tuple-element.76), channel_id=1, source_target_pairs={{0,16},{16,32},{32,48},{48,64},{64,80},{80,96},{96,112},{112,0},{1... | collective-permute-start | bytes 172040 | tf_op jit(solution)/shard_map/ppermute | solution.py:29
  132.7 1.0 collective-permute-done.28
  133.7 1.2 collective-permute-done.29
  134.9 1.9 %collective-permute-done.30 = bf16[32,896]{1,0:T(8,128)(2,1)S(1)} collective-permute-done((bf16[32,896]{1,0:T(8,128)(2,1)S(1)}, bf16[32,896]{1,0:T(8,128)(2,1)S(1)}, u32[]{:S(2)}, u32[]{:S(2)}) %collective-permute-start.30) | collective-permute-done | bytes 57376 | tf_op jit(solution)/shard_map/ppermute | solution.py:29
  136.9 15.7 %collective-permute-done.20.taken = bf16[10752,128]{1,0:T(8,128)(2,1)S(1)} collective-permute-done((bf16[10752,128]{1,0:T(8,128)(2,1)}, bf16[10752,128]{1,0:T(8,128)(2,1)S(1)}, u32[]{:S(2)}, u32[]{:S(2)}) %collective-permute-start.20) | collective-permute-done | bytes 2752544 | tf_op jit(solution)/shard_map/ppermute | solution.py:328
  152.6 1.5 copy-done.8
  154.1 5.2 %swapped.1 = (bf16[2,3584,128]{2,1,0:T(8,128)(2,1)}, bf16[2,3584,128]{2,1,0:T(8,128)(2,1)}, bf16[2,128,3584]{2,1,0:T(8,128)(2,1)}) custom-call(s32[5]{0:T(128)} %copy-done.3, s32[32]{0:T(128)} %slots.3, bf16[2,3584,128]{2,1,0:T(8,128)(2,1)} %gate.3, bf16[2,3584,128]{2,1,0:T(8,128)(2,1)} %up.3, bf16[2,128,3584]{2,1,0:T(8,128)(2,1)} %down.3, ...), custom_call_target="tpu_custom_call" | custom-call | bytes 11534336 | tf_op jit(solution)/shard_map/swapped/pallas_call | solution.py:195
  159.4 0.9 slice_bitcast_fusion.3
  160.3 3.8 %collective-permute-start.31 = (bf16[32,896]{1,0:T(8,128)(2,1)S(1)}, bf16[32,896]{1,0:T(8,128)(2,1)S(1)}, u32[]{:S(2)}, u32[]{:S(2)}) collective-permute-start(bf16[32,896]{1,0:T(8,128)(2,1)S(1)} %get-tuple-element.72), channel_id=1, source_target_pairs={{0,6},{2,0},{4,2},{6,4},{1,7},{3,1},{5,3},{7,5},{8,14},{10,8},{12,... | collective-permute-start | bytes 172040 | tf_op jit(solution)/shard_map/ppermute | solution.py:29
  165.0 0.9 collective-permute-done.31
  165.9 3.9 %collective-permute-done.32 = bf16[32,896]{1,0:T(8,128)(2,1)S(1)} collective-permute-done((bf16[32,896]{1,0:T(8,128)(2,1)S(1)}, bf16[32,896]{1,0:T(8,128)(2,1)S(1)}, u32[]{:S(2)}, u32[]{:S(2)}) %collective-permute-start.32) | collective-permute-done | bytes 57376 | tf_op jit(solution)/shard_map/ppermute | solution.py:29
  170.3 0.9 fusion.2
  171.8 2.0 %collective-permute-start.36 = (bf16[2,16,448]{2,1,0:T(8,128)(2,1)S(1)}, bf16[2,16,448]{2,1,0:T(8,128)(2,1)S(1)}, u32[]{:S(2)}, u32[]{:S(2)}) collective-permute-start(bf16[2,16,448]{2,1,0:T(8,128)(2,1)S(1)} %get-tuple-element.78), channel_id=1, source_target_pairs={{0,1},{1,128},{128,129},{129,0},{2,3},{3,130},{130,131},{131,2},{4... | collective-permute-start | bytes 86024 | tf_op jit(solution)/shard_map/ppermute | solution.py:29
  175.1 1.8 collective-permute-done.35
  176.8 2.1 %collective-permute-done.34 = bf16[2,16,448]{2,1,0:T(8,128)(2,1)S(1)} collective-permute-done((bf16[2,16,448]{2,1,0:T(8,128)(2,1)S(1)}, bf16[2,16,448]{2,1,0:T(8,128)(2,1)S(1)}, u32[]{:S(2)}, u32[]{:S(2)}) %collective-permute-start.34) | collective-permute-done | bytes 28704 | tf_op jit(solution)/shard_map/ppermute | solution.py:29
  (85 shorter events, 13.7 us)
Async XLA Ops:
  7.2 69.7 %all-gather.3.cloned.1.call-start = ((), (), s32[]{:S(2)}) async-start(), calls=%async_computation.2 | async-start | bytes 2359296 | tf_op jit(solution)/shard_map/all_gather | solution.py:326
  7.2 11.6 %collective-permute-start.3 = (bf16[2,8,448,128]{3,2,1,0:T(8,128)(2,1)}, bf16[2,8,448,128]{3,2,1,0:T(8,128)(2,1)}, u32[]{:S(2)}, u32[]{:S(2)}) collective-permute-start(bf16[2,8,448,128]{3,2,1,0:T(8,128)(2,1)} %bitcast.74), channel_id=1, source_target_pairs={{0,8},{8,0},{1,9},{9,1},{2,10},{10,2},{3,11},{11,3},{4,12},{12,4},... | collective-permute-start | bytes 5505032 | tf_op jit(solution)/shard_map/ppermute | solution.py:318
  7.3 17.8 %collective-permute-start.7 = (bf16[2,8,448,128]{3,2,1,0:T(8,128)(2,1)}, bf16[2,8,448,128]{3,2,1,0:T(8,128)(2,1)S(1)}, u32[]{:S(2)}, u32[]{:S(2)}) collective-permute-start(bf16[2,8,448,128]{3,2,1,0:T(8,128)(2,1)} %bitcast.76), channel_id=1, source_target_pairs={{0,8},{8,0},{1,9},{9,1},{2,10},{10,2},{3,11},{11,3},{4,12},{12,4},... | collective-permute-start | bytes 5505032 | tf_op jit(solution)/shard_map/ppermute | solution.py:318
  7.9 31.5 %copy-start.3 = (s32[5]{0:T(128)}, s32[5]{0:T(128)S(1)}, u32[]{:S(2)}) copy-start(s32[5]{0:T(128)S(1)} %stack.57.place) | copy-start | bytes 64
  10.8 4.3 %collective-permute-start = (bf16[2,16,512]{2,1,0:T(8,128)(2,1)S(1)}, bf16[2,16,512]{2,1,0:T(8,128)(2,1)S(1)}, u32[]{:S(2)}, u32[]{:S(2)}) collective-permute-start(bf16[2,16,512]{2,1,0:T(8,128)(2,1)S(1)} %ride.1.refs_0_), channel_id=1, source_target_pairs={{0,1},{1,128},{128,129},{129,0},{2,3},{3,130},{130,131},{131,2},{4... | collective-permute-start | bytes 98312 | tf_op jit(solution)/shard_map/ppermute | solution.py:29
  12.8 5.4 %collective-permute-start.1 = (bf16[2,16,512]{2,1,0:T(8,128)(2,1)S(1)}, bf16[2,16,512]{2,1,0:T(8,128)(2,1)S(1)}, u32[]{:S(2)}, u32[]{:S(2)}) collective-permute-start(bf16[2,16,512]{2,1,0:T(8,128)(2,1)S(1)} %ride.1.refs_0_), channel_id=1, source_target_pairs={{0,128},{1,129},{128,0},{129,1},{2,130},{3,131},{130,2},{131,3},{4... | collective-permute-start | bytes 98312 | tf_op jit(solution)/shard_map/ppermute | solution.py:29
  13.7 5.1 %collective-permute-start.2 = (bf16[2,16,512]{2,1,0:T(8,128)(2,1)S(1)}, bf16[2,16,512]{2,1,0:T(8,128)(2,1)S(1)}, u32[]{:S(2)}, u32[]{:S(2)}) collective-permute-start(bf16[2,16,512]{2,1,0:T(8,128)(2,1)S(1)} %ride.1.refs_0_), channel_id=1, source_target_pairs={{0,129},{1,0},{128,1},{129,128},{2,131},{3,2},{130,3},{131,130},{4... | collective-permute-start | bytes 98312 | tf_op jit(solution)/shard_map/ppermute | solution.py:29
  19.4 20.0 %copy-start = (bf16[32,1024]{1,0:T(8,128)(2,1)}, bf16[32,1024]{1,0:T(8,128)(2,1)S(1)}, u32[]{:S(2)}) copy-start(bf16[32,1024]{1,0:T(8,128)(2,1)S(1)} %get-tuple-element.44.earlier_ref) | copy-start | bytes 196612
  19.4 5.7 %collective-permute-start.4 = (bf16[32,1024]{1,0:T(8,128)(2,1)S(1)}, bf16[32,1024]{1,0:T(8,128)(2,1)S(1)}, u32[]{:S(2)}, u32[]{:S(2)}) collective-permute-start(bf16[32,1024]{1,0:T(8,128)(2,1)S(1)} %get-tuple-element.40), channel_id=1, source_target_pairs={{0,2},{2,4},{4,6},{6,0},{1,3},{3,5},{5,7},{7,1},{8,10},{10,12},{12... | collective-permute-start | bytes 196616 | tf_op jit(solution)/shard_map/ppermute | solution.py:29
  21.0 5.8 %collective-permute-start.5 = (bf16[32,1024]{1,0:T(8,128)(2,1)S(1)}, bf16[32,1024]{1,0:T(8,128)(2,1)S(1)}, u32[]{:S(2)}, u32[]{:S(2)}) collective-permute-start(bf16[32,1024]{1,0:T(8,128)(2,1)S(1)} %get-tuple-element.40), channel_id=1, source_target_pairs={{0,4},{2,6},{4,0},{6,2},{1,5},{3,7},{5,1},{7,3},{8,12},{10,14},{12... | collective-permute-start | bytes 196616 | tf_op jit(solution)/shard_map/ppermute | solution.py:29
  23.7 4.3 %collective-permute-start.6 = (bf16[32,1024]{1,0:T(8,128)(2,1)S(1)}, bf16[32,1024]{1,0:T(8,128)(2,1)S(1)}, u32[]{:S(2)}, u32[]{:S(2)}) collective-permute-start(bf16[32,1024]{1,0:T(8,128)(2,1)S(1)} %get-tuple-element.40), channel_id=1, source_target_pairs={{0,6},{2,0},{4,2},{6,4},{1,7},{3,1},{5,3},{7,5},{8,14},{10,8},{12,... | collective-permute-start | bytes 196616 | tf_op jit(solution)/shard_map/ppermute | solution.py:29
  25.1 18.4 %copy-start.10 = (bf16[2,8,448,128]{3,2,1,0:T(8,128)(2,1)}, bf16[2,8,448,128]{3,2,1,0:T(8,128)(2,1)S(1)}, u32[]{:S(2)}) copy-start(bf16[2,8,448,128]{3,2,1,0:T(8,128)(2,1)S(1)} %collective-permute-done.7.refs_13_) | copy-start | bytes 5505028
  28.7 130.6 %reduce-scatter.2.cloned.1.call-start = ((), (), s32[]{:S(2)}) async-start(), calls=%async_computation.1 | async-start | bytes 2064384 | tf_op jit(solution)/shard_map/reduce_scatter | solution.py:333
  28.8 14.8 %collective-permute-start.11 = (bf16[2,128,3584]{2,1,0:T(8,128)(2,1)}, bf16[2,128,3584]{2,1,0:T(8,128)(2,1)}, u32[]{:S(2)}, u32[]{:S(2)}) collective-permute-start(bf16[2,128,3584]{2,1,0:T(8,128)(2,1)} %down.3), channel_id=1, source_target_pairs={{0,8},{8,0},{1,9},{9,1},{2,10},{10,2},{3,11},{11,3},{4,12},{12,4},... | collective-permute-start | bytes 5505032 | tf_op jit(solution)/shard_map/ppermute | solution.py:318
  28.9 48.0 %copy-start.7 = (s32[64]{0:T(128)S(1)}, s32[64]{0:T(128)}, u32[]{:S(2)}) copy-start(s32[64]{0:T(128)} %param.11) | copy-start | bytes 772
  28.9 14.6 %collective-permute-start.10 = (bf16[32,1024]{1,0:T(8,128)(2,1)S(1)}, bf16[32,1024]{1,0:T(8,128)(2,1)S(1)}, u32[]{:S(2)}, u32[]{:S(2)}) collective-permute-start(bf16[32,1024]{1,0:T(8,128)(2,1)S(1)} %get-tuple-element.44.earlier_ref), channel_id=1, source_target_pairs={{0,64},{16,80},{32,96},{48,112},{64,0},{80,16},{96,32},{112,48},{1... | collective-permute-start | bytes 196616 | tf_op jit(solution)/shard_map/ppermute | solution.py:29
  36.2 7.4 %collective-permute-start.8 = (bf16[32,1024]{1,0:T(8,128)(2,1)S(1)}, bf16[32,1024]{1,0:T(8,128)(2,1)S(1)}, u32[]{:S(2)}, u32[]{:S(2)}) collective-permute-start(bf16[32,1024]{1,0:T(8,128)(2,1)S(1)} %get-tuple-element.44.earlier_ref), channel_id=1, source_target_pairs={{0,16},{16,32},{32,48},{48,64},{64,80},{80,96},{96,112},{112,0},{1... | collective-permute-start | bytes 196616 | tf_op jit(solution)/shard_map/ppermute | solution.py:29
  37.2 6.4 %collective-permute-start.9 = (bf16[32,1024]{1,0:T(8,128)(2,1)S(1)}, bf16[32,1024]{1,0:T(8,128)(2,1)S(1)}, u32[]{:S(2)}, u32[]{:S(2)}) collective-permute-start(bf16[32,1024]{1,0:T(8,128)(2,1)S(1)} %get-tuple-element.44.earlier_ref), channel_id=1, source_target_pairs={{0,112},{16,0},{32,16},{48,32},{64,48},{80,64},{96,80},{112,96},{1... | collective-permute-start | bytes 196616 | tf_op jit(solution)/shard_map/ppermute | solution.py:29
  43.6 0.8 copy-start.1
  44.4 17.8 %collective-permute-start.14 = (bf16[4,32,1024]{2,1,0:T(8,128)(2,1)S(1)}, bf16[4,32,1024]{2,1,0:T(8,128)(2,1)S(1)}, u32[]{:S(2)}, u32[]{:S(2)}) collective-permute-start(bf16[4,32,1024]{2,1,0:T(8,128)(2,1)S(1)} %join.2.refs_1_), channel_id=1, source_target_pairs={{0,2},{2,4},{4,6},{6,0},{1,3},{3,5},{5,7},{7,1},{8,10},{10,12},{12... | collective-permute-start | bytes 786440 | tf_op jit(solution)/shard_map/ppermute | solution.py:29
  45.1 17.1 %collective-permute-start.15 = (bf16[4,32,1024]{2,1,0:T(8,128)(2,1)S(1)}, bf16[4,32,1024]{2,1,0:T(8,128)(2,1)S(1)}, u32[]{:S(2)}, u32[]{:S(2)}) collective-permute-start(bf16[4,32,1024]{2,1,0:T(8,128)(2,1)S(1)} %join.2.refs_1_), channel_id=1, source_target_pairs={{0,4},{2,6},{4,0},{6,2},{1,5},{3,7},{5,1},{7,3},{8,12},{10,14},{12... | collective-permute-start | bytes 786440 | tf_op jit(solution)/shard_map/ppermute | solution.py:29
  48.6 13.6 %collective-permute-start.16 = (bf16[4,32,1024]{2,1,0:T(8,128)(2,1)S(1)}, bf16[4,32,1024]{2,1,0:T(8,128)(2,1)S(1)}, u32[]{:S(2)}, u32[]{:S(2)}) collective-permute-start(bf16[4,32,1024]{2,1,0:T(8,128)(2,1)S(1)} %join.2.refs_1_), channel_id=1, source_target_pairs={{0,6},{2,0},{4,2},{6,4},{1,7},{3,1},{5,3},{7,5},{8,14},{10,8},{12,... | collective-permute-start | bytes 786440 | tf_op jit(solution)/shard_map/ppermute | solution.py:29
  49.6 12.6 %collective-permute-start.12 = (bf16[2,32,1024]{2,1,0:T(8,128)(2,1)S(1)}, bf16[2,32,1024]{2,1,0:T(8,128)(2,1)S(1)}, u32[]{:S(2)}, u32[]{:S(2)}) collective-permute-start(bf16[2,32,1024]{2,1,0:T(8,128)(2,1)S(1)} %get-tuple-element.80), channel_id=1, source_target_pairs={{0,32},{16,48},{32,64},{48,80},{64,96},{80,112},{96,0},{112,16},{1... | collective-permute-start | bytes 393224 | tf_op jit(solution)/shard_map/ppermute | solution.py:29
  49.9 12.3 %collective-permute-start.13 = (bf16[2,32,1024]{2,1,0:T(8,128)(2,1)S(1)}, bf16[2,32,1024]{2,1,0:T(8,128)(2,1)S(1)}, u32[]{:S(2)}, u32[]{:S(2)}) collective-permute-start(bf16[2,32,1024]{2,1,0:T(8,128)(2,1)S(1)} %get-tuple-element.79), channel_id=1, source_target_pairs={{0,96},{16,112},{32,0},{48,16},{64,32},{80,48},{96,64},{112,80},{1... | collective-permute-start | bytes 393224 | tf_op jit(solution)/shard_map/ppermute | solution.py:29
  62.2 14.6 %copy-start.11 = (bf16[4,32,1024]{2,1,0:T(8,128)(2,1)}, bf16[4,32,1024]{2,1,0:T(8,128)(2,1)S(1)}, u32[]{:S(2)}) copy-start(bf16[4,32,1024]{2,1,0:T(8,128)(2,1)S(1)} %collective-permute-done.16.refs_7_) | copy-start | bytes 786436
  62.2 9.0 %collective-permute-start.17 = (bf16[4,32,1024]{2,1,0:T(8,128)(2,1)S(1)}, bf16[4,32,1024]{2,1,0:T(8,128)(2,1)S(1)}, u32[]{:S(2)}, u32[]{:S(2)}) collective-permute-start(bf16[4,32,1024]{2,1,0:T(8,128)(2,1)S(1)} %join.3.refs_2_), channel_id=1, source_target_pairs={{0,2},{2,4},{4,6},{6,0},{1,3},{3,5},{5,7},{7,1},{8,10},{10,12},{12... | collective-permute-start | bytes 786440 | tf_op jit(solution)/shard_map/ppermute | solution.py:29
  64.2 11.6 %collective-permute-start.18 = (bf16[4,32,1024]{2,1,0:T(8,128)(2,1)S(1)}, bf16[4,32,1024]{2,1,0:T(8,128)(2,1)S(1)}, u32[]{:S(2)}, u32[]{:S(2)}) collective-permute-start(bf16[4,32,1024]{2,1,0:T(8,128)(2,1)S(1)} %join.3.refs_2_), channel_id=1, source_target_pairs={{0,4},{2,6},{4,0},{6,2},{1,5},{3,7},{5,1},{7,3},{8,12},{10,14},{12... | collective-permute-start | bytes 786440 | tf_op jit(solution)/shard_map/ppermute | solution.py:29
  64.5 11.7 %collective-permute-start.19 = (bf16[4,32,1024]{2,1,0:T(8,128)(2,1)S(1)}, bf16[4,32,1024]{2,1,0:T(8,128)(2,1)S(1)}, u32[]{:S(2)}, u32[]{:S(2)}) collective-permute-start(bf16[4,32,1024]{2,1,0:T(8,128)(2,1)S(1)} %join.3.refs_2_), channel_id=1, source_target_pairs={{0,6},{2,0},{4,2},{6,4},{1,7},{3,1},{5,3},{7,5},{8,14},{10,8},{12,... | collective-permute-start | bytes 786440 | tf_op jit(solution)/shard_map/ppermute | solution.py:29
  91.0 41.6 %copy-start.9 = (s32[32]{0:T(128)S(1)}, s32[32]{0:T(128)}, u32[]{:S(2)}) copy-start(s32[32]{0:T(128)} %slots.3) | copy-start | bytes 388
  91.0 61.6 %collective-permute-start.20 = (bf16[10752,128]{1,0:T(8,128)(2,1)}, bf16[10752,128]{1,0:T(8,128)(2,1)S(1)}, u32[]{:S(2)}, u32[]{:S(2)}) collective-permute-start(bf16[10752,128]{1,0:T(8,128)(2,1)} %handed.1), channel_id=1, source_target_pairs={{0,128},{128,0},{1,129},{129,1},{2,130},{130,2},{3,131},{131,3},{4... | collective-permute-start | bytes 8257544 | tf_op jit(solution)/shard_map/ppermute | solution.py:328
  92.5 20.9 %collective-permute-start.24 = (bf16[8,32,896]{2,1,0:T(8,128)(2,1)}, bf16[8,32,896]{2,1,0:T(8,128)(2,1)}, u32[]{:S(2)}, u32[]{:S(2)}) collective-permute-start(bf16[8,32,896]{2,1,0:T(8,128)(2,1)} %get-tuple-element.56), channel_id=1, source_target_pairs={{0,4},{2,6},{4,0},{6,2},{1,5},{3,7},{5,1},{7,3},{8,12},{10,14},{12... | collective-permute-start | bytes 1376264 | tf_op jit(solution)/shard_map/ppermute | solution.py:29
  94.8 16.0 %collective-permute-start.21 = (bf16[5,32,896]{2,1,0:T(8,128)(2,1)}, bf16[5,32,896]{2,1,0:T(8,128)(2,1)S(1)}, u32[]{:S(2)}, u32[]{:S(2)}) collective-permute-start(bf16[5,32,896]{2,1,0:T(8,128)(2,1)} %get-tuple-element.53), channel_id=1, source_target_pairs={{0,6},{2,0},{4,2},{6,4},{1,7},{3,1},{5,3},{7,5},{8,14},{10,8},{12,... | collective-permute-start | bytes 860168 | tf_op jit(solution)/shard_map/ppermute | solution.py:29
  96.7 14.0 %collective-permute-start.22 = (bf16[5,32,896]{2,1,0:T(8,128)(2,1)}, bf16[5,32,896]{2,1,0:T(8,128)(2,1)}, u32[]{:S(2)}, u32[]{:S(2)}) collective-permute-start(bf16[5,32,896]{2,1,0:T(8,128)(2,1)} %get-tuple-element.54), channel_id=1, source_target_pairs={{0,2},{2,4},{4,6},{6,0},{1,3},{3,5},{5,7},{7,1},{8,10},{10,12},{12... | collective-permute-start | bytes 860168 | tf_op jit(solution)/shard_map/ppermute | solution.py:29
  110.8 9.0 %collective-permute-start.23 = (bf16[3,32,896]{2,1,0:T(8,128)(2,1)S(1)}, bf16[3,32,896]{2,1,0:T(8,128)(2,1)S(1)}, u32[]{:S(2)}, u32[]{:S(2)}) collective-permute-start(bf16[3,32,896]{2,1,0:T(8,128)(2,1)S(1)} %get-tuple-element.55), channel_id=1, source_target_pairs={{0,6},{2,0},{4,2},{6,4},{1,7},{3,1},{5,3},{7,5},{8,14},{10,8},{12,... | collective-permute-start | bytes 516104 | tf_op jit(solution)/shard_map/ppermute | solution.py:29
  113.4 8.9 %collective-permute-start.25 = (bf16[3,32,896]{2,1,0:T(8,128)(2,1)S(1)}, bf16[3,32,896]{2,1,0:T(8,128)(2,1)S(1)}, u32[]{:S(2)}, u32[]{:S(2)}) collective-permute-start(bf16[3,32,896]{2,1,0:T(8,128)(2,1)S(1)} %get-tuple-element.58), channel_id=1, source_target_pairs={{0,2},{2,4},{4,6},{6,0},{1,3},{3,5},{5,7},{7,1},{8,10},{10,12},{12... | collective-permute-start | bytes 516104 | tf_op jit(solution)/shard_map/ppermute | solution.py:29
  114.8 14.3 %collective-permute-start.26 = (bf16[2,32,896]{2,1,0:T(8,128)(2,1)S(1)}, bf16[2,32,896]{2,1,0:T(8,128)(2,1)S(1)}, u32[]{:S(2)}, u32[]{:S(2)}) collective-permute-start(bf16[2,32,896]{2,1,0:T(8,128)(2,1)S(1)} %get-tuple-element.70), channel_id=1, source_target_pairs={{0,96},{16,112},{32,0},{48,16},{64,32},{80,48},{96,64},{112,80},{1... | collective-permute-start | bytes 344072 | tf_op jit(solution)/shard_map/ppermute | solution.py:29
  119.8 10.7 %collective-permute-start.27 = (bf16[2,32,896]{2,1,0:T(8,128)(2,1)S(1)}, bf16[2,32,896]{2,1,0:T(8,128)(2,1)S(1)}, u32[]{:S(2)}, u32[]{:S(2)}) collective-permute-start(bf16[2,32,896]{2,1,0:T(8,128)(2,1)S(1)} %get-tuple-element.71), channel_id=1, source_target_pairs={{0,32},{16,48},{32,64},{48,80},{64,96},{80,112},{96,0},{112,16},{1... | collective-permute-start | bytes 344072 | tf_op jit(solution)/shard_map/ppermute | solution.py:29
  119.8 13.9 %collective-permute-start.28 = (bf16[32,896]{1,0:T(8,128)(2,1)S(1)}, bf16[32,896]{1,0:T(8,128)(2,1)S(1)}, u32[]{:S(2)}, u32[]{:S(2)}) collective-permute-start(bf16[32,896]{1,0:T(8,128)(2,1)S(1)} %slice_bitcast_fusion), channel_id=1, source_target_pairs={{0,64},{16,80},{32,96},{48,112},{64,0},{80,16},{96,32},{112,48},{1... | collective-permute-start | bytes 172040 | tf_op jit(solution)/shard_map/ppermute | solution.py:29
  130.5 4.4 %collective-permute-start.29 = (bf16[32,896]{1,0:T(8,128)(2,1)S(1)}, bf16[32,896]{1,0:T(8,128)(2,1)S(1)}, u32[]{:S(2)}, u32[]{:S(2)}) collective-permute-start(bf16[32,896]{1,0:T(8,128)(2,1)S(1)} %get-tuple-element.75), channel_id=1, source_target_pairs={{0,112},{16,0},{32,16},{48,32},{64,48},{80,64},{96,80},{112,96},{1... | collective-permute-start | bytes 172040 | tf_op jit(solution)/shard_map/ppermute | solution.py:29
  130.6 6.3 %collective-permute-start.30 = (bf16[32,896]{1,0:T(8,128)(2,1)S(1)}, bf16[32,896]{1,0:T(8,128)(2,1)S(1)}, u32[]{:S(2)}, u32[]{:S(2)}) collective-permute-start(bf16[32,896]{1,0:T(8,128)(2,1)S(1)} %get-tuple-element.76), channel_id=1, source_target_pairs={{0,16},{16,32},{32,48},{48,64},{64,80},{80,96},{96,112},{112,0},{1... | collective-permute-start | bytes 172040 | tf_op jit(solution)/shard_map/ppermute | solution.py:29
  152.6 1.5 copy-start.8
  160.3 5.6 %collective-permute-start.31 = (bf16[32,896]{1,0:T(8,128)(2,1)S(1)}, bf16[32,896]{1,0:T(8,128)(2,1)S(1)}, u32[]{:S(2)}, u32[]{:S(2)}) collective-permute-start(bf16[32,896]{1,0:T(8,128)(2,1)S(1)} %get-tuple-element.72), channel_id=1, source_target_pairs={{0,6},{2,0},{4,2},{6,4},{1,7},{3,1},{5,3},{7,5},{8,14},{10,8},{12,... | collective-permute-start | bytes 172040 | tf_op jit(solution)/shard_map/ppermute | solution.py:29
  164.0 5.7 %collective-permute-start.32 = (bf16[32,896]{1,0:T(8,128)(2,1)S(1)}, bf16[32,896]{1,0:T(8,128)(2,1)S(1)}, u32[]{:S(2)}, u32[]{:S(2)}) collective-permute-start(bf16[32,896]{1,0:T(8,128)(2,1)S(1)} %get-tuple-element.74), channel_id=1, source_target_pairs={{0,4},{2,6},{4,0},{6,2},{1,5},{3,7},{5,1},{7,3},{8,12},{10,14},{12... | collective-permute-start | bytes 172040 | tf_op jit(solution)/shard_map/ppermute | solution.py:29
  164.3 6.0 %collective-permute-start.33 = (bf16[32,896]{1,0:T(8,128)(2,1)S(1)}, bf16[32,896]{1,0:T(8,128)(2,1)S(1)}, u32[]{:S(2)}, u32[]{:S(2)}) collective-permute-start(bf16[32,896]{1,0:T(8,128)(2,1)S(1)} %get-tuple-element.73), channel_id=1, source_target_pairs={{0,2},{2,4},{4,6},{6,0},{1,3},{3,5},{5,7},{7,1},{8,10},{10,12},{12... | collective-permute-start | bytes 172040 | tf_op jit(solution)/shard_map/ppermute | solution.py:29
  165.0 8.8 %collective-permute-start.37 = (f32[64]{0:T(128)S(1)}, f32[64]{0:T(128)S(1)}, u32[]{:S(2)}, u32[]{:S(2)}) collective-permute-start(f32[64]{0:T(128)S(1)} %slice_bitcast_fusion.4), channel_id=1, source_target_pairs={{0,8},{8,0},{1,9},{9,1},{2,10},{10,2},{3,11},{11,3},{4,12},{12,4},... | collective-permute-start | bytes 776 | tf_op jit(solution)/shard_map/ppermute | solution.py:340
  171.3 5.5 %collective-permute-start.35 = (bf16[2,16,448]{2,1,0:T(8,128)(2,1)S(1)}, bf16[2,16,448]{2,1,0:T(8,128)(2,1)S(1)}, u32[]{:S(2)}, u32[]{:S(2)}) collective-permute-start(bf16[2,16,448]{2,1,0:T(8,128)(2,1)S(1)} %get-tuple-element.77), channel_id=1, source_target_pairs={{0,128},{1,129},{128,0},{129,1},{2,130},{3,131},{130,2},{131,3},{4... | collective-permute-start | bytes 86024 | tf_op jit(solution)/shard_map/ppermute | solution.py:29
  171.8 5.1 %collective-permute-start.36 = (bf16[2,16,448]{2,1,0:T(8,128)(2,1)S(1)}, bf16[2,16,448]{2,1,0:T(8,128)(2,1)S(1)}, u32[]{:S(2)}, u32[]{:S(2)}) collective-permute-start(bf16[2,16,448]{2,1,0:T(8,128)(2,1)S(1)} %get-tuple-element.78), channel_id=1, source_target_pairs={{0,1},{1,128},{128,129},{129,0},{2,3},{3,130},{130,131},{131,2},{4... | collective-permute-start | bytes 86024 | tf_op jit(solution)/shard_map/ppermute | solution.py:29
  173.8 5.1 %collective-permute-start.34 = (bf16[2,16,448]{2,1,0:T(8,128)(2,1)S(1)}, bf16[2,16,448]{2,1,0:T(8,128)(2,1)S(1)}, u32[]{:S(2)}, u32[]{:S(2)}) collective-permute-start(bf16[2,16,448]{2,1,0:T(8,128)(2,1)S(1)} %get-tuple-element.65), channel_id=1, source_target_pairs={{0,129},{1,0},{128,1},{129,128},{2,131},{3,2},{130,3},{131,130},{4... | collective-permute-start | bytes 86024 | tf_op jit(solution)/shard_map/ppermute | solution.py:29
  (5 other events, 3.5 us)
Sparse Core Ops, SparseCore 0:
  28.9 47.9 all-gather.2
  91.1 45.2 reduce-scatter.1
